TPU v7x, 32 devices: a whole 2x2x4 slice. The times are simulated.
32 devices in a mesh: orbit: 2 (over x), lon: 16 (over z, y, core).
Axes of the slice: x: 2, y: 2, z: 4, core: 2. Of those that a mesh axis runs over, the one named last changes fastest.
Arguments:
- interp: bfloat16 [64, 16, 256, 128], P('orbit', 'lon'), may hold values from -0.5 to 0.5
- obs_value: float32 [64, 16, 256], P('orbit', 'lon'), may hold values from -20 to 20
- obs_weight: float32 [64, 16, 256], P('orbit', 'lon'), may hold values from 0.5 to 4
- block_map: int32 [64, 16], P('orbit', 'lon'), may hold values from 0 to 511
- live_count: int32 [2, 16], P('orbit', 'lon'), may hold values from 4 to 32, as said below
- kappa2: float32 [1024, 1024], P('lon'), may hold values from 0.01 to 1
Outputs:
- solution: float32 [1024, 1024], P('lon')
- residual: float32 [1024, 1024], P('lon')
Inputs may be any that keep to these rules, and one draw needn't show every extreme that they name: `live_count`: live blocks of the device of orbit group o in band l; its slots at or beyond this count are padding; some device holds exactly 32.
All inputs are finite; a program needn't handle non-finite values.
Results may differ from a plain program's by a relative error of at most 0.014.
Values sent between devices are 32-bit elements; how exact they have to be, the bound alone decides.
No kernel may reach another device: no remote copies, remote signals or barrier semaphores. Data moves between devices by JAX's collectives and lax.ppermute only.
A program may use at most 64 MiB of HBM per device.

v0:
```python
import functools

import jax
import jax.numpy as jnp
from jax import lax
from jax.experimental import pallas as pl
from jax.experimental.pallas import tpu as pltpu
from jax.sharding import PartitionSpec as P

PRIOR_WEIGHT = 0.0625
GROUP = 8
LANES = 128
F32 = jnp.float32
BF16 = jnp.bfloat16
VMEM_BYTES = 48 * 1024 * 1024


def two_terms(value):
    high = value.astype(BF16)
    low = (value - high.astype(F32)).astype(BF16)
    return high, low


def stacked_terms(value):
    return jnp.concatenate(two_terms(value), axis=0)


def fold_terms(product):
    half = product.shape[0] // 2
    return product[:half] + product[half:]


def dot(left, right):
    return lax.dot_general(left, right, (((1,), (0,)), ((), ())), preferred_element_type=F32)


def dot_transposed(left, right):
    return lax.dot_general(left, right, (((1,), (1,)), ((), ())), preferred_element_type=F32)


def pick_row(total, product, slot):
    rows = lax.broadcasted_iota(jnp.int32, product.shape, 0)
    return jnp.where(rows == slot, product, total)


def lat_pair(field):
    pieces = field.shape[1]
    piece = lax.broadcasted_iota(jnp.int32, field.shape, 1)
    lane = lax.broadcasted_iota(jnp.int32, field.shape, 2)
    south = pltpu.roll(field, 1, 2)
    north = pltpu.roll(field, LANES - 1, 2)
    south_over = jnp.where(piece == 0, 0.0, pltpu.roll(south, 1, 1))
    north_over = jnp.where(piece == pieces - 1, 0.0, pltpu.roll(north, pieces - 1, 1))
    return jnp.where(lane == 0, south_over, south) + jnp.where(lane == LANES - 1, north_over, north)


def stencil(field, shifted):
    center = field[1:-1]
    return shifted * center - field[2:] - field[:-2] - lat_pair(center)


def data_kernel(
    orbits, count_ref, map_ref, interp_ref, value_ref, weight_ref, message_ref, matrices_ref, sems
):
    slots = matrices_ref.shape[0]
    groups = slots // GROUP
    copies = []
    for group in range(groups):
        part = pl.ds(group * GROUP, GROUP)
        copies.append(
            pltpu.make_async_copy(interp_ref.at[part], matrices_ref.at[part], sems.at[group])
        )
        copies[-1].start()
    orbit = lax.axis_index("orbit")
    total = orbits * slots
    place = lax.broadcasted_iota(jnp.int32, (GROUP, LANES), 0) * LANES
    place = place + lax.broadcasted_iota(jnp.int32, (GROUP, LANES), 1)
    slot_here = jnp.where(place >= total, place - total, place) - orbit * slots
    target_row = jnp.zeros((GROUP, LANES), jnp.int32)
    count = count_ref[0]
    for slot in range(slots):
        live_target = jnp.where(slot < count, map_ref[slot] + 1, 0)
        target_row = jnp.where(slot_here == slot, live_target, target_row)
    target_row = jnp.where(place < 2 * total, target_row, 0)
    message_ref[pl.ds(2 * slots, GROUP), :] = target_row.astype(F32)
    for group in range(groups):
        part = pl.ds(group * GROUP, GROUP)
        weights = weight_ref[part, 0, :]
        scaled = (weights * value_ref[part, 0, :]).astype(BF16)
        scaled = jnp.concatenate([scaled, scaled], axis=0)
        weight_terms = stacked_terms(weights)
        first = jnp.zeros((2 * GROUP, LANES), F32)
        second = jnp.zeros((GROUP, LANES), F32)
        copies[group].wait()
        for slot in range(GROUP):
            matrix = matrices_ref[group * GROUP + slot]
            first = pick_row(first, dot(scaled, matrix), slot)
            wide = matrix.astype(F32)
            square_high, square_low = two_terms(wide * wide)
            product = dot(weight_terms, square_high) + dot(weight_terms, square_low)
            second = pick_row(second, fold_terms(product), slot)
        message_ref[part, :] = first[:GROUP]
        message_ref[pl.ds(slots + group * GROUP, GROUP), :] = second


def kappa_kernel(kappa_ref, shifted_ref):
    columns, pieces, _ = shifted_ref.shape
    for piece in range(pieces):
        part = kappa_ref[:, pl.ds(piece * LANES, LANES)]
        shifted_ref[:, piece, :] = part + 4.0


def gather_messages(orbits, slots, message_refs, order_ref):
    orbit = lax.axis_index("orbit")
    for step in range(orbits):
        source = lax.rem(orbit + step, orbits)
        rows = pl.ds(pl.multiple_of(source * slots, slots), slots)
        order_ref[rows, :] = message_refs[step]


def start_kernel(
    orbits, parity, shifted_ref, *refs
):
    message_refs = refs[:orbits]
    field_ref, right_ref, precond_ref, scatter_ref, even_ref, odd_ref, order_ref = refs[orbits:]
    slots = (message_refs[0].shape[0] - GROUP) // 2
    cells = scatter_ref.shape[0]
    targets = message_refs[0][pl.ds(2 * slots, GROUP), :]
    for ref in message_refs[1:]:
        targets = targets + ref[pl.ds(2 * slots, GROUP), :]
    targets = targets.astype(jnp.int32) - 1
    row = lax.broadcasted_iota(jnp.int32, (cells, LANES), 0)
    for piece in range(scatter_ref.shape[1] // LANES):
        hit = row == targets[piece : piece + 1, :]
        scatter_ref[:, pl.ds(piece * LANES, LANES)] = jnp.where(hit, 1.0, 0.0).astype(BF16)
    sums = []
    for part in range(2):
        rows = pl.ds(part * slots, slots)
        gather_messages(orbits, slots, [ref[rows, :] for ref in message_refs], order_ref)
        sums.append(scattered(scatter_ref[...], order_ref[...]))
    right_side, obs_diag = (value.reshape(field_ref.shape) for value in sums)
    shifted = shifted_ref[...]
    precond = PRIOR_WEIGHT * (shifted * shifted + 4.0) + obs_diag
    field = right_side / precond
    right_ref[...] = right_side
    precond_ref[...] = precond
    field_ref[...] = field
    columns = field.shape[0]
    top = jnp.concatenate([field[:2], shifted[:1]], axis=0)
    bottom = jnp.concatenate([field[columns - 2 :], shifted[columns - 1 :]], axis=0)
    store_edges(parity, top, bottom, even_ref, odd_ref)


def scattered(one_hot, slots):
    terms = stacked_terms(slots)
    spare = one_hot.shape[1] - terms.shape[0]
    if spare:
        terms = jnp.concatenate([terms, jnp.zeros((spare, LANES), BF16)], axis=0)
    return dot(one_hot, terms)


def store_edges(parity, top, bottom, even_ref, odd_ref):
    flip = parity()
    even_ref[...] = jnp.where(flip, top, bottom)
    odd_ref[...] = jnp.where(flip, bottom, top)


def load_edges(parity, even_ref, odd_ref):
    flip = parity()
    even, odd = even_ref[...], odd_ref[...]
    return jnp.where(flip, even, odd), jnp.where(flip, odd, even)


def normal_kernel(map_ref, field_ref, weight_ref, matrices_ref, out_ref, picked_ref):
    slots = matrices_ref.shape[0]
    for slot in range(slots):
        picked_ref[pl.ds(slot, 1), :] = field_ref[pl.ds(map_ref[slot], 1), :]
    for group in range(slots // GROUP):
        part = pl.ds(group * GROUP, GROUP)
        cells = stacked_terms(picked_ref[part, :])
        predicted = jnp.zeros((GROUP, matrices_ref.shape[1]), F32)
        for slot in range(GROUP):
            product = dot_transposed(cells, matrices_ref[group * GROUP + slot])
            predicted = pick_row(predicted, fold_terms(product), slot)
        scaled = stacked_terms(weight_ref[part, 0, :] * predicted)
        back = jnp.zeros((GROUP, LANES), F32)
        for slot in range(GROUP):
            product = dot(scaled, matrices_ref[group * GROUP + slot])
            back = pick_row(back, fold_terms(product), slot)
        out_ref[part, :] = back


def extended(field, top, bottom):
    return jnp.concatenate([top, field, bottom], axis=0)


def prior_parts(field, shifted, top, bottom, shifted_top, shifted_bottom):
    first = stencil(
        extended(field, top, bottom), extended(shifted, shifted_top, shifted_bottom)
    )
    return PRIOR_WEIGHT * stencil(first, shifted)


def system(parity, orbits, refs):
    (field_ref, shifted_ref, even_ref, odd_ref, rim_even_ref, rim_odd_ref, scatter_ref) = refs[:7]
    slot_refs = refs[7 : 7 + orbits]
    order_ref = refs[-1]
    slots = slot_refs[0].shape[0]
    gather_messages(orbits, slots, [ref[...] for ref in slot_refs], order_ref)
    normal = scattered(scatter_ref[...], order_ref[...]).reshape(field_ref.shape)
    top, bottom = load_edges(parity, even_ref, odd_ref)
    rim_top, rim_bottom = load_edges(parity, rim_even_ref, rim_odd_ref)
    prior = prior_parts(
        field_ref[...], shifted_ref[...], top[:2], bottom[:2], rim_top[2:], rim_bottom[2:]
    )
    return prior + normal, refs[7 + orbits : -1]


def first_kernel(parity, orbits, *refs):
    image, rest = system(parity, orbits, refs)
    precond_ref, image_ref, next_ref, even_ref, odd_ref = rest
    following = image / precond_ref[...]
    image_ref[...] = image
    next_ref[...] = following
    store_edges(parity, following[:2], following[following.shape[0] - 2 :], even_ref, odd_ref)


def second_kernel(parity, orbits, *refs):
    image, rest = system(parity, orbits, refs)
    start_ref, right_ref, first_ref, image_ref, sums_ref = rest
    field = refs[0][...]
    start, first = start_ref[...], first_ref[...]
    own = jnp.where(lax.axis_index("orbit") == 0, 1.0, 0.0)
    lane = lax.broadcasted_iota(jnp.int32, (1, LANES), 1)
    line = jnp.zeros((1, LANES), F32)
    pairs = ((right_ref[...], start), (start, first), (first, field), (field, image))
    for index, (left, right) in enumerate(pairs):
        by_lane = jnp.sum(jnp.sum(left * right, axis=0), axis=0, keepdims=True)
        value = jnp.sum(by_lane, axis=1, keepdims=True) * own
        line = jnp.where(lane == index, value, line)
    sums_ref[...] = jnp.broadcast_to(line[None], sums_ref.shape)
    image_ref[...] = image


def last_kernel(
    sums_ref, start_ref, next_ref, right_ref, first_ref, second_ref, out_ref, residual_ref
):
    line = jnp.sum(sums_ref[...], axis=0)
    lane = lax.broadcasted_iota(jnp.int32, line.shape, 1)
    product, energy, cross, following = (
        jnp.sum(jnp.where(lane == index, line, 0.0), axis=1, keepdims=True) for index in range(4)
    )
    alpha = product / energy
    later = product - 2.0 * alpha * energy + alpha * alpha * cross
    grown = 1.0 + later / product
    later_energy = (
        grown * grown * energy - 2.0 * alpha * grown * cross + alpha * alpha * following
    )
    later_alpha = later / later_energy
    on_start = alpha + later_alpha * grown
    on_next = -alpha * later_alpha
    columns, pieces, _ = start_ref.shape
    for piece in range(pieces):
        lanes = pl.ds(piece * LANES, LANES)
        out_ref[:, lanes] = on_start * start_ref[:, piece, :] + on_next * next_ref[:, piece, :]
        residual_ref[:, lanes] = (
            right_ref[:, piece, :]
            - on_start * first_ref[:, piece, :]
            - on_next * second_ref[:, piece, :]
        )


def per_device(orbits, bands, interp, obs_value, obs_weight, block_map, live_count, kappa2):
    slots, _, observations, width = interp.shape
    columns, latitudes = kappa2.shape
    pieces = latitudes // width
    cells = columns * pieces
    field_shape = (columns, pieces, width)
    paired = bands % 2 == 0

    def parity():
        return lax.rem(lax.axis_index("lon"), 2) == 1 if paired else False

    vmem = pl.BlockSpec(memory_space=pltpu.VMEM)
    smem = pl.BlockSpec(memory_space=pltpu.SMEM)

    def call(kernel, outs, in_specs, scratch=(), name=None):
        return pl.pallas_call(
            kernel,
            out_shape=tuple(jax.ShapeDtypeStruct(shape, dtype) for shape, dtype in outs),
            in_specs=in_specs,
            out_specs=tuple(vmem for _ in outs),
            scratch_shapes=list(scratch),
            compiler_params=pltpu.CompilerParams(vmem_limit_bytes=VMEM_BYTES),
            name=name,
        )

    def from_others(value):
        return [value] + [
            lax.ppermute(value, "orbit", [((i + step) % orbits, i) for i in range(orbits)])
            for step in range(1, orbits)
        ]

    def from_neighbours(even, odd):
        if paired:
            even_pairs = [(i, i ^ 1) for i in range(bands)]
            odd_pairs = [(i, (i + 1 if i % 2 else i - 1) % bands) for i in range(bands)]
            return lax.ppermute(even, "lon", even_pairs), lax.ppermute(odd, "lon", odd_pairs)
        up = [(i, (i + 1) % bands) for i in range(bands)]
        down = [((i + 1) % bands, i) for i in range(bands)]
        return lax.ppermute(odd, "lon", down), lax.ppermute(even, "lon", up)

    matrices_in = interp.reshape(slots, observations, width)
    targets = block_map.reshape(slots)
    message, matrices = call(
        functools.partial(data_kernel, orbits),
        (((2 * slots + GROUP, width), F32), ((slots, observations, width), BF16)),
        [smem, smem, pl.BlockSpec(memory_space=pl.ANY), vmem, vmem],
        [pltpu.SemaphoreType.DMA((slots // GROUP,))],
        "data_terms",
    )(live_count.reshape(1), targets, matrices_in, obs_value, obs_weight)
    messages = from_others(message)
    (shifted,) = call(kappa_kernel, ((field_shape, F32),), [vmem], (), "kappa_rows")(kappa2)

    order = pltpu.VMEM((orbits * slots, width), F32)
    edge_width = -(-2 * orbits * slots // LANES) * LANES
    rim = ((3, pieces, width), F32)
    edge = ((2, pieces, width), F32)
    field = (field_shape, F32)
    start, right_side, precond, scatter, even, odd = call(
        functools.partial(start_kernel, orbits, parity),
        (field, field, field, ((cells, edge_width), BF16), rim, rim),
        [vmem] * (1 + orbits),
        [order],
        "start",
    )(shifted, *messages)

    def normal_slots(value, name):
        (out,) = call(
            normal_kernel,
            (((slots, width), F32),),
            [smem, vmem, vmem, vmem],
            [pltpu.VMEM((slots, width), F32)],
            name,
        )(targets, value.reshape(cells, width), obs_weight, matrices)
        return from_others(out)

    rim_even, rim_odd = from_neighbours(even, odd)
    terms = normal_slots(start, "normal_start")
    first, following, even, odd = call(
        functools.partial(first_kernel, parity, orbits),
        (field, field, edge, edge),
        [vmem] * (8 + orbits),
        [order],
        "first_image",
    )(start, shifted, rim_even, rim_odd, rim_even, rim_odd, scatter, *terms, precond)

    even, odd = from_neighbours(even, odd)
    terms = normal_slots(following, "normal_next")
    second, sums = call(
        functools.partial(second_kernel, parity, orbits),
        (field, ((orbits * bands, 1, width), F32)),
        [vmem] * (10 + orbits),
        [order],
        "second_image",
    )(following, shifted, even, odd, rim_even, rim_odd, scatter, *terms, start, right_side, first)
    sums = lax.all_to_all(sums, ("orbit", "lon"), 0, 0, tiled=True)
    return call(
        last_kernel,
        ((kappa2.shape, F32), (kappa2.shape, F32)),
        [vmem] * 6,
        (),
        "combine",
    )(sums, start, following, right_side, first, second)


def solution(mesh):
    in_specs = (
        P("orbit", "lon", None, None),
        P("orbit", "lon", None),
        P("orbit", "lon", None),
        P("orbit", "lon"),
        P("orbit", "lon"),
        P("lon", None),
    )
    out_specs = (P("lon", None), P("lon", None))
    body = functools.partial(per_device, mesh.shape["orbit"], mesh.shape["lon"])
    return jax.shard_map(
        body, mesh=mesh, in_specs=in_specs, out_specs=out_specs, check_vma=False
    )
```

profile of v0, /device:TPU:0, one launch (start us, length us, event | category | flops | bytes accessed | tf_op | source)
XLA Modules:
  0.0 46.2 jit_solution(5014505980182962383)
XLA Ops:
  1.3 0.0 copy-start
  1.3 1.6 %copy-done = bf16[32,1,256,128]{3,2,1,0:T(8,128)(2,1)S(1)} copy-done((bf16[32,1,256,128]{3,2,1,0:T(8,128)(2,1)S(1)}, bf16[32,1,256,128]{3,2,1,0:T(8,128)(2,1)}, u32[]{:S(2)}) %copy-start) | copy-done | bytes 2097176
  2.9 0.0 copy-start.1
  2.9 0.8 %copy-done.1 = f32[32,1,256]{2,1,0:T(1,128)S(1)} copy-done((f32[32,1,256]{2,1,0:T(1,128)S(1)}, f32[32,1,256]{2,1,0:T(1,128)}, u32[]{:S(2)}) %copy-start.1) | copy-done | bytes 32792
  3.6 0.0 copy-start.4
  3.6 0.8 %copy-done.4 = f32[32,1,256]{2,1,0:T(1,128)S(1)} copy-done((f32[32,1,256]{2,1,0:T(1,128)S(1)}, f32[32,1,256]{2,1,0:T(1,128)}, u32[]{:S(2)}) %copy-start.4) | copy-done | bytes 32792
  4.4 0.0 copy-start.5
  4.4 0.7 %copy-done.5 = s32[32,1]{0,1:T(1,128)S(1)} copy-done((s32[32,1]{0,1:T(1,128)S(1)}, s32[32,1]{0,1:T(1,128)}, u32[]{:S(2)}) %copy-start.5) | copy-done | bytes 152
  5.0 0.0 copy-start.3
  5.0 2.2 %data_terms.1 = (f32[72,128]{1,0:T(8,128)S(1)}, bf16[32,256,128]{2,1,0:T(8,128)(2,1)S(1)}) custom-call(s32[1]{0:T(128)} %bitcast.5.count_ref, s32[32]{0:T(128)S(1)} %bitcast.9, bf16[32,256,128]{2,1,0:T(8,128)(2,1)S(1)} %bitcast.8, f32[32,1,256]{2,1,0:T(1,128)S(1)} %copy-done.4, f32[32,1,256]{2,1,0:T(1,128)S(1)} %copy-done.1), custom_call_target="tpu_custom_call" | custom-call | tf_op jit(solution)/shard_map/data_terms/pallas_call | solution.py:315
  7.3 0.0 copy-start.2
  7.3 3.0 %collective-permute-start = (f32[72,128]{1,0:T(8,128)S(1)}, f32[72,128]{1,0:T(8,128)S(1)}, u32[]{:S(2)}, u32[]{:S(2)}) collective-permute-start(f32[72,128]{1,0:T(8,128)S(1)} %get-tuple-element.16.refs_0_), channel_id=1, source_target_pairs={{16,0},{0,16},{17,1},{1,17},{18,2},{2,18},{19,3},{3,19},{20,4},{4,... | collective-permute-start | bytes 110600 | tf_op jit(solution)/shard_map/ppermute | solution.py:300
  10.3 0.0 copy-done.3
  10.3 0.2 kappa_rows.1.shifted_ref.refs_1_
  10.5 1.8 %collective-permute-done.refs_1_ = f32[72,128]{1,0:T(8,128)S(1)} collective-permute-done((f32[72,128]{1,0:T(8,128)S(1)}, f32[72,128]{1,0:T(8,128)S(1)}, u32[]{:S(2)}, u32[]{:S(2)}) %collective-permute-start) | collective-permute-done | bytes 36896 | tf_op jit(solution)/shard_map/ppermute | solution.py:300
  12.2 0.3 start.1
  12.5 1.9 %normal_start.1.refs_7_ = f32[32,128]{1,0:T(8,128)S(1)} custom-call(s32[32]{0:T(128)S(1)} %bitcast.10, f32[512,128]{1,0:T(8,128)S(1)} %bitcast.6, f32[32,1,256]{2,1,0:T(1,128)S(1)} %copy-done.1, bf16[32,256,128]{2,1,0:T(8,128)(2,1)S(1)} %get-tuple-element.21.matrices_ref), custom_call_target="tpu_custom_call" | custom-call | tf_op jit(solution)/shard_map/normal_start/pallas_call | solution.py:339
  14.4 2.1 %collective-permute-start.3 = (f32[32,128]{1,0:T(8,128)S(1)}, f32[32,128]{1,0:T(8,128)S(1)}, u32[]{:S(2)}, u32[]{:S(2)}) collective-permute-start(f32[32,128]{1,0:T(8,128)S(1)} %normal_start.1.refs_7_), channel_id=1, source_target_pairs={{16,0},{0,16},{17,1},{1,17},{18,2},{2,18},{19,3},{3,19},{20,4},{4,... | collective-permute-start | bytes 49160 | tf_op jit(solution)/shard_map/ppermute | solution.py:300
  16.5 0.0 collective-permute-start.1
  16.5 4.7 %collective-permute-start.2 = (f32[3,8,128]{2,1,0:T(8,128)S(1)}, f32[3,8,128]{2,1,0:T(8,128)S(1)}, u32[]{:S(2)}, u32[]{:S(2)}) collective-permute-start(f32[3,8,128]{2,1,0:T(8,128)S(1)} %get-tuple-element.19), channel_id=1, source_target_pairs={{0,15},{1,2},{2,1},{3,4},{4,3},{5,6},{6,5},{7,8},{8,7},{9,10},{10,... | collective-permute-start | bytes 36872 | tf_op jit(solution)/shard_map/ppermute | solution.py:308
  21.2 0.0 collective-permute-done.1.refs_2_.refs_4_
  21.2 1.4 %collective-permute-done.2.refs_3_.refs_5_ = f32[3,8,128]{2,1,0:T(8,128)S(1)} collective-permute-done((f32[3,8,128]{2,1,0:T(8,128)S(1)}, f32[3,8,128]{2,1,0:T(8,128)S(1)}, u32[]{:S(2)}, u32[]{:S(2)}) %collective-permute-start.2) | collective-permute-done | bytes 12320 | tf_op jit(solution)/shard_map/ppermute | solution.py:308
  22.6 0.0 collective-permute-done.3.refs_8_
  22.6 0.4 first_image.1
  23.0 0.0 copy-done.2
  23.0 1.9 %normal_next.1.refs_7_ = f32[32,128]{1,0:T(8,128)S(1)} custom-call(s32[32]{0:T(128)S(1)} %bitcast.11, f32[512,128]{1,0:T(8,128)S(1)} %bitcast.7, f32[32,1,256]{2,1,0:T(1,128)S(1)} %copy-done.2, bf16[32,256,128]{2,1,0:T(8,128)(2,1)S(1)} %get-tuple-element.21.matrices_ref), custom_call_target="tpu_custom_call" | custom-call | tf_op jit(solution)/shard_map/normal_next/pallas_call | solution.py:339
  24.9 0.6 %collective-permute-start.6 = (f32[32,128]{1,0:T(8,128)S(1)}, f32[32,128]{1,0:T(8,128)S(1)}, u32[]{:S(2)}, u32[]{:S(2)}) collective-permute-start(f32[32,128]{1,0:T(8,128)S(1)} %normal_next.1.refs_7_), channel_id=1, source_target_pairs={{16,0},{0,16},{17,1},{1,17},{18,2},{2,18},{19,3},{3,19},{20,4},{4,... | collective-permute-start | bytes 49160 | tf_op jit(solution)/shard_map/ppermute | solution.py:300
  25.5 0.0 collective-permute-start.4
  25.5 4.1 %collective-permute-start.5 = (f32[2,8,128]{2,1,0:T(8,128)S(1)}, f32[2,8,128]{2,1,0:T(8,128)S(1)}, u32[]{:S(2)}, u32[]{:S(2)}) collective-permute-start(f32[2,8,128]{2,1,0:T(8,128)S(1)} %get-tuple-element.25), channel_id=1, source_target_pairs={{0,15},{1,2},{2,1},{3,4},{4,3},{5,6},{6,5},{7,8},{8,7},{9,10},{10,... | collective-permute-start | bytes 24584 | tf_op jit(solution)/shard_map/ppermute | solution.py:308
  29.6 0.0 collective-permute-done.4.refs_2_
  29.6 1.6 %collective-permute-done.5.refs_3_ = f32[2,8,128]{2,1,0:T(8,128)S(1)} collective-permute-done((f32[2,8,128]{2,1,0:T(8,128)S(1)}, f32[2,8,128]{2,1,0:T(8,128)S(1)}, u32[]{:S(2)}, u32[]{:S(2)}) %collective-permute-start.5) | collective-permute-done | bytes 8224 | tf_op jit(solution)/shard_map/ppermute | solution.py:308
  31.3 0.0 collective-permute-done.6.refs_8_
  31.3 0.5 %second_image.1 = (f32[64,8,128]{2,1,0:T(8,128)S(1)}, f32[32,1,128]{2,1,0:T(1,128)S(1)}) custom-call(f32[64,8,128]{2,1,0:T(8,128)S(1)} %get-tuple-element.23.refs_0_.next_ref, f32[64,8,128]{2,1,0:T(8,128)S(1)} %kappa_rows.1.shifted_ref.refs_1_, f32[2,8,128]{2,1,0:T(8,128)S(1)} %collective-permute-done.4.refs_2_, ...), custom_call_target="tpu_custom_call" | custom-call | tf_op jit(solution)/shard_map/second_image/pallas_call | solution.py:360
  31.8 12.4 %all_to_all.5.sums_ref = f32[32,1,128]{2,1,0:T(1,128)S(1)} all-to-all(f32[32,1,128]{2,1,0:T(1,128)S(1)} %get-tuple-element.28), channel_id=1, replica_groups=mesh['orbit'=2,'lon'=16] {'orbit','lon'}, dimensions={0} | all-to-all | bytes 32768 | tf_op jit(solution)/shard_map/all_to_all | solution.py:367
  44.2 2.0 %combine.1 = (f32[64,1024]{1,0:T(8,128)}, f32[64,1024]{1,0:T(8,128)}) custom-call(f32[32,1,128]{2,1,0:T(1,128)S(1)} %all_to_all.5.sums_ref, f32[64,8,128]{2,1,0:T(8,128)S(1)} %get-tuple-element.17.refs_0_.refs_9_.start_ref, f32[64,8,128]{2,1,0:T(8,128)S(1)} %get-tuple-element.23.refs_0_.next_ref, f32[64,8,128]{2,1,0:T(8,128)S(1)} %get-tuple-element.26.refs_10_.right_ref, ...), custom_call_target="tpu_custom_call" | custom-call | tf_op jit(solution)/shard_map/combine/pallas_call | solution.py:368
Async XLA Ops:
  1.3 1.6 %copy-start = (bf16[32,1,256,128]{3,2,1,0:T(8,128)(2,1)S(1)}, bf16[32,1,256,128]{3,2,1,0:T(8,128)(2,1)}, u32[]{:S(2)}) copy-start(bf16[32,1,256,128]{3,2,1,0:T(8,128)(2,1)} %param.6) | copy-start | bytes 6291460
  2.9 0.8 %copy-start.1 = (f32[32,1,256]{2,1,0:T(1,128)S(1)}, f32[32,1,256]{2,1,0:T(1,128)}, u32[]{:S(2)}) copy-start(f32[32,1,256]{2,1,0:T(1,128)} %weight_ref.5) | copy-start | bytes 98308
  3.6 0.8 %copy-start.4 = (f32[32,1,256]{2,1,0:T(1,128)S(1)}, f32[32,1,256]{2,1,0:T(1,128)}, u32[]{:S(2)}) copy-start(f32[32,1,256]{2,1,0:T(1,128)} %value_ref.1) | copy-start | bytes 98308
  4.4 0.7 %copy-start.5 = (s32[32,1]{0,1:T(1,128)S(1)}, s32[32,1]{0,1:T(1,128)}, u32[]{:S(2)}) copy-start(s32[32,1]{0,1:T(1,128)} %param.9) | copy-start | bytes 388
  5.0 5.3 %copy-start.3 = (f32[64,1024]{1,0:T(8,128)S(1)}, f32[64,1024]{1,0:T(8,128)}, u32[]{:S(2)}) copy-start(f32[64,1024]{1,0:T(8,128)} %kappa_ref.1) | copy-start | bytes 786436
  7.3 15.7 %copy-start.2 = (f32[32,1,256]{2,1,0:T(1,128)S(1)}, f32[32,1,256]{2,1,0:T(1,128)}, u32[]{:S(2)}) copy-start(f32[32,1,256]{2,1,0:T(1,128)} %weight_ref.5) | copy-start | bytes 98308
  7.3 4.9 %collective-permute-start = (f32[72,128]{1,0:T(8,128)S(1)}, f32[72,128]{1,0:T(8,128)S(1)}, u32[]{:S(2)}, u32[]{:S(2)}) collective-permute-start(f32[72,128]{1,0:T(8,128)S(1)} %get-tuple-element.16.refs_0_), channel_id=1, source_target_pairs={{16,0},{0,16},{17,1},{1,17},{18,2},{2,18},{19,3},{3,19},{20,4},{4,... | collective-permute-start | bytes 110600 | tf_op jit(solution)/shard_map/ppermute | solution.py:300
  14.4 8.2 %collective-permute-start.3 = (f32[32,128]{1,0:T(8,128)S(1)}, f32[32,128]{1,0:T(8,128)S(1)}, u32[]{:S(2)}, u32[]{:S(2)}) collective-permute-start(f32[32,128]{1,0:T(8,128)S(1)} %normal_start.1.refs_7_), channel_id=1, source_target_pairs={{16,0},{0,16},{17,1},{1,17},{18,2},{2,18},{19,3},{3,19},{20,4},{4,... | collective-permute-start | bytes 49160 | tf_op jit(solution)/shard_map/ppermute | solution.py:300
  16.5 4.7 %collective-permute-start.1 = (f32[3,8,128]{2,1,0:T(8,128)S(1)}, f32[3,8,128]{2,1,0:T(8,128)S(1)}, u32[]{:S(2)}, u32[]{:S(2)}) collective-permute-start(f32[3,8,128]{2,1,0:T(8,128)S(1)} %get-tuple-element.18), channel_id=1, source_target_pairs={{0,1},{1,0},{2,3},{3,2},{4,5},{5,4},{6,7},{7,6},{8,9},{9,8},{10,11... | collective-permute-start | bytes 36872 | tf_op jit(solution)/shard_map/ppermute | solution.py:308
  16.5 6.1 %collective-permute-start.2 = (f32[3,8,128]{2,1,0:T(8,128)S(1)}, f32[3,8,128]{2,1,0:T(8,128)S(1)}, u32[]{:S(2)}, u32[]{:S(2)}) collective-permute-start(f32[3,8,128]{2,1,0:T(8,128)S(1)} %get-tuple-element.19), channel_id=1, source_target_pairs={{0,15},{1,2},{2,1},{3,4},{4,3},{5,6},{6,5},{7,8},{8,7},{9,10},{10,... | collective-permute-start | bytes 36872 | tf_op jit(solution)/shard_map/ppermute | solution.py:308
  24.9 6.4 %collective-permute-start.6 = (f32[32,128]{1,0:T(8,128)S(1)}, f32[32,128]{1,0:T(8,128)S(1)}, u32[]{:S(2)}, u32[]{:S(2)}) collective-permute-start(f32[32,128]{1,0:T(8,128)S(1)} %normal_next.1.refs_7_), channel_id=1, source_target_pairs={{16,0},{0,16},{17,1},{1,17},{18,2},{2,18},{19,3},{3,19},{20,4},{4,... | collective-permute-start | bytes 49160 | tf_op jit(solution)/shard_map/ppermute | solution.py:300
  25.5 4.1 %collective-permute-start.4 = (f32[2,8,128]{2,1,0:T(8,128)S(1)}, f32[2,8,128]{2,1,0:T(8,128)S(1)}, u32[]{:S(2)}, u32[]{:S(2)}) collective-permute-start(f32[2,8,128]{2,1,0:T(8,128)S(1)} %get-tuple-element.24), channel_id=1, source_target_pairs={{0,1},{1,0},{2,3},{3,2},{4,5},{5,4},{6,7},{7,6},{8,9},{9,8},{10,11... | collective-permute-start | bytes 24584 | tf_op jit(solution)/shard_map/ppermute | solution.py:308
  25.5 5.8 %collective-permute-start.5 = (f32[2,8,128]{2,1,0:T(8,128)S(1)}, f32[2,8,128]{2,1,0:T(8,128)S(1)}, u32[]{:S(2)}, u32[]{:S(2)}) collective-permute-start(f32[2,8,128]{2,1,0:T(8,128)S(1)} %get-tuple-element.25), channel_id=1, source_target_pairs={{0,15},{1,2},{2,1},{3,4},{4,3},{5,6},{6,5},{7,8},{8,7},{9,10},{10,... | collective-permute-start | bytes 24584 | tf_op jit(solution)/shard_map/ppermute | solution.py:308
where the time goes:
time: 46.5 us; the launch traced here: 46.2 us
  starting transfers between devices  14.5 us (31%)
  blocking collectives  12.4 us (27%)
  Pallas kernels  9.35 us (20%)
  waiting for transfers between devices  4.83 us (10%)
  local copies, waits for them, and re-layouts  3.76 us (8%)
  between operations  1.36 us (3%)
    all_to_all x1, blocking collectives, per_device(): sums = lax.all_to_all(sums, ('orbit', 'lon'), 0, 0, tiled=True)  12.4 us
    ppermute x2, starting transfers between devices, from_neighbours(): lax.ppermute(odd, 'lon', odd_pairs)  8.8 us
    ppermute x3, starting transfers between devices, from_others(): lax.ppermute(value, 'orbit', [((i + step) % orbits, i) for i in range(orb...  5.69 us
    pallas_call x2, Pallas kernels, normal_slots(): call(normal_kernel, (((slots, width), F32),), [smem, vmem, vmem, vmem], [...  3.82 us
    unnamed x12, local copies, waits for them, and re-layouts  3.76 us
    ppermute x2, waiting for transfers between devices, from_neighbours(): lax.ppermute(odd, 'lon', odd_pairs)  3.04 us
    pallas_call x1, Pallas kernels, per_device(): call(functools.partial(data_kernel, orbits), (((2 * slots + GROUP, width)...  2.22 us
    pallas_call x1, Pallas kernels, per_device(): call(last_kernel, ((kappa2.shape, F32), (kappa2.shape, F32)), [vmem] * 6,...  2 us
  transfers between devices with their start and end apart: 7, of which 3 were waited for; matrix products, arithmetic and copies ran while one was open for 0% of the time, Pallas kernels for 0%

commit v1 on v0

--- a/solution.py
+++ b/solution.py
@@ -13,6 +13,9 @@
 F32 = jnp.float32
 BF16 = jnp.bfloat16
 VMEM_BYTES = 48 * 1024 * 1024
+DATA_VMEM_BYTES = 59 * 1024 * 1024
+CHUNK = 16
+WORK = 1 << 32
 
 
 def two_terms(value):
@@ -60,17 +63,40 @@
 
 
 def data_kernel(
-    orbits, count_ref, map_ref, interp_ref, value_ref, weight_ref, message_ref, matrices_ref, sems
+    orbits,
+    count_in,
+    map_in,
+    interp_in,
+    value_in,
+    weight_in,
+    message_ref,
+    matrices_ref,
+    weight_ref,
+    pick_ref,
+    count_ref,
+    map_ref,
+    value_rows,
+    weight_rows,
+    sems,
 ):
     slots = matrices_ref.shape[0]
-    groups = slots // GROUP
-    copies = []
-    for group in range(groups):
-        part = pl.ds(group * GROUP, GROUP)
-        copies.append(
-            pltpu.make_async_copy(interp_ref.at[part], matrices_ref.at[part], sems.at[group])
+    pairs = ((weight_in, weight_rows), (value_in, value_rows), (map_in, map_ref), (count_in, count_ref))
+    small = [
+        pltpu.make_async_copy(source, target, sems.at[index])
+        for index, (source, target) in enumerate(pairs)
+    ]
+    large = []
+    for index in range(slots // CHUNK):
+        part = pl.ds(index * CHUNK, CHUNK)
+        large.append(
+            pltpu.make_async_copy(
+                interp_in.at[part], matrices_ref.at[part], sems.at[len(small) + index]
+            )
         )
-        copies[-1].start()
+    for copy in small + large:
+        copy.start()
+    for copy in small:
+        copy.wait()
     orbit = lax.axis_index("orbit")
     total = orbits * slots
     place = lax.broadcasted_iota(jnp.int32, (GROUP, LANES), 0) * LANES
@@ -83,31 +109,46 @@
         target_row = jnp.where(slot_here == slot, live_target, target_row)
     target_row = jnp.where(place < 2 * total, target_row, 0)
     message_ref[pl.ds(2 * slots, GROUP), :] = target_row.astype(F32)
-    for group in range(groups):
+    row = lax.broadcasted_iota(jnp.int32, (GROUP, pick_ref.shape[1]), 0)
+    cell = lax.broadcasted_iota(jnp.int32, row.shape, 1)
+    for group in range(slots // GROUP):
+        target = jnp.zeros(row.shape, jnp.int32)
+        for slot in range(GROUP):
+            target = jnp.where(row == slot, map_ref[group * GROUP + slot], target)
         part = pl.ds(group * GROUP, GROUP)
-        weights = weight_ref[part, 0, :]
-        scaled = (weights * value_ref[part, 0, :]).astype(BF16)
-        scaled = jnp.concatenate([scaled, scaled], axis=0)
-        weight_terms = stacked_terms(weights)
-        first = jnp.zeros((2 * GROUP, LANES), F32)
+        pick_ref[part, :] = jnp.where(cell == target, 1.0, 0.0).astype(BF16)
+    for group in range(slots // GROUP):
+        part = pl.ds(group * GROUP, GROUP)
+        weights = weight_rows[part, 0, :]
+        weight_ref[part, :] = weights
+        scaled = (weights * value_rows[part, 0, :]).astype(BF16)
+        high, low = two_terms(weights)
+        rows = jnp.concatenate([scaled, high, low, low], axis=0)
+        first = jnp.zeros((GROUP, LANES), F32)
         second = jnp.zeros((GROUP, LANES), F32)
-        copies[group].wait()
         for slot in range(GROUP):
-            matrix = matrices_ref[group * GROUP + slot]
-            first = pick_row(first, dot(scaled, matrix), slot)
-            wide = matrix.astype(F32)
-            square_high, square_low = two_terms(wide * wide)
-            product = dot(weight_terms, square_high) + dot(weight_terms, square_low)
-            second = pick_row(second, fold_terms(product), slot)
-        message_ref[part, :] = first[:GROUP]
+            index = group * GROUP + slot
+            if index % CHUNK == 0:
+                large[index // CHUNK].wait()
+            matrix = matrices_ref[index]
+            both = dot(rows, jnp.concatenate([matrix, matrix * matrix], axis=1))
+            squares = both[GROUP : 2 * GROUP, LANES:] + both[2 * GROUP : 3 * GROUP, LANES:]
+            first = pick_row(first, both[:GROUP, :LANES], slot)
+            second = pick_row(second, squares, slot)
+        message_ref[part, :] = first
         message_ref[pl.ds(slots + group * GROUP, GROUP), :] = second
 
 
-def kappa_kernel(kappa_ref, shifted_ref):
-    columns, pieces, _ = shifted_ref.shape
-    for piece in range(pieces):
-        part = kappa_ref[:, pl.ds(piece * LANES, LANES)]
-        shifted_ref[:, piece, :] = part + 4.0
+def block_kernel(kappa_ref, matrices_ref, weight_ref, shifted_ref, blocks_ref):
+    shifted_ref[...] = kappa_ref[...].reshape(shifted_ref.shape) + 4.0
+    width = matrices_ref.shape[2]
+    for slot in range(matrices_ref.shape[0]):
+        matrix = matrices_ref[slot]
+        weighted = matrix.T.astype(F32) * weight_ref[pl.ds(slot, 1), :]
+        high, low = two_terms(fold_terms(dot(stacked_terms(weighted), matrix)))
+        columns = pl.ds(slot % 2 * width, width)
+        blocks_ref[slot // 2, pl.ds(0, width), columns] = high
+        blocks_ref[slot // 2, pl.ds(width, width), columns] = low
 
 
 def gather_messages(orbits, slots, message_refs, order_ref):
@@ -161,33 +202,34 @@
 
 def store_edges(parity, top, bottom, even_ref, odd_ref):
     flip = parity()
+    used = top.shape[0]
     even_ref[...] = jnp.where(flip, top, bottom)
-    odd_ref[...] = jnp.where(flip, bottom, top)
+    odd_ref[:used] = jnp.where(flip, bottom, top)
+    if odd_ref.shape[0] > used:
+        odd_ref[used:] = jnp.zeros((odd_ref.shape[0] - used,) + top.shape[1:], F32)
 
 
 def load_edges(parity, even_ref, odd_ref):
     flip = parity()
-    even, odd = even_ref[...], odd_ref[...]
+    even = even_ref[...]
+    odd = odd_ref[: even.shape[0]]
     return jnp.where(flip, even, odd), jnp.where(flip, odd, even)
 
 
-def normal_kernel(map_ref, field_ref, weight_ref, matrices_ref, out_ref, picked_ref):
-    slots = matrices_ref.shape[0]
-    for slot in range(slots):
-        picked_ref[pl.ds(slot, 1), :] = field_ref[pl.ds(map_ref[slot], 1), :]
-    for group in range(slots // GROUP):
-        part = pl.ds(group * GROUP, GROUP)
-        cells = stacked_terms(picked_ref[part, :])
-        predicted = jnp.zeros((GROUP, matrices_ref.shape[1]), F32)
-        for slot in range(GROUP):
-            product = dot_transposed(cells, matrices_ref[group * GROUP + slot])
-            predicted = pick_row(predicted, fold_terms(product), slot)
-        scaled = stacked_terms(weight_ref[part, 0, :] * predicted)
-        back = jnp.zeros((GROUP, LANES), F32)
-        for slot in range(GROUP):
-            product = dot(scaled, matrices_ref[group * GROUP + slot])
-            back = pick_row(back, fold_terms(product), slot)
-        out_ref[part, :] = back
+def normal_kernel(pick_ref, field_ref, blocks_ref, edge_ref, out_ref, edge_out_ref):
+    edge_out_ref[...] = edge_ref[...]
+    width = field_ref.shape[1]
+    picked = dot(pick_ref[...], jnp.concatenate(two_terms(field_ref[...]), axis=1))
+    picked = picked[:, :width] + picked[:, width:]
+    for group in range(picked.shape[0] // GROUP):
+        rows = stacked_terms(picked[group * GROUP : (group + 1) * GROUP])
+        rows = jnp.concatenate([rows, rows], axis=1)
+        total = jnp.zeros((GROUP, width), F32)
+        for slot in range(0, GROUP, 2):
+            product = fold_terms(dot(rows, blocks_ref[(group * GROUP + slot) // 2]))
+            total = pick_row(total, product[:, :width], slot)
+            total = pick_row(total, product[:, width:], slot + 1)
+        out_ref[pl.ds(group * GROUP, GROUP), :] = total
 
 
 def extended(field, top, bottom):
@@ -259,15 +301,10 @@
     later_alpha = later / later_energy
     on_start = alpha + later_alpha * grown
     on_next = -alpha * later_alpha
-    columns, pieces, _ = start_ref.shape
-    for piece in range(pieces):
-        lanes = pl.ds(piece * LANES, LANES)
-        out_ref[:, lanes] = on_start * start_ref[:, piece, :] + on_next * next_ref[:, piece, :]
-        residual_ref[:, lanes] = (
-            right_ref[:, piece, :]
-            - on_start * first_ref[:, piece, :]
-            - on_next * second_ref[:, piece, :]
-        )
+    out = on_start * start_ref[...] + on_next * next_ref[...]
+    residual = right_ref[...] - on_start * first_ref[...] - on_next * second_ref[...]
+    out_ref[...] = out.reshape(out_ref.shape)
+    residual_ref[...] = residual.reshape(residual_ref.shape)
 
 
 def per_device(orbits, bands, interp, obs_value, obs_weight, block_map, live_count, kappa2):
@@ -282,16 +319,19 @@
         return lax.rem(lax.axis_index("lon"), 2) == 1 if paired else False
 
     vmem = pl.BlockSpec(memory_space=pltpu.VMEM)
-    smem = pl.BlockSpec(memory_space=pltpu.SMEM)
-
-    def call(kernel, outs, in_specs, scratch=(), name=None):
+    anywhere = pl.BlockSpec(memory_space=pl.ANY)
+
+    def call(kernel, outs, in_specs, scratch=(), name=None, limit=VMEM_BYTES, work=0):
+        held = pltpu.VMEM if name != "combine" else jax.ShapeDtypeStruct
+        cost = pl.CostEstimate(flops=work, bytes_accessed=0, transcendentals=0) if work else None
         return pl.pallas_call(
             kernel,
-            out_shape=tuple(jax.ShapeDtypeStruct(shape, dtype) for shape, dtype in outs),
+            out_shape=tuple(held(shape, dtype) for shape, dtype in outs),
             in_specs=in_specs,
             out_specs=tuple(vmem for _ in outs),
             scratch_shapes=list(scratch),
-            compiler_params=pltpu.CompilerParams(vmem_limit_bytes=VMEM_BYTES),
+            compiler_params=pltpu.CompilerParams(vmem_limit_bytes=limit),
+            cost_estimate=cost,
             name=name,
         )
 
@@ -311,52 +351,71 @@
         return lax.ppermute(odd, "lon", down), lax.ppermute(even, "lon", up)
 
     matrices_in = interp.reshape(slots, observations, width)
-    targets = block_map.reshape(slots)
-    message, matrices = call(
+    line = (slots, 1, observations)
+    message, matrices, weights, pick = call(
         functools.partial(data_kernel, orbits),
-        (((2 * slots + GROUP, width), F32), ((slots, observations, width), BF16)),
-        [smem, smem, pl.BlockSpec(memory_space=pl.ANY), vmem, vmem],
-        [pltpu.SemaphoreType.DMA((slots // GROUP,))],
+        (
+            ((2 * slots + GROUP, width), F32),
+            ((slots, observations, width), BF16),
+            ((slots, observations), F32),
+            ((slots, cells), BF16),
+        ),
+        [anywhere] * 5,
+        [
+            pltpu.SMEM((1,), jnp.int32),
+            pltpu.SMEM((slots,), jnp.int32),
+            pltpu.VMEM(line, F32),
+            pltpu.VMEM(line, F32),
+            pltpu.SemaphoreType.DMA((4 + slots // CHUNK,)),
+        ],
         "data_terms",
-    )(live_count.reshape(1), targets, matrices_in, obs_value, obs_weight)
+        DATA_VMEM_BYTES,
+    )(live_count.reshape(1), block_map.reshape(slots), matrices_in, obs_value, obs_weight)
     messages = from_others(message)
-    (shifted,) = call(kappa_kernel, ((field_shape, F32),), [vmem], (), "kappa_rows")(kappa2)
+    shifted, blocks = call(
+        block_kernel,
+        ((field_shape, F32), ((slots // 2, 2 * width, 2 * width), BF16)),
+        [vmem] * 3,
+        (),
+        "blocks",
+        work=WORK,
+    )(kappa2, matrices, weights)
 
     order = pltpu.VMEM((orbits * slots, width), F32)
     edge_width = -(-2 * orbits * slots // LANES) * LANES
     rim = ((3, pieces, width), F32)
     edge = ((2, pieces, width), F32)
+    wide_edge = ((max(slots // pieces + 1, rim[0][0]), pieces, width), F32)
     field = (field_shape, F32)
     start, right_side, precond, scatter, even, odd = call(
         functools.partial(start_kernel, orbits, parity),
-        (field, field, field, ((cells, edge_width), BF16), rim, rim),
+        (field, field, field, ((cells, edge_width), BF16), rim, wide_edge),
         [vmem] * (1 + orbits),
         [order],
         "start",
     )(shifted, *messages)
 
-    def normal_slots(value, name):
-        (out,) = call(
+    def exchanged(value, even, odd, name):
+        terms, odd = call(
             normal_kernel,
-            (((slots, width), F32),),
-            [smem, vmem, vmem, vmem],
-            [pltpu.VMEM((slots, width), F32)],
+            (((slots, width), F32), (odd.shape, F32)),
+            [vmem] * 4,
+            (),
             name,
-        )(targets, value.reshape(cells, width), obs_weight, matrices)
-        return from_others(out)
-
-    rim_even, rim_odd = from_neighbours(even, odd)
-    terms = normal_slots(start, "normal_start")
+            work=WORK,
+        )(pick, value.reshape(cells, width), blocks, odd)
+        return from_others(terms), from_neighbours(even, odd)
+
+    terms, (rim_even, rim_odd) = exchanged(start, even, odd, "normal_start")
     first, following, even, odd = call(
         functools.partial(first_kernel, parity, orbits),
-        (field, field, edge, edge),
+        (field, field, edge, wide_edge),
         [vmem] * (8 + orbits),
         [order],
         "first_image",
     )(start, shifted, rim_even, rim_odd, rim_even, rim_odd, scatter, *terms, precond)
 
-    even, odd = from_neighbours(even, odd)
-    terms = normal_slots(following, "normal_next")
+    terms, (even, odd) = exchanged(following, even, odd, "normal_next")
     second, sums = call(
         functools.partial(second_kernel, parity, orbits),
         (field, ((orbits * bands, 1, width), F32)),

time: 46.5 us -> 35.7 us (0.77)
  local copies, waits for them, and re-layouts: 3.76 us -> 0.01 us
  starting transfers between devices: 14.5 us -> 11.6 us
  Pallas kernels: 9.35 us -> 7.22 us
  blocking collectives: 12.4 us -> 10.4 us
    unnamed x12 -> x2, local copies, waits for them, and re-layouts: 3.76 us -> 0.01 us
    ppermute x2, starting transfers between devices: 8.8 us -> 5.63 us  [from_neighbours(): lax.ppermute(odd, 'lon', odd_pairs)]
    ppermute x2, waiting for transfers between devices: 3.04 us -> 0.01 us  [from_neighbours(): lax.ppermute(odd, 'lon', odd_pairs)]
    ppermute x2, waiting for transfers between devices: 0.01 us -> 2.34 us  [from_neighbours(): lax.ppermute(even, 'lon', even_pairs)]
    all_to_all x1, blocking collectives: 12.4 us -> 10.4 us  [per_device(): sums = lax.all_to_all(sums, ('orbit', 'lon'), 0, 0, tiled=True)]
    pallas_call x3, Pallas kernels: 3.97 us -> 2.66 us  [the longest x1 1.52 us: per_device(): call(block_kernel, ((field_shape, F32), ((slots // 2, 2 * width, 2 * widt...]
    pallas_call x1, Pallas kernels: 2 us -> 1.09 us  [per_device(): call(last_kernel, ((kappa2.shape, F32), (kappa2.shape, F32)), [vmem] * 6,...]
    ppermute x3, waiting for transfers between devices: 1.78 us -> 2.54 us  [from_others(): lax.ppermute(value, 'orbit', [((i + step) % orbits, i) for i in range(orb...]
  transfers between devices with their start and end apart: 7 -> 7, of which waited for: 3 -> 5; matrix products, arithmetic and copies ran while one was open for 0% -> 0% of each run, Pallas kernels for 0% -> 4%
where the time goes in v1:
time: 35.7 us; the launch traced here: 35.5 us
  starting transfers between devices  11.6 us (32%)
  blocking collectives  10.4 us (29%)
  Pallas kernels  7.22 us (20%)
  waiting for transfers between devices  4.89 us (14%)
  between operations  1.37 us (4%)
    all_to_all x1, blocking collectives, per_device(): sums = lax.all_to_all(sums, ('orbit', 'lon'), 0, 0, tiled=True)  10.4 us
    ppermute x3, starting transfers between devices, from_others(): lax.ppermute(value, 'orbit', [((i + step) % orbits, i) for i in range(orb...  6 us
    ppermute x2, starting transfers between devices, from_neighbours(): lax.ppermute(odd, 'lon', odd_pairs)  5.63 us
    ppermute x3, waiting for transfers between devices, from_others(): lax.ppermute(value, 'orbit', [((i + step) % orbits, i) for i in range(orb...  2.54 us
    ppermute x2, waiting for transfers between devices, from_neighbours(): lax.ppermute(even, 'lon', even_pairs)  2.34 us
    pallas_call x1, Pallas kernels, per_device(): call(functools.partial(data_kernel, orbits), (((2 * slots + GROUP, width)...  2.32 us
    pallas_call x1, Pallas kernels, per_device(): call(block_kernel, ((field_shape, F32), ((slots // 2, 2 * width, 2 * widt...  1.52 us
    pallas_call x2, Pallas kernels, exchanged(): call(normal_kernel, (((slots, width), F32), (odd.shape, F32)), [vmem] * 4...  1.14 us
  transfers between devices with their start and end apart: 7, of which 5 were waited for; matrix products, arithmetic and copies ran while one was open for 0% of the time, Pallas kernels for 4%

profile of v1, /device:TPU:0, one launch (start us, length us, event | category | flops | bytes accessed | tf_op | source)
XLA Modules:
  0.0 35.5 jit_solution(13118586428628453868)
XLA Ops:
  0.6 0.0 copy-start
  1.3 2.3 %data_terms.1 = (f32[72,128]{1,0:T(8,128)S(1)}, bf16[32,256,128]{2,1,0:T(8,128)(2,1)S(1)}, f32[32,256]{1,0:T(8,128)S(1)}, bf16[32,512]{1,0:T(8,128)(2,1)S(1)}) custom-call(s32[1]{0:T(128)} %bitcast.5.count_in, s32[32]{0:T(128)} %bitcast.9, bf16[32,256,128]{2,1,0:T(8,128)(2,1)} %bitcast.8, f32[32,1,256]{2,1,0:T(1,128)} %value_in.1, f32[32,1,256]{2,1,0:T(1,128)} %weight_in.1), custom_call_target="tpu_custom_call" | custom-call | tf_op jit(solution)/shard_map/data_terms/pallas_call | solution.py:355
  3.7 3.0 %collective-permute-start = (f32[72,128]{1,0:T(8,128)S(1)}, f32[72,128]{1,0:T(8,128)S(1)}, u32[]{:S(2)}, u32[]{:S(2)}) collective-permute-start(f32[72,128]{1,0:T(8,128)S(1)} %get-tuple-element.27.refs_0_), channel_id=1, source_target_pairs={{16,0},{0,16},{17,1},{1,17},{18,2},{2,18},{19,3},{3,19},{20,4},{4,... | collective-permute-start | bytes 110600 | tf_op jit(solution)/shard_map/ppermute | solution.py:340
  6.7 0.0 copy-done
  6.7 1.5 %blocks.1 = (f32[64,8,128]{2,1,0:T(8,128)S(1)}, bf16[16,256,256]{2,1,0:T(8,128)(2,1)S(1)}) custom-call(f32[64,1024]{1,0:T(8,128)S(1)} %copy-done, bf16[32,256,128]{2,1,0:T(8,128)(2,1)S(1)} %get-tuple-element.24.matrices_ref, f32[32,256]{1,0:T(8,128)S(1)} %get-tuple-element.25.weight_ref), custom_call_target="tpu_custom_call" | custom-call | flops 4294967296 | tf_op jit(solution)/shard_map/blocks/pallas_call | solution.py:375
  8.2 0.4 %collective-permute-done.refs_1_ = f32[72,128]{1,0:T(8,128)S(1)} collective-permute-done((f32[72,128]{1,0:T(8,128)S(1)}, f32[72,128]{1,0:T(8,128)S(1)}, u32[]{:S(2)}, u32[]{:S(2)}) %collective-permute-start) | collective-permute-done | bytes 36896 | tf_op jit(solution)/shard_map/ppermute | solution.py:340
  8.6 0.3 start.1
  8.9 0.6 %normal_start.1 = (f32[32,128]{1,0:T(8,128)S(1)}, f32[5,8,128]{2,1,0:T(8,128)S(1)}) custom-call(bf16[32,512]{1,0:T(8,128)(2,1)S(1)} %get-tuple-element.30.pick_ref, f32[512,128]{1,0:T(8,128)S(1)} %bitcast.6, bf16[16,256,256]{2,1,0:T(8,128)(2,1)S(1)} %get-tuple-element.31.blocks_ref, f32[5,8,128]{2,1,0:T(8,128)S(1)} %get-tuple-element.32.edge_ref), custom_call_target="tpu_custom_call" | custom-call | flops 4294967296 | tf_op jit(solution)/shard_map/normal_start/pallas_call | solution.py:399
  9.4 3.4 %collective-permute-start.2 = (f32[5,8,128]{2,1,0:T(8,128)S(1)}, f32[5,8,128]{2,1,0:T(8,128)S(1)}, u32[]{:S(2)}, u32[]{:S(2)}) collective-permute-start(f32[5,8,128]{2,1,0:T(8,128)S(1)} %get-tuple-element.33), channel_id=1, source_target_pairs={{0,15},{1,2},{2,1},{3,4},{4,3},{5,6},{6,5},{7,8},{8,7},{9,10},{10,... | collective-permute-start | bytes 61448 | tf_op jit(solution)/shard_map/ppermute | solution.py:348
  12.9 1.5 %collective-permute-start.3 = (f32[32,128]{1,0:T(8,128)S(1)}, f32[32,128]{1,0:T(8,128)S(1)}, u32[]{:S(2)}, u32[]{:S(2)}) collective-permute-start(f32[32,128]{1,0:T(8,128)S(1)} %get-tuple-element.35.refs_7_), channel_id=1, source_target_pairs={{16,0},{0,16},{17,1},{1,17},{18,2},{2,18},{19,3},{3,19},{20,4},{4,... | collective-permute-start | bytes 49160 | tf_op jit(solution)/shard_map/ppermute | solution.py:340
  14.4 0.0 collective-permute-start.1
  14.4 1.2 %collective-permute-done.1.refs_2_.refs_4_ = f32[3,8,128]{2,1,0:T(8,128)S(1)} collective-permute-done((f32[3,8,128]{2,1,0:T(8,128)S(1)}, f32[3,8,128]{2,1,0:T(8,128)S(1)}, u32[]{:S(2)}, u32[]{:S(2)}) %collective-permute-start.1) | collective-permute-done | bytes 12320 | tf_op jit(solution)/shard_map/ppermute | solution.py:348
  15.5 1.1 %collective-permute-done.3.refs_8_ = f32[32,128]{1,0:T(8,128)S(1)} collective-permute-done((f32[32,128]{1,0:T(8,128)S(1)}, f32[32,128]{1,0:T(8,128)S(1)}, u32[]{:S(2)}, u32[]{:S(2)}) %collective-permute-start.3) | collective-permute-done | bytes 16416 | tf_op jit(solution)/shard_map/ppermute | solution.py:340
  16.6 0.0 collective-permute-done.2.refs_3_.refs_5_
  16.6 0.4 %first_image.1 = (f32[64,8,128]{2,1,0:T(8,128)S(1)}, f32[64,8,128]{2,1,0:T(8,128)S(1)}, f32[2,8,128]{2,1,0:T(8,128)S(1)}, f32[5,8,128]{2,1,0:T(8,128)S(1)}) custom-call(f32[64,8,128]{2,1,0:T(8,128)S(1)} %get-tuple-element.28.refs_0_.refs_9_.start_ref, f32[64,8,128]{2,1,0:T(8,128)S(1)} %get-tuple-element.26.shifted_ref.refs_1_, ...), custom_call_target="tpu_custom_call" | custom-call | tf_op jit(solution)/shard_map/first_image/pallas_call | solution.py:410
  17.0 0.6 %normal_next.1 = (f32[32,128]{1,0:T(8,128)S(1)}, f32[5,8,128]{2,1,0:T(8,128)S(1)}) custom-call(bf16[32,512]{1,0:T(8,128)(2,1)S(1)} %get-tuple-element.30.pick_ref, f32[512,128]{1,0:T(8,128)S(1)} %bitcast.7, bf16[16,256,256]{2,1,0:T(8,128)(2,1)S(1)} %get-tuple-element.31.blocks_ref, f32[5,8,128]{2,1,0:T(8,128)S(1)} %get-tuple-element.39.edge_ref), custom_call_target="tpu_custom_call" | custom-call | flops 4294967296 | tf_op jit(solution)/shard_map/normal_next/pallas_call | solution.py:399
  17.6 2.2 %collective-permute-start.5 = (f32[5,8,128]{2,1,0:T(8,128)S(1)}, f32[5,8,128]{2,1,0:T(8,128)S(1)}, u32[]{:S(2)}, u32[]{:S(2)}) collective-permute-start(f32[5,8,128]{2,1,0:T(8,128)S(1)} %get-tuple-element.40), channel_id=1, source_target_pairs={{0,15},{1,2},{2,1},{3,4},{4,3},{5,6},{6,5},{7,8},{8,7},{9,10},{10,... | collective-permute-start | bytes 61448 | tf_op jit(solution)/shard_map/ppermute | solution.py:348
  19.8 1.5 %collective-permute-start.6 = (f32[32,128]{1,0:T(8,128)S(1)}, f32[32,128]{1,0:T(8,128)S(1)}, u32[]{:S(2)}, u32[]{:S(2)}) collective-permute-start(f32[32,128]{1,0:T(8,128)S(1)} %get-tuple-element.41.refs_7_), channel_id=1, source_target_pairs={{16,0},{0,16},{17,1},{1,17},{18,2},{2,18},{19,3},{3,19},{20,4},{4,... | collective-permute-start | bytes 49160 | tf_op jit(solution)/shard_map/ppermute | solution.py:340
  21.3 0.0 collective-permute-start.4
  21.3 1.2 %collective-permute-done.4.refs_2_ = f32[2,8,128]{2,1,0:T(8,128)S(1)} collective-permute-done((f32[2,8,128]{2,1,0:T(8,128)S(1)}, f32[2,8,128]{2,1,0:T(8,128)S(1)}, u32[]{:S(2)}, u32[]{:S(2)}) %collective-permute-start.4) | collective-permute-done | bytes 8224 | tf_op jit(solution)/shard_map/ppermute | solution.py:348
  22.5 1.1 %collective-permute-done.6.refs_8_ = f32[32,128]{1,0:T(8,128)S(1)} collective-permute-done((f32[32,128]{1,0:T(8,128)S(1)}, f32[32,128]{1,0:T(8,128)S(1)}, u32[]{:S(2)}, u32[]{:S(2)}) %collective-permute-start.6) | collective-permute-done | bytes 16416 | tf_op jit(solution)/shard_map/ppermute | solution.py:340
  23.5 0.0 collective-permute-done.5.refs_3_
  23.5 0.5 %second_image.1 = (f32[64,8,128]{2,1,0:T(8,128)S(1)}, f32[32,1,128]{2,1,0:T(1,128)S(1)}) custom-call(f32[64,8,128]{2,1,0:T(8,128)S(1)} %get-tuple-element.37.refs_0_.next_ref, f32[64,8,128]{2,1,0:T(8,128)S(1)} %get-tuple-element.26.shifted_ref.refs_1_, f32[2,8,128]{2,1,0:T(8,128)S(1)} %collective-permute-done.4.refs_2_, ...), custom_call_target="tpu_custom_call" | custom-call | tf_op jit(solution)/shard_map/second_image/pallas_call | solution.py:419
  24.0 10.4 %all_to_all.5.sums_ref = f32[32,1,128]{2,1,0:T(1,128)S(1)} all-to-all(f32[32,1,128]{2,1,0:T(1,128)S(1)} %get-tuple-element.44), channel_id=1, replica_groups=mesh['orbit'=2,'lon'=16] {'orbit','lon'}, dimensions={0} | all-to-all | bytes 32768 | tf_op jit(solution)/shard_map/all_to_all | solution.py:426
  34.4 1.1 %combine.1 = (f32[64,1024]{1,0:T(8,128)}, f32[64,1024]{1,0:T(8,128)}) custom-call(f32[32,1,128]{2,1,0:T(1,128)S(1)} %all_to_all.5.sums_ref, f32[64,8,128]{2,1,0:T(8,128)S(1)} %get-tuple-element.28.refs_0_.refs_9_.start_ref, f32[64,8,128]{2,1,0:T(8,128)S(1)} %get-tuple-element.37.refs_0_.next_ref, f32[64,8,128]{2,1,0:T(8,128)S(1)} %get-tuple-element.42.refs_10_.right_ref, ...), custom_call_target="tpu_custom_call" | custom-call | tf_op jit(solution)/shard_map/combine/pallas_call | solution.py:427
Async XLA Ops:
  0.6 6.0 %copy-start = (f32[64,1024]{1,0:T(8,128)S(1)}, f32[64,1024]{1,0:T(8,128)}, u32[]{:S(2)}) copy-start(f32[64,1024]{1,0:T(8,128)} %kappa_ref.1) | copy-start | bytes 786436
  3.7 4.9 %collective-permute-start = (f32[72,128]{1,0:T(8,128)S(1)}, f32[72,128]{1,0:T(8,128)S(1)}, u32[]{:S(2)}, u32[]{:S(2)}) collective-permute-start(f32[72,128]{1,0:T(8,128)S(1)} %get-tuple-element.27.refs_0_), channel_id=1, source_target_pairs={{16,0},{0,16},{17,1},{1,17},{18,2},{2,18},{19,3},{3,19},{20,4},{4,... | collective-permute-start | bytes 110600 | tf_op jit(solution)/shard_map/ppermute | solution.py:340
  9.4 7.2 %collective-permute-start.2 = (f32[5,8,128]{2,1,0:T(8,128)S(1)}, f32[5,8,128]{2,1,0:T(8,128)S(1)}, u32[]{:S(2)}, u32[]{:S(2)}) collective-permute-start(f32[5,8,128]{2,1,0:T(8,128)S(1)} %get-tuple-element.33), channel_id=1, source_target_pairs={{0,15},{1,2},{2,1},{3,4},{4,3},{5,6},{6,5},{7,8},{8,7},{9,10},{10,... | collective-permute-start | bytes 61448 | tf_op jit(solution)/shard_map/ppermute | solution.py:348
  12.9 3.7 %collective-permute-start.3 = (f32[32,128]{1,0:T(8,128)S(1)}, f32[32,128]{1,0:T(8,128)S(1)}, u32[]{:S(2)}, u32[]{:S(2)}) collective-permute-start(f32[32,128]{1,0:T(8,128)S(1)} %get-tuple-element.35.refs_7_), channel_id=1, source_target_pairs={{16,0},{0,16},{17,1},{1,17},{18,2},{2,18},{19,3},{3,19},{20,4},{4,... | collective-permute-start | bytes 49160 | tf_op jit(solution)/shard_map/ppermute | solution.py:340
  14.4 1.2 %collective-permute-start.1 = (f32[3,8,128]{2,1,0:T(8,128)S(1)}, f32[3,8,128]{2,1,0:T(8,128)S(1)}, u32[]{:S(2)}, u32[]{:S(2)}) collective-permute-start(f32[3,8,128]{2,1,0:T(8,128)S(1)} %get-tuple-element.29), channel_id=1, source_target_pairs={{0,1},{1,0},{2,3},{3,2},{4,5},{5,4},{6,7},{7,6},{8,9},{9,8},{10,11... | collective-permute-start | bytes 36872 | tf_op jit(solution)/shard_map/ppermute | solution.py:348
  17.6 6.0 %collective-permute-start.5 = (f32[5,8,128]{2,1,0:T(8,128)S(1)}, f32[5,8,128]{2,1,0:T(8,128)S(1)}, u32[]{:S(2)}, u32[]{:S(2)}) collective-permute-start(f32[5,8,128]{2,1,0:T(8,128)S(1)} %get-tuple-element.40), channel_id=1, source_target_pairs={{0,15},{1,2},{2,1},{3,4},{4,3},{5,6},{6,5},{7,8},{8,7},{9,10},{10,... | collective-permute-start | bytes 61448 | tf_op jit(solution)/shard_map/ppermute | solution.py:348
  19.8 3.7 %collective-permute-start.6 = (f32[32,128]{1,0:T(8,128)S(1)}, f32[32,128]{1,0:T(8,128)S(1)}, u32[]{:S(2)}, u32[]{:S(2)}) collective-permute-start(f32[32,128]{1,0:T(8,128)S(1)} %get-tuple-element.41.refs_7_), channel_id=1, source_target_pairs={{16,0},{0,16},{17,1},{1,17},{18,2},{2,18},{19,3},{3,19},{20,4},{4,... | collective-permute-start | bytes 49160 | tf_op jit(solution)/shard_map/ppermute | solution.py:340
  21.3 1.2 %collective-permute-start.4 = (f32[2,8,128]{2,1,0:T(8,128)S(1)}, f32[2,8,128]{2,1,0:T(8,128)S(1)}, u32[]{:S(2)}, u32[]{:S(2)}) collective-permute-start(f32[2,8,128]{2,1,0:T(8,128)S(1)} %get-tuple-element.38), channel_id=1, source_target_pairs={{0,1},{1,0},{2,3},{3,2},{4,5},{5,4},{6,7},{7,6},{8,9},{9,8},{10,11... | collective-permute-start | bytes 24584 | tf_op jit(solution)/shard_map/ppermute | solution.py:348

commit v2 on v1

--- a/solution.py
+++ b/solution.py
@@ -103,7 +103,7 @@
     place = place + lax.broadcasted_iota(jnp.int32, (GROUP, LANES), 1)
     slot_here = jnp.where(place >= total, place - total, place) - orbit * slots
     target_row = jnp.zeros((GROUP, LANES), jnp.int32)
-    count = count_ref[0]
+    count = count_ref[0, 0]
     for slot in range(slots):
         live_target = jnp.where(slot < count, map_ref[slot] + 1, 0)
         target_row = jnp.where(slot_here == slot, live_target, target_row)
@@ -114,7 +114,9 @@
     for group in range(slots // GROUP):
         target = jnp.zeros(row.shape, jnp.int32)
         for slot in range(GROUP):
-            target = jnp.where(row == slot, map_ref[group * GROUP + slot], target)
+            index = group * GROUP + slot
+            live_target = jnp.where(index < count, map_ref[index], -1)
+            target = jnp.where(row == slot, live_target, target)
         part = pl.ds(group * GROUP, GROUP)
         pick_ref[part, :] = jnp.where(cell == target, 1.0, 0.0).astype(BF16)
     for group in range(slots // GROUP):
@@ -160,10 +162,19 @@
 
 
 def start_kernel(
-    orbits, parity, shifted_ref, *refs
+    orbits, parity, shifted_ref, pick_ref, blocks_ref, *refs
 ):
     message_refs = refs[:orbits]
-    field_ref, right_ref, precond_ref, scatter_ref, even_ref, odd_ref, order_ref = refs[orbits:]
+    (
+        field_ref,
+        right_ref,
+        precond_ref,
+        scatter_ref,
+        even_ref,
+        odd_ref,
+        out_ref,
+        order_ref,
+    ) = refs[orbits:]
     slots = (message_refs[0].shape[0] - GROUP) // 2
     cells = scatter_ref.shape[0]
     targets = message_refs[0][pl.ds(2 * slots, GROUP), :]
@@ -190,6 +201,7 @@
     top = jnp.concatenate([field[:2], shifted[:1]], axis=0)
     bottom = jnp.concatenate([field[columns - 2 :], shifted[columns - 1 :]], axis=0)
     store_edges(parity, top, bottom, even_ref, odd_ref)
+    normal_slots(pick_ref, field, blocks_ref, out_ref)
 
 
 def scattered(one_hot, slots):
@@ -216,13 +228,15 @@
     return jnp.where(flip, even, odd), jnp.where(flip, odd, even)
 
 
-def normal_kernel(pick_ref, field_ref, blocks_ref, edge_ref, out_ref, edge_out_ref):
-    edge_out_ref[...] = edge_ref[...]
-    width = field_ref.shape[1]
-    picked = dot(pick_ref[...], jnp.concatenate(two_terms(field_ref[...]), axis=1))
+def normal_slots(pick_ref, field, blocks_ref, out_ref):
+    width = field.shape[-1]
+    field = field.reshape(pick_ref.shape[1], width)
+    picked = dot(pick_ref[...], jnp.concatenate(two_terms(field), axis=1))
     picked = picked[:, :width] + picked[:, width:]
+    energy = jnp.zeros((GROUP, width), F32)
     for group in range(picked.shape[0] // GROUP):
-        rows = stacked_terms(picked[group * GROUP : (group + 1) * GROUP])
+        cells = picked[group * GROUP : (group + 1) * GROUP]
+        rows = stacked_terms(cells)
         rows = jnp.concatenate([rows, rows], axis=1)
         total = jnp.zeros((GROUP, width), F32)
         for slot in range(0, GROUP, 2):
@@ -230,6 +244,8 @@
             total = pick_row(total, product[:, :width], slot)
             total = pick_row(total, product[:, width:], slot + 1)
         out_ref[pl.ds(group * GROUP, GROUP), :] = total
+        energy = energy + cells * total
+    return energy
 
 
 def extended(field, top, bottom):
@@ -243,55 +259,138 @@
     return PRIOR_WEIGHT * stencil(first, shifted)
 
 
-def system(parity, orbits, refs):
-    (field_ref, shifted_ref, even_ref, odd_ref, rim_even_ref, rim_odd_ref, scatter_ref) = refs[:7]
-    slot_refs = refs[7 : 7 + orbits]
-    order_ref = refs[-1]
+def scattered_slots(orbits, scatter_ref, slot_refs, order_ref):
     slots = slot_refs[0].shape[0]
     gather_messages(orbits, slots, [ref[...] for ref in slot_refs], order_ref)
-    normal = scattered(scatter_ref[...], order_ref[...]).reshape(field_ref.shape)
+    return scattered(scatter_ref[...], order_ref[...])
+
+
+def first_kernel(
+    parity,
+    orbits,
+    field_ref,
+    shifted_ref,
+    even_ref,
+    odd_ref,
+    scatter_ref,
+    precond_ref,
+    *refs,
+):
+    slot_refs = refs[:orbits]
+    image_ref, next_ref, edge_ref, order_ref = refs[orbits:]
+    normal = scattered_slots(orbits, scatter_ref, slot_refs, order_ref)
     top, bottom = load_edges(parity, even_ref, odd_ref)
-    rim_top, rim_bottom = load_edges(parity, rim_even_ref, rim_odd_ref)
     prior = prior_parts(
-        field_ref[...], shifted_ref[...], top[:2], bottom[:2], rim_top[2:], rim_bottom[2:]
-    )
-    return prior + normal, refs[7 + orbits : -1]
-
-
-def first_kernel(parity, orbits, *refs):
-    image, rest = system(parity, orbits, refs)
-    precond_ref, image_ref, next_ref, even_ref, odd_ref = rest
+        field_ref[...], shifted_ref[...], top[:2], bottom[:2], top[2:], bottom[2:]
+    )
+    image = prior + normal.reshape(field_ref.shape)
     following = image / precond_ref[...]
     image_ref[...] = image
     next_ref[...] = following
-    store_edges(parity, following[:2], following[following.shape[0] - 2 :], even_ref, odd_ref)
-
-
-def second_kernel(parity, orbits, *refs):
-    image, rest = system(parity, orbits, refs)
-    start_ref, right_ref, first_ref, image_ref, sums_ref = rest
-    field = refs[0][...]
+    edge_ref[...] = jnp.where(parity(), following[:2], following[following.shape[0] - 2 :])
+
+
+def alone(field, shifted):
+    zero = jnp.zeros((1,) + field.shape[1:], F32)
+    return stencil(extended(field, zero, zero), shifted)
+
+
+def inner_kernel(
+    field_ref,
+    shifted_ref,
+    start_ref,
+    right_ref,
+    first_ref,
+    pick_ref,
+    blocks_ref,
+    base_ref,
+    ends_ref,
+    parts_ref,
+    out_ref,
+):
+    field, shifted = field_ref[...], shifted_ref[...]
+    energy = normal_slots(pick_ref, field, blocks_ref, out_ref)
     start, first = start_ref[...], first_ref[...]
+    once = alone(field, shifted)
+    base_ref[...] = PRIOR_WEIGHT * alone(once, shifted)
+    ends_ref[0] = once[0]
+    ends_ref[1] = once[once.shape[0] - 1]
     own = jnp.where(lax.axis_index("orbit") == 0, 1.0, 0.0)
-    lane = lax.broadcasted_iota(jnp.int32, (1, LANES), 1)
-    line = jnp.zeros((1, LANES), F32)
-    pairs = ((right_ref[...], start), (start, first), (first, field), (field, image))
-    for index, (left, right) in enumerate(pairs):
-        by_lane = jnp.sum(jnp.sum(left * right, axis=0), axis=0, keepdims=True)
-        value = jnp.sum(by_lane, axis=1, keepdims=True) * own
-        line = jnp.where(lane == index, value, line)
-    sums_ref[...] = jnp.broadcast_to(line[None], sums_ref.shape)
-    image_ref[...] = image
+    parts_ref[0] = own * jnp.sum(right_ref[...] * start, axis=0)
+    parts_ref[1] = own * jnp.sum(start * first, axis=0)
+    parts_ref[2] = own * jnp.sum(first * field, axis=0)
+    parts_ref[3] = own * PRIOR_WEIGHT * jnp.sum(once * once, axis=0) + energy
+
+
+def sides(parity, top, bottom):
+    flip = parity()
+    return jnp.where(flip, top, bottom), jnp.where(flip, bottom, top)
+
+
+def near_far(parity, even_ref):
+    flip = parity()
+    return jnp.where(flip, even_ref[1], even_ref[0]), jnp.where(flip, even_ref[0], even_ref[1])
+
+
+def edge_kernel(parity, field_ref, even_ref, ends_ref, parts_ref, message_ref):
+    columns = field_ref.shape[0]
+    near, _ = near_far(parity, even_ref)
+    even_end, odd_end = sides(parity, ends_ref[0], ends_ref[1])
+    _, odd_field = sides(parity, field_ref[0], field_ref[columns - 1])
+    orbit = lax.axis_index("orbit")
+    own = jnp.where(orbit == 0, PRIOR_WEIGHT, 0.0)
+    more = own * (near * (near - 2.0 * even_end) + odd_field * odd_field)
+    sums = [jnp.sum(parts_ref[index], axis=0, keepdims=True) for index in range(3)]
+    sums.append(jnp.sum(parts_ref[3] + more, axis=0, keepdims=True))
+    sums = jnp.sum(jnp.concatenate(sums, axis=0), axis=1, keepdims=True)
+    lane = lax.broadcasted_iota(jnp.int32, (4, LANES), 1)
+    index = lax.broadcasted_iota(jnp.int32, (4, LANES), 0)
+    line = jnp.sum(jnp.where(lane == index, sums, 0.0), axis=0, keepdims=True)
+    row = jnp.concatenate([jnp.where(orbit == 0, odd_end, odd_field), line], axis=0)
+    several = jnp.concatenate([row] * GROUP, axis=0)
+    for index in range(message_ref.shape[0] // several.shape[0]):
+        message_ref[pl.ds(index * several.shape[0], several.shape[0]), :] = several
 
 
 def last_kernel(
-    sums_ref, start_ref, next_ref, right_ref, first_ref, second_ref, out_ref, residual_ref
+    parity,
+    orbits,
+    bands,
+    received_ref,
+    start_ref,
+    next_ref,
+    right_ref,
+    first_ref,
+    base_ref,
+    shifted_ref,
+    even_ref,
+    rim_ref,
+    scatter_ref,
+    *refs,
 ):
-    line = jnp.sum(sums_ref[...], axis=0)
+    slot_refs = refs[:orbits]
+    out_ref, residual_ref, order_ref, second_ref = refs[orbits:]
+    columns, pieces, _ = start_ref.shape
+    rows = pieces + 1
+
+    def end_of(band):
+        return received_ref[pl.ds(band * rows, pieces), :]
+
+    def field_of(band):
+        return received_ref[pl.ds((bands + band) * rows, pieces), :]
+
+    open_sides = jnp.zeros((pieces, LANES), F32)
+    for band in range(1, bands, 2):
+        above = (band + 1) % bands
+        open_sides = open_sides + end_of(band) * field_of(above) + end_of(above) * field_of(band)
+    open_sides = jnp.sum(jnp.sum(open_sides, axis=0, keepdims=True), axis=1, keepdims=True)
+    lines = received_ref[pl.ds(pieces, orbits * bands, stride=rows), :]
+    line = jnp.sum(lines, axis=0, keepdims=True)
     lane = lax.broadcasted_iota(jnp.int32, line.shape, 1)
     product, energy, cross, following = (
         jnp.sum(jnp.where(lane == index, line, 0.0), axis=1, keepdims=True) for index in range(4)
     )
+    following = following - (2.0 * PRIOR_WEIGHT) * open_sides
     alpha = product / energy
     later = product - 2.0 * alpha * energy + alpha * alpha * cross
     grown = 1.0 + later / product
@@ -301,6 +400,31 @@
     later_alpha = later / later_energy
     on_start = alpha + later_alpha * grown
     on_next = -alpha * later_alpha
+
+    normal = scattered_slots(orbits, scatter_ref, slot_refs, order_ref)
+    second_ref[...] = base_ref[...] + normal.reshape(second_ref.shape)
+    flip = parity()
+    band = lax.axis_index("lon")
+    across = lax.rem(band + jnp.where(flip, 1, bands - 1), bands)
+    even_field, odd_field = sides(parity, next_ref[0], next_ref[columns - 1])
+    near, far = near_far(parity, even_ref)
+    even_first = rim_ref[2] * near - far - even_field - lat_pair(near[None])[0]
+    odd_near = field_of(across)
+    odd_first = end_of(across) - odd_field
+    ends = (
+        (0, 1, jnp.where(flip, near, odd_near), jnp.where(flip, even_first, odd_first)),
+        (
+            columns - 1,
+            columns - 2,
+            jnp.where(flip, odd_near, near),
+            jnp.where(flip, odd_first, even_first),
+        ),
+    )
+    for end, inner, field, first in ends:
+        change = lat_pair(field[None])[0] - shifted_ref[end] * field - first
+        second_ref[end] = second_ref[end] + PRIOR_WEIGHT * change
+        second_ref[inner] = second_ref[inner] + PRIOR_WEIGHT * field
+
     out = on_start * start_ref[...] + on_next * next_ref[...]
     residual = right_ref[...] - on_start * first_ref[...] - on_next * second_ref[...]
     out_ref[...] = out.reshape(out_ref.shape)
@@ -313,10 +437,9 @@
     pieces = latitudes // width
     cells = columns * pieces
     field_shape = (columns, pieces, width)
-    paired = bands % 2 == 0
 
     def parity():
-        return lax.rem(lax.axis_index("lon"), 2) == 1 if paired else False
+        return lax.rem(lax.axis_index("lon"), 2) == 1
 
     vmem = pl.BlockSpec(memory_space=pltpu.VMEM)
     anywhere = pl.BlockSpec(memory_space=pl.ANY)
@@ -341,14 +464,8 @@
             for step in range(1, orbits)
         ]
 
-    def from_neighbours(even, odd):
-        if paired:
-            even_pairs = [(i, i ^ 1) for i in range(bands)]
-            odd_pairs = [(i, (i + 1 if i % 2 else i - 1) % bands) for i in range(bands)]
-            return lax.ppermute(even, "lon", even_pairs), lax.ppermute(odd, "lon", odd_pairs)
-        up = [(i, (i + 1) % bands) for i in range(bands)]
-        down = [((i + 1) % bands, i) for i in range(bands)]
-        return lax.ppermute(odd, "lon", down), lax.ppermute(even, "lon", up)
+    even_pairs = [(i, i ^ 1) for i in range(bands)]
+    odd_pairs = [(i, (i + 1 if i % 2 else i - 1) % bands) for i in range(bands)]
 
     matrices_in = interp.reshape(slots, observations, width)
     line = (slots, 1, observations)
@@ -362,7 +479,7 @@
         ),
         [anywhere] * 5,
         [
-            pltpu.SMEM((1,), jnp.int32),
+            pltpu.SMEM((1, 1), jnp.int32),
             pltpu.SMEM((slots,), jnp.int32),
             pltpu.VMEM(line, F32),
             pltpu.VMEM(line, F32),
@@ -370,7 +487,7 @@
         ],
         "data_terms",
         DATA_VMEM_BYTES,
-    )(live_count.reshape(1), block_map.reshape(slots), matrices_in, obs_value, obs_weight)
+    )(live_count, block_map.reshape(slots), matrices_in, obs_value, obs_weight)
     messages = from_others(message)
     shifted, blocks = call(
         block_kernel,
@@ -387,50 +504,49 @@
     edge = ((2, pieces, width), F32)
     wide_edge = ((max(slots // pieces + 1, rim[0][0]), pieces, width), F32)
     field = (field_shape, F32)
-    start, right_side, precond, scatter, even, odd = call(
+    slot_terms = ((slots, width), F32)
+    start, right_side, precond, scatter, even, odd, terms = call(
         functools.partial(start_kernel, orbits, parity),
-        (field, field, field, ((cells, edge_width), BF16), rim, wide_edge),
-        [vmem] * (1 + orbits),
+        (field, field, field, ((cells, edge_width), BF16), rim, wide_edge, slot_terms),
+        [vmem] * (3 + orbits),
         [order],
         "start",
-    )(shifted, *messages)
-
-    def exchanged(value, even, odd, name):
-        terms, odd = call(
-            normal_kernel,
-            (((slots, width), F32), (odd.shape, F32)),
-            [vmem] * 4,
-            (),
-            name,
-            work=WORK,
-        )(pick, value.reshape(cells, width), blocks, odd)
-        return from_others(terms), from_neighbours(even, odd)
-
-    terms, (rim_even, rim_odd) = exchanged(start, even, odd, "normal_start")
-    first, following, even, odd = call(
+    )(shifted, pick, blocks, *messages)
+    rim_odd = lax.ppermute(odd, "lon", odd_pairs)
+    terms = from_others(terms)
+    rim_even = lax.ppermute(even, "lon", even_pairs)
+    first, following, even = call(
         functools.partial(first_kernel, parity, orbits),
-        (field, field, edge, wide_edge),
-        [vmem] * (8 + orbits),
+        (field, field, edge),
+        [vmem] * (6 + orbits),
         [order],
         "first_image",
-    )(start, shifted, rim_even, rim_odd, rim_even, rim_odd, scatter, *terms, precond)
-
-    terms, (even, odd) = exchanged(following, even, odd, "normal_next")
-    second, sums = call(
-        functools.partial(second_kernel, parity, orbits),
-        (field, ((orbits * bands, 1, width), F32)),
+    )(start, shifted, rim_even, rim_odd, scatter, precond, *terms)
+
+    even = lax.ppermute(even, "lon", even_pairs)
+    base, ends, parts, terms = call(
+        inner_kernel,
+        (field, edge, ((4, pieces, width), F32), slot_terms),
+        [vmem] * 7,
+        (),
+        "inner_image",
+        work=WORK,
+    )(following, shifted, start, right_side, first, pick, blocks)
+    terms = from_others(terms)
+    message = ((orbits * bands * (pieces + 1), width), F32)
+    (sums,) = call(
+        functools.partial(edge_kernel, parity), (message,), [vmem] * 4, (), "edge_sums"
+    )(following, even, ends, parts)
+    sums = lax.all_to_all(sums[:, None], ("orbit", "lon"), 0, 0, tiled=True)[:, 0]
+    return call(
+        functools.partial(last_kernel, parity, orbits, bands),
+        ((kappa2.shape, F32), (kappa2.shape, F32)),
         [vmem] * (10 + orbits),
-        [order],
-        "second_image",
-    )(following, shifted, even, odd, rim_even, rim_odd, scatter, *terms, start, right_side, first)
-    sums = lax.all_to_all(sums, ("orbit", "lon"), 0, 0, tiled=True)
-    return call(
-        last_kernel,
-        ((kappa2.shape, F32), (kappa2.shape, F32)),
-        [vmem] * 6,
-        (),
+        [order, pltpu.VMEM(field_shape, F32)],
         "combine",
-    )(sums, start, following, right_side, first, second)
+    )(
+        sums, start, following, right_side, first, base, shifted, even, rim_even, scatter, *terms
+    )
 
 
 def solution(mesh):

time: 35.7 us -> 32.1 us (0.90)
  blocking collectives: 10.4 us -> 0 us
  waiting for transfers between devices: 4.89 us -> 9.8 us
  starting transfers between devices: 11.6 us -> 13.3 us
    all_to_all x1 -> x0, blocking collectives: 10.4 us -> none  [per_device(): sums = lax.all_to_all(sums, ('orbit', 'lon'), 0, 0, tiled=True)]
    all_to_all x0 -> x1, waiting for transfers between devices: none -> 4.62 us  [per_device(): lax.all_to_all(sums[:, None], ('orbit', 'lon'), 0, 0, tiled=True)[:, 0]]
    all_to_all x0 -> x1, starting transfers between devices: none -> 3.51 us  [per_device(): lax.all_to_all(sums[:, None], ('orbit', 'lon'), 0, 0, tiled=True)[:, 0]]
    ppermute x4 -> x3, starting transfers between devices: 5.63 us -> 3.49 us  [the longest x1 3.42 us: per_device(): rim_odd = lax.ppermute(odd, 'lon', odd_pairs)]
    ppermute x3, waiting for transfers between devices: 2.54 us -> 3.5 us  [from_others(): lax.ppermute(value, 'orbit', [((i + step) % orbits, i) for i in range(orb...]
    ppermute x4 -> x3, waiting for transfers between devices: 2.35 us -> 1.68 us  [the longest x1 1.18 us: per_device(): rim_even = lax.ppermute(even, 'lon', even_pairs)]
    pallas_call x1, Pallas kernels: 0.26 us -> 0.76 us  [per_device(): call(functools.partial(start_kernel, orbits, parity), (field, field, fiel...]
    pallas_call x4 -> x3, Pallas kernels: 2.71 us -> 2.48 us  [the longest x1 1.05 us: per_device(): call(functools.partial(last_kernel, parity, orbits, bands), ((kappa2.shap...]
  transfers between devices with their start and end apart: 7 -> 7, of which waited for: 5 -> 6; matrix products, arithmetic and copies ran while one was open for 0% -> 0% of each run, Pallas kernels for 4% -> 7%
where the time goes in v2:
time: 32.1 us; the launch traced here: 31.9 us
  starting transfers between devices  13.3 us (41%)
  waiting for transfers between devices  9.8 us (31%)
  Pallas kernels  7.4 us (23%)
  between operations  1.37 us (4%)
    ppermute x3, starting transfers between devices, from_others(): lax.ppermute(value, 'orbit', [((i + step) % orbits, i) for i in range(orb...  6.33 us
    all_to_all x1, waiting for transfers between devices, per_device(): lax.all_to_all(sums[:, None], ('orbit', 'lon'), 0, 0, tiled=True)[:, 0]  4.62 us
    all_to_all x1, starting transfers between devices, per_device(): lax.all_to_all(sums[:, None], ('orbit', 'lon'), 0, 0, tiled=True)[:, 0]  3.51 us
    ppermute x3, waiting for transfers between devices, from_others(): lax.ppermute(value, 'orbit', [((i + step) % orbits, i) for i in range(orb...  3.5 us
    ppermute x1, starting transfers between devices, per_device(): rim_odd = lax.ppermute(odd, 'lon', odd_pairs)  3.42 us
    pallas_call x1, Pallas kernels, per_device(): call(functools.partial(data_kernel, orbits), (((2 * slots + GROUP, width)...  2.32 us
    pallas_call x1, Pallas kernels, per_device(): call(block_kernel, ((field_shape, F32), ((slots // 2, 2 * width, 2 * widt...  1.47 us
    ppermute x1, waiting for transfers between devices, per_device(): rim_even = lax.ppermute(even, 'lon', even_pairs)  1.18 us
  transfers between devices with their start and end apart: 7, of which 6 were waited for; matrix products, arithmetic and copies ran while one was open for 0% of the time, Pallas kernels for 7%

profile of v2, /device:TPU:0, one launch (start us, length us, event | category | flops | bytes accessed | tf_op | source)
XLA Modules:
  0.0 31.9 jit_solution(1176513625185491284)
XLA Ops:
  0.6 0.0 copy-start
  1.3 2.3 %data_terms.1 = (f32[72,128]{1,0:T(8,128)S(1)}, bf16[32,256,128]{2,1,0:T(8,128)(2,1)S(1)}, f32[32,256]{1,0:T(8,128)S(1)}, bf16[32,512]{1,0:T(8,128)(2,1)S(1)}) custom-call(s32[1,1]{1,0:T(1,128)S(6)} %copy.9.count_in, s32[32]{0:T(128)} %bitcast.8, bf16[32,256,128]{2,1,0:T(8,128)(2,1)} %bitcast.7, f32[32,1,256]{2,1,0:T(1,128)} %value_in.1, f32[32,1,256]{2,1,0:T(1,128)} %weight_in.1), custom_call_target="tpu_custom_call" | custom-call | tf_op jit(solution)/shard_map/data_terms/pallas_call | solution.py:472
  3.7 3.0 %collective-permute-start = (f32[72,128]{1,0:T(8,128)S(1)}, f32[72,128]{1,0:T(8,128)S(1)}, u32[]{:S(2)}, u32[]{:S(2)}) collective-permute-start(f32[72,128]{1,0:T(8,128)S(1)} %get-tuple-element.27.refs_0_), channel_id=1, source_target_pairs={{16,0},{0,16},{17,1},{1,17},{18,2},{2,18},{19,3},{3,19},{20,4},{4,... | collective-permute-start | bytes 110600 | tf_op jit(solution)/shard_map/ppermute | solution.py:463
  6.7 0.0 copy-done
  6.7 1.5 %blocks.1 = (f32[64,8,128]{2,1,0:T(8,128)S(1)}, bf16[16,256,256]{2,1,0:T(8,128)(2,1)S(1)}) custom-call(f32[64,1024]{1,0:T(8,128)S(1)} %copy-done, bf16[32,256,128]{2,1,0:T(8,128)(2,1)S(1)} %get-tuple-element.22.matrices_ref, f32[32,256]{1,0:T(8,128)S(1)} %get-tuple-element.23.weight_ref), custom_call_target="tpu_custom_call" | custom-call | flops 4294967296 | tf_op jit(solution)/shard_map/blocks/pallas_call | solution.py:492
  8.1 0.5 %collective-permute-done.refs_1_ = f32[72,128]{1,0:T(8,128)S(1)} collective-permute-done((f32[72,128]{1,0:T(8,128)S(1)}, f32[72,128]{1,0:T(8,128)S(1)}, u32[]{:S(2)}, u32[]{:S(2)}) %collective-permute-start) | collective-permute-done | bytes 36896 | tf_op jit(solution)/shard_map/ppermute | solution.py:463
  8.6 0.8 %start.1 = (f32[64,8,128]{2,1,0:T(8,128)S(1)}, f32[64,8,128]{2,1,0:T(8,128)S(1)}, f32[64,8,128]{2,1,0:T(8,128)S(1)}, bf16[512,128]{1,0:T(8,128)(2,1)S(1)}, f32[3...) custom-call(f32[64,8,128]{2,1,0:T(8,128)S(1)} %get-tuple-element.24.shifted_ref, ...), custom_call_target="tpu_custom_call" | custom-call | tf_op jit(solution)/shard_map/start/pallas_call | solution.py:508
  9.4 3.4 %collective-permute-start.2 = (f32[5,8,128]{2,1,0:T(8,128)S(1)}, f32[5,8,128]{2,1,0:T(8,128)S(1)}, u32[]{:S(2)}, u32[]{:S(2)}) collective-permute-start(f32[5,8,128]{2,1,0:T(8,128)S(1)} %get-tuple-element.30), channel_id=1, source_target_pairs={{0,15},{1,2},{2,1},{3,4},{4,3},{5,6},{6,5},{7,8},{8,7},{9,10},{10,... | collective-permute-start | bytes 61448 | tf_op jit(solution)/shard_map/ppermute | solution.py:515
  12.8 1.5 %collective-permute-start.3 = (f32[32,128]{1,0:T(8,128)S(1)}, f32[32,128]{1,0:T(8,128)S(1)}, u32[]{:S(2)}, u32[]{:S(2)}) collective-permute-start(f32[32,128]{1,0:T(8,128)S(1)} %get-tuple-element.33.refs_0_), channel_id=1, source_target_pairs={{16,0},{0,16},{17,1},{1,17},{18,2},{2,18},{19,3},{3,19},{20,4},{4,... | collective-permute-start | bytes 49160 | tf_op jit(solution)/shard_map/ppermute | solution.py:463
  14.3 0.0 collective-permute-start.1
  14.3 1.2 %collective-permute-done.1.even_ref.rim_ref = f32[3,8,128]{2,1,0:T(8,128)S(1)} collective-permute-done((f32[3,8,128]{2,1,0:T(8,128)S(1)}, f32[3,8,128]{2,1,0:T(8,128)S(1)}, u32[]{:S(2)}, u32[]{:S(2)}) %collective-permute-start.1) | collective-permute-done | bytes 12320 | tf_op jit(solution)/shard_map/ppermute | solution.py:517
  15.4 1.1 %collective-permute-done.3.refs_1_ = f32[32,128]{1,0:T(8,128)S(1)} collective-permute-done((f32[32,128]{1,0:T(8,128)S(1)}, f32[32,128]{1,0:T(8,128)S(1)}, u32[]{:S(2)}, u32[]{:S(2)}) %collective-permute-start.3) | collective-permute-done | bytes 16416 | tf_op jit(solution)/shard_map/ppermute | solution.py:463
  16.5 0.0 collective-permute-done.2.odd_ref
  16.5 0.4 %first_image.1 = (f32[64,8,128]{2,1,0:T(8,128)S(1)}, f32[64,8,128]{2,1,0:T(8,128)S(1)}, f32[2,8,128]{2,1,0:T(8,128)S(1)}) custom-call(f32[64,8,128]{2,1,0:T(8,128)S(1)} %get-tuple-element.28.field_ref.start_ref, f32[64,8,128]{2,1,0:T(8,128)S(1)} %get-tuple-element.24.shifted_ref, f32[3,8,128]{2,1,0:T(8,128)S(1)} %collective-permute-done.1.even_ref.rim_ref, ...), custom_call_target="tpu_custom_call" | custom-call | tf_op jit(solution)/shard_map/first_image/pallas_call | solution.py:518
  16.9 0.1 collective-permute-start.4
  17.0 0.7 %inner_image.1 = (f32[64,8,128]{2,1,0:T(8,128)S(1)}, f32[2,8,128]{2,1,0:T(8,128)S(1)}, f32[4,8,128]{2,1,0:T(8,128)S(1)}, f32[32,128]{1,0:T(8,128)S(1)}) custom-call(f32[64,8,128]{2,1,0:T(8,128)S(1)} %get-tuple-element.34.field_ref.next_ref, f32[64,8,128]{2,1,0:T(8,128)S(1)} %get-tuple-element.24.shifted_ref, ...), custom_call_target="tpu_custom_call" | custom-call | flops 4294967296 | tf_op jit(solution)/shard_map/inner_image/pallas_call | solution.py:527
  17.6 0.5 %collective-permute-done.4.even_ref = f32[2,8,128]{2,1,0:T(8,128)S(1)} collective-permute-done((f32[2,8,128]{2,1,0:T(8,128)S(1)}, f32[2,8,128]{2,1,0:T(8,128)S(1)}, u32[]{:S(2)}, u32[]{:S(2)}) %collective-permute-start.4) | collective-permute-done | bytes 8224 | tf_op jit(solution)/shard_map/ppermute | solution.py:526
  18.1 0.8 %edge_sums.1 = f32[288,128]{1,0:T(8,128)} custom-call(f32[64,8,128]{2,1,0:T(8,128)S(1)} %get-tuple-element.34.field_ref.next_ref, f32[2,8,128]{2,1,0:T(8,128)S(1)} %collective-permute-done.4.even_ref, f32[2,8,128]{2,1,0:T(8,128)S(1)} %get-tuple-element.38.ends_ref, f32[4,8,128]{2,1,0:T(8,128)S(1)} %get-tuple-element.39.parts_ref), custom_call_target="tpu_custom_call" | custom-call | tf_op jit(solution)/shard_map/edge_sums/pallas_call | solution.py:537
  18.9 3.5 %all-to-all-start = ((f32[288,1,128]{2,1,0:T(1,128)}), f32[288,1,128]{2,1,0:T(1,128)S(1)}, u32[]{:S(2)}, u32[]{:S(2)}) async-start(f32[288,1,128]{2,1,0:T(1,128)} %bitcast.3), calls=%async_computation | async-start | bytes 294912 | tf_op jit(solution)/shard_map/all_to_all | solution.py:540
  22.4 1.8 %collective-permute-start.5 = (f32[32,128]{1,0:T(8,128)S(1)}, f32[32,128]{1,0:T(8,128)S(1)}, u32[]{:S(2)}, u32[]{:S(2)}) collective-permute-start(f32[32,128]{1,0:T(8,128)S(1)} %get-tuple-element.41.refs_0_), channel_id=1, source_target_pairs={{16,0},{0,16},{17,1},{1,17},{18,2},{2,18},{19,3},{3,19},{20,4},{4,... | collective-permute-start | bytes 49160 | tf_op jit(solution)/shard_map/ppermute | solution.py:463
  24.3 2.0 %collective-permute-done.5.refs_1_ = f32[32,128]{1,0:T(8,128)S(1)} collective-permute-done((f32[32,128]{1,0:T(8,128)S(1)}, f32[32,128]{1,0:T(8,128)S(1)}, u32[]{:S(2)}, u32[]{:S(2)}) %collective-permute-start.5) | collective-permute-done | bytes 16416 | tf_op jit(solution)/shard_map/ppermute | solution.py:463
  26.2 4.6 %all-to-all-done = f32[288,1,128]{2,1,0:T(1,128)S(1)} async-done(((f32[288,1,128]{2,1,0:T(1,128)}), f32[288,1,128]{2,1,0:T(1,128)S(1)}, u32[]{:S(2)}, u32[]{:S(2)}) %all-to-all-start) | async-done | bytes 147488 | tf_op jit(solution)/shard_map/all_to_all | solution.py:540
  30.9 1.0 %combine.1 = (f32[64,1024]{1,0:T(8,128)}, f32[64,1024]{1,0:T(8,128)}) custom-call(f32[288,128]{1,0:T(8,128)S(1)} %bitcast.6, f32[64,8,128]{2,1,0:T(8,128)S(1)} %get-tuple-element.28.field_ref.start_ref, f32[64,8,128]{2,1,0:T(8,128)S(1)} %get-tuple-element.34.field_ref.next_ref, f32[64,8,128]{2,1,0:T(8,128)S(1)} %get-tuple-element.36.right_ref, ...), custom_call_target="tpu_custom_call" | custom-call | tf_op jit(solution)/shard_map/combine/pallas_call | solution.py:541
Async XLA Ops:
  0.6 6.0 %copy-start = (f32[64,1024]{1,0:T(8,128)S(1)}, f32[64,1024]{1,0:T(8,128)}, u32[]{:S(2)}) copy-start(f32[64,1024]{1,0:T(8,128)} %kappa_ref.1) | copy-start | bytes 786436
  3.7 4.9 %collective-permute-start = (f32[72,128]{1,0:T(8,128)S(1)}, f32[72,128]{1,0:T(8,128)S(1)}, u32[]{:S(2)}, u32[]{:S(2)}) collective-permute-start(f32[72,128]{1,0:T(8,128)S(1)} %get-tuple-element.27.refs_0_), channel_id=1, source_target_pairs={{16,0},{0,16},{17,1},{1,17},{18,2},{2,18},{19,3},{3,19},{20,4},{4,... | collective-permute-start | bytes 110600 | tf_op jit(solution)/shard_map/ppermute | solution.py:463
  9.4 7.2 %collective-permute-start.2 = (f32[5,8,128]{2,1,0:T(8,128)S(1)}, f32[5,8,128]{2,1,0:T(8,128)S(1)}, u32[]{:S(2)}, u32[]{:S(2)}) collective-permute-start(f32[5,8,128]{2,1,0:T(8,128)S(1)} %get-tuple-element.30), channel_id=1, source_target_pairs={{0,15},{1,2},{2,1},{3,4},{4,3},{5,6},{6,5},{7,8},{8,7},{9,10},{10,... | collective-permute-start | bytes 61448 | tf_op jit(solution)/shard_map/ppermute | solution.py:515
  12.8 3.7 %collective-permute-start.3 = (f32[32,128]{1,0:T(8,128)S(1)}, f32[32,128]{1,0:T(8,128)S(1)}, u32[]{:S(2)}, u32[]{:S(2)}) collective-permute-start(f32[32,128]{1,0:T(8,128)S(1)} %get-tuple-element.33.refs_0_), channel_id=1, source_target_pairs={{16,0},{0,16},{17,1},{1,17},{18,2},{2,18},{19,3},{3,19},{20,4},{4,... | collective-permute-start | bytes 49160 | tf_op jit(solution)/shard_map/ppermute | solution.py:463
  14.3 1.2 %collective-permute-start.1 = (f32[3,8,128]{2,1,0:T(8,128)S(1)}, f32[3,8,128]{2,1,0:T(8,128)S(1)}, u32[]{:S(2)}, u32[]{:S(2)}) collective-permute-start(f32[3,8,128]{2,1,0:T(8,128)S(1)} %get-tuple-element.29), channel_id=1, source_target_pairs={{0,1},{1,0},{2,3},{3,2},{4,5},{5,4},{6,7},{7,6},{8,9},{9,8},{10,11... | collective-permute-start | bytes 36872 | tf_op jit(solution)/shard_map/ppermute | solution.py:517
  16.9 1.2 %collective-permute-start.4 = (f32[2,8,128]{2,1,0:T(8,128)S(1)}, f32[2,8,128]{2,1,0:T(8,128)S(1)}, u32[]{:S(2)}, u32[]{:S(2)}) collective-permute-start(f32[2,8,128]{2,1,0:T(8,128)S(1)} %get-tuple-element.35), channel_id=1, source_target_pairs={{0,1},{1,0},{2,3},{3,2},{4,5},{5,4},{6,7},{7,6},{8,9},{9,8},{10,11... | collective-permute-start | bytes 24584 | tf_op jit(solution)/shard_map/ppermute | solution.py:526
  18.9 11.9 %all-to-all-start = ((f32[288,1,128]{2,1,0:T(1,128)}), f32[288,1,128]{2,1,0:T(1,128)S(1)}, u32[]{:S(2)}, u32[]{:S(2)}) async-start(f32[288,1,128]{2,1,0:T(1,128)} %bitcast.3), calls=%async_computation | async-start | bytes 294912 | tf_op jit(solution)/shard_map/all_to_all | solution.py:540
  22.4 3.8 %collective-permute-start.5 = (f32[32,128]{1,0:T(8,128)S(1)}, f32[32,128]{1,0:T(8,128)S(1)}, u32[]{:S(2)}, u32[]{:S(2)}) collective-permute-start(f32[32,128]{1,0:T(8,128)S(1)} %get-tuple-element.41.refs_0_), channel_id=1, source_target_pairs={{16,0},{0,16},{17,1},{1,17},{18,2},{2,18},{19,3},{3,19},{20,4},{4,... | collective-permute-start | bytes 49160 | tf_op jit(solution)/shard_map/ppermute | solution.py:463

commit v3 on v2

--- a/solution.py
+++ b/solution.py
@@ -14,7 +14,7 @@
 BF16 = jnp.bfloat16
 VMEM_BYTES = 48 * 1024 * 1024
 DATA_VMEM_BYTES = 59 * 1024 * 1024
-CHUNK = 16
+CHUNK = 8
 WORK = 1 << 32
 
 
@@ -64,7 +64,7 @@
 
 def data_kernel(
     orbits,
-    count_in,
+    count_ref,
     map_in,
     interp_in,
     value_in,
@@ -73,14 +73,13 @@
     matrices_ref,
     weight_ref,
     pick_ref,
-    count_ref,
     map_ref,
     value_rows,
     weight_rows,
     sems,
 ):
     slots = matrices_ref.shape[0]
-    pairs = ((weight_in, weight_rows), (value_in, value_rows), (map_in, map_ref), (count_in, count_ref))
+    pairs = ((weight_in, weight_rows), (value_in, value_rows), (map_in, map_ref))
     small = [
         pltpu.make_async_copy(source, target, sems.at[index])
         for index, (source, target) in enumerate(pairs)
@@ -93,8 +92,11 @@
                 interp_in.at[part], matrices_ref.at[part], sems.at[len(small) + index]
             )
         )
-    for copy in small + large:
+    count = count_ref[0, 0]
+    for copy in small:
         copy.start()
+    for index, copy in enumerate(large):
+        pl.when(index * CHUNK < count)(copy.start)
     for copy in small:
         copy.wait()
     orbit = lax.axis_index("orbit")
@@ -103,7 +105,6 @@
     place = place + lax.broadcasted_iota(jnp.int32, (GROUP, LANES), 1)
     slot_here = jnp.where(place >= total, place - total, place) - orbit * slots
     target_row = jnp.zeros((GROUP, LANES), jnp.int32)
-    count = count_ref[0, 0]
     for slot in range(slots):
         live_target = jnp.where(slot < count, map_ref[slot] + 1, 0)
         target_row = jnp.where(slot_here == slot, live_target, target_row)
@@ -119,26 +120,39 @@
             target = jnp.where(row == slot, live_target, target)
         part = pl.ds(group * GROUP, GROUP)
         pick_ref[part, :] = jnp.where(cell == target, 1.0, 0.0).astype(BF16)
-    for group in range(slots // GROUP):
-        part = pl.ds(group * GROUP, GROUP)
-        weights = weight_rows[part, 0, :]
-        weight_ref[part, :] = weights
-        scaled = (weights * value_rows[part, 0, :]).astype(BF16)
-        high, low = two_terms(weights)
-        rows = jnp.concatenate([scaled, high, low, low], axis=0)
-        first = jnp.zeros((GROUP, LANES), F32)
-        second = jnp.zeros((GROUP, LANES), F32)
-        for slot in range(GROUP):
-            index = group * GROUP + slot
-            if index % CHUNK == 0:
-                large[index // CHUNK].wait()
-            matrix = matrices_ref[index]
-            both = dot(rows, jnp.concatenate([matrix, matrix * matrix], axis=1))
-            squares = both[GROUP : 2 * GROUP, LANES:] + both[2 * GROUP : 3 * GROUP, LANES:]
-            first = pick_row(first, both[:GROUP, :LANES], slot)
-            second = pick_row(second, squares, slot)
-        message_ref[part, :] = first
-        message_ref[pl.ds(slots + group * GROUP, GROUP), :] = second
+    weight_ref[...] = weight_rows[:, 0, :]
+
+    def work(index):
+        large[index].wait()
+        for group in range(index * CHUNK // GROUP, (index + 1) * CHUNK // GROUP):
+            part = pl.ds(group * GROUP, GROUP)
+            weights = weight_rows[part, 0, :]
+            scaled = (weights * value_rows[part, 0, :]).astype(BF16)
+            high, low = two_terms(weights)
+            rows = jnp.concatenate([scaled, high, low, low], axis=0)
+            first = jnp.zeros((GROUP, LANES), F32)
+            second = jnp.zeros((GROUP, LANES), F32)
+            for slot in range(GROUP):
+                matrix = matrices_ref[group * GROUP + slot]
+                both = dot(rows, jnp.concatenate([matrix, matrix * matrix], axis=1))
+                squares = both[GROUP : 2 * GROUP, LANES:] + both[2 * GROUP : 3 * GROUP, LANES:]
+                first = pick_row(first, both[:GROUP, :LANES], slot)
+                second = pick_row(second, squares, slot)
+            message_ref[part, :] = first
+            message_ref[pl.ds(slots + group * GROUP, GROUP), :] = second
+
+    def rest(index):
+        part = pl.ds(index * CHUNK, CHUNK)
+        matrices_ref[part] = jnp.zeros((CHUNK,) + matrices_ref.shape[1:], BF16)
+        for start in (0, slots):
+            part = pl.ds(start + index * CHUNK, CHUNK)
+            message_ref[part, :] = jnp.zeros((CHUNK, LANES), F32)
+
+    chunks = range(slots // CHUNK)
+    for index in chunks:
+        pl.when(index * CHUNK >= count)(functools.partial(rest, index))
+    for index in chunks:
+        pl.when(index * CHUNK < count)(functools.partial(work, index))
 
 
 def block_kernel(kappa_ref, matrices_ref, weight_ref, shifted_ref, blocks_ref):
@@ -162,7 +176,7 @@
 
 
 def start_kernel(
-    orbits, parity, shifted_ref, pick_ref, blocks_ref, *refs
+    orbits, parity, shifted_ref, *refs
 ):
     message_refs = refs[:orbits]
     (
@@ -172,7 +186,6 @@
         scatter_ref,
         even_ref,
         odd_ref,
-        out_ref,
         order_ref,
     ) = refs[orbits:]
     slots = (message_refs[0].shape[0] - GROUP) // 2
@@ -201,7 +214,11 @@
     top = jnp.concatenate([field[:2], shifted[:1]], axis=0)
     bottom = jnp.concatenate([field[columns - 2 :], shifted[columns - 1 :]], axis=0)
     store_edges(parity, top, bottom, even_ref, odd_ref)
-    normal_slots(pick_ref, field, blocks_ref, out_ref)
+
+
+def normal_kernel(pick_ref, field_ref, blocks_ref, even_ref, out_ref, even_out_ref):
+    normal_slots(pick_ref, field_ref[...], blocks_ref, out_ref)
+    even_out_ref[...] = even_ref[...]
 
 
 def scattered(one_hot, slots):
@@ -442,10 +459,11 @@
         return lax.rem(lax.axis_index("lon"), 2) == 1
 
     vmem = pl.BlockSpec(memory_space=pltpu.VMEM)
+    smem = pl.BlockSpec(memory_space=pltpu.SMEM)
     anywhere = pl.BlockSpec(memory_space=pl.ANY)
 
     def call(kernel, outs, in_specs, scratch=(), name=None, limit=VMEM_BYTES, work=0):
-        held = pltpu.VMEM if name != "combine" else jax.ShapeDtypeStruct
+        held = pltpu.VMEM if name not in ("combine", "edge_sums") else jax.ShapeDtypeStruct
         cost = pl.CostEstimate(flops=work, bytes_accessed=0, transcendentals=0) if work else None
         return pl.pallas_call(
             kernel,
@@ -477,13 +495,12 @@
             ((slots, observations), F32),
             ((slots, cells), BF16),
         ),
-        [anywhere] * 5,
+        [smem] + [anywhere] * 4,
         [
-            pltpu.SMEM((1, 1), jnp.int32),
             pltpu.SMEM((slots,), jnp.int32),
             pltpu.VMEM(line, F32),
             pltpu.VMEM(line, F32),
-            pltpu.SemaphoreType.DMA((4 + slots // CHUNK,)),
+            pltpu.SemaphoreType.DMA((3 + slots // CHUNK,)),
         ],
         "data_terms",
         DATA_VMEM_BYTES,
@@ -505,14 +522,17 @@
     wide_edge = ((max(slots // pieces + 1, rim[0][0]), pieces, width), F32)
     field = (field_shape, F32)
     slot_terms = ((slots, width), F32)
-    start, right_side, precond, scatter, even, odd, terms = call(
+    start, right_side, precond, scatter, even, odd = call(
         functools.partial(start_kernel, orbits, parity),
-        (field, field, field, ((cells, edge_width), BF16), rim, wide_edge, slot_terms),
-        [vmem] * (3 + orbits),
+        (field, field, field, ((cells, edge_width), BF16), rim, wide_edge),
+        [vmem] * (1 + orbits),
         [order],
         "start",
-    )(shifted, pick, blocks, *messages)
+    )(shifted, *messages)
     rim_odd = lax.ppermute(odd, "lon", odd_pairs)
+    terms, even = call(normal_kernel, (slot_terms, rim), [vmem] * 4, (), "normal_start", work=WORK)(
+        pick, start, blocks, even
+    )
     terms = from_others(terms)
     rim_even = lax.ppermute(even, "lon", even_pairs)
     first, following, even = call(

time: 32.1 us -> 31.3 us (0.975)
  Pallas kernels: 7.4 us -> 6.96 us
    all_to_all x1, starting transfers between devices: 3.51 us -> 2.89 us  [per_device(): lax.all_to_all(sums[:, None], ('orbit', 'lon'), 0, 0, tiled=True)[:, 0]]
    pallas_call x0 -> x1, Pallas kernels: none -> 0.56 us  [per_device(): call(normal_kernel, (slot_terms, rim), [vmem] * 4, (), 'normal_start', wo...]
    pallas_call x1, Pallas kernels: 2.32 us -> 1.77 us  [per_device(): call(functools.partial(data_kernel, orbits), (((2 * slots + GROUP, width)...]
    pallas_call x1, Pallas kernels: 0.76 us -> 0.26 us  [per_device(): call(functools.partial(start_kernel, orbits, parity), (field, field, fiel...]
    ppermute x1, starting transfers between devices: 3.42 us -> 3.76 us  [per_device(): rim_odd = lax.ppermute(odd, 'lon', odd_pairs)]
  transfers between devices with their start and end apart: 7 -> 7, of which waited for: 6 -> 6; matrix products, arithmetic and copies ran while one was open for 0% -> 0% of each run, Pallas kernels for 7% -> 9%
where the time goes in v3:
time: 31.3 us; the launch traced here: 31.2 us
  starting transfers between devices  13.1 us (42%)
  waiting for transfers between devices  9.76 us (31%)
  Pallas kernels  6.96 us (22%)
  between operations  1.38 us (4%)
    ppermute x3, starting transfers between devices, from_others(): lax.ppermute(value, 'orbit', [((i + step) % orbits, i) for i in range(orb...  6.37 us
    all_to_all x1, waiting for transfers between devices, per_device(): lax.all_to_all(sums[:, None], ('orbit', 'lon'), 0, 0, tiled=True)[:, 0]  4.62 us
    ppermute x1, starting transfers between devices, per_device(): rim_odd = lax.ppermute(odd, 'lon', odd_pairs)  3.76 us
    ppermute x3, waiting for transfers between devices, from_others(): lax.ppermute(value, 'orbit', [((i + step) % orbits, i) for i in range(orb...  3.46 us
    all_to_all x1, starting transfers between devices, per_device(): lax.all_to_all(sums[:, None], ('orbit', 'lon'), 0, 0, tiled=True)[:, 0]  2.89 us
    pallas_call x1, Pallas kernels, per_device(): call(functools.partial(data_kernel, orbits), (((2 * slots + GROUP, width)...  1.77 us
    pallas_call x1, Pallas kernels, per_device(): call(block_kernel, ((field_shape, F32), ((slots // 2, 2 * width, 2 * widt...  1.51 us
    ppermute x1, waiting for transfers between devices, per_device(): rim_even = lax.ppermute(even, 'lon', even_pairs)  1.18 us
  transfers between devices with their start and end apart: 7, of which 6 were waited for; matrix products, arithmetic and copies ran while one was open for 0% of the time, Pallas kernels for 9%

profile of v3, /device:TPU:0, one launch (start us, length us, event | category | flops | bytes accessed | tf_op | source)
XLA Modules:
  0.0 31.2 jit_solution(17590338007277514401)
XLA Ops:
  0.6 0.0 copy-start
  1.3 1.8 %data_terms.1 = (f32[72,128]{1,0:T(8,128)S(1)}, bf16[32,256,128]{2,1,0:T(8,128)(2,1)S(1)}, f32[32,256]{1,0:T(8,128)S(1)}, bf16[32,512]{1,0:T(8,128)(2,1)S(1)}) custom-call(s32[1,1]{1,0:T(1,128)S(6)} %copy.9.count_ref, s32[32]{0:T(128)} %bitcast.8, bf16[32,256,128]{2,1,0:T(8,128)(2,1)} %bitcast.7, f32[32,1,256]{2,1,0:T(1,128)} %value_in.1, ...), custom_call_target="tpu_custom_call" | custom-call | tf_op jit(solution)/shard_map/data_terms/pallas_call | solution.py:490
  3.1 3.0 %collective-permute-start = (f32[72,128]{1,0:T(8,128)S(1)}, f32[72,128]{1,0:T(8,128)S(1)}, u32[]{:S(2)}, u32[]{:S(2)}) collective-permute-start(f32[72,128]{1,0:T(8,128)S(1)} %get-tuple-element.26.refs_0_), channel_id=1, source_target_pairs={{16,0},{0,16},{17,1},{1,17},{18,2},{2,18},{19,3},{3,19},{20,4},{4,... | collective-permute-start | bytes 110600 | tf_op jit(solution)/shard_map/ppermute | solution.py:481
  6.1 0.0 copy-done
  6.1 1.5 %blocks.1 = (f32[64,8,128]{2,1,0:T(8,128)S(1)}, bf16[16,256,256]{2,1,0:T(8,128)(2,1)S(1)}) custom-call(f32[64,1024]{1,0:T(8,128)S(1)} %copy-done, bf16[32,256,128]{2,1,0:T(8,128)(2,1)S(1)} %get-tuple-element.23.matrices_ref, f32[32,256]{1,0:T(8,128)S(1)} %get-tuple-element.24.weight_ref), custom_call_target="tpu_custom_call" | custom-call | flops 4294967296 | tf_op jit(solution)/shard_map/blocks/pallas_call | solution.py:509
  7.6 0.4 %collective-permute-done.refs_1_ = f32[72,128]{1,0:T(8,128)S(1)} collective-permute-done((f32[72,128]{1,0:T(8,128)S(1)}, f32[72,128]{1,0:T(8,128)S(1)}, u32[]{:S(2)}, u32[]{:S(2)}) %collective-permute-start) | collective-permute-done | bytes 36896 | tf_op jit(solution)/shard_map/ppermute | solution.py:481
  8.0 0.3 start.1
  8.3 3.8 %collective-permute-start.2 = (f32[5,8,128]{2,1,0:T(8,128)S(1)}, f32[5,8,128]{2,1,0:T(8,128)S(1)}, u32[]{:S(2)}, u32[]{:S(2)}) collective-permute-start(f32[5,8,128]{2,1,0:T(8,128)S(1)} %get-tuple-element.32), channel_id=1, source_target_pairs={{0,15},{1,2},{2,1},{3,4},{4,3},{5,6},{6,5},{7,8},{8,7},{9,10},{10,... | collective-permute-start | bytes 61448 | tf_op jit(solution)/shard_map/ppermute | solution.py:532
  12.1 0.6 %normal_start.1 = (f32[32,128]{1,0:T(8,128)S(1)}, f32[3,8,128]{2,1,0:T(8,128)S(1)}) custom-call(bf16[32,512]{1,0:T(8,128)(2,1)S(1)} %get-tuple-element.28.pick_ref, f32[64,8,128]{2,1,0:T(8,128)S(1)} %get-tuple-element.27.field_ref.start_ref, bf16[16,256,256]{2,1,0:T(8,128)(2,1)S(1)} %get-tuple-element.29.blocks_ref, f32[3,8,128]{2,1,0:T(8,128)S(1)} %get-tuple-element.30.even_ref), custom_call_target="tpu_custom_call" | custom-call | flops 4294967296 | tf_op jit(solution)/shard_map/normal_start/pallas_call | solution.py:533
  12.6 1.5 %collective-permute-start.3 = (f32[32,128]{1,0:T(8,128)S(1)}, f32[32,128]{1,0:T(8,128)S(1)}, u32[]{:S(2)}, u32[]{:S(2)}) collective-permute-start(f32[32,128]{1,0:T(8,128)S(1)} %get-tuple-element.35.refs_0_), channel_id=1, source_target_pairs={{16,0},{0,16},{17,1},{1,17},{18,2},{2,18},{19,3},{3,19},{20,4},{4,... | collective-permute-start | bytes 49160 | tf_op jit(solution)/shard_map/ppermute | solution.py:481
  14.2 0.0 collective-permute-start.1
  14.2 1.2 %collective-permute-done.1.even_ref.rim_ref = f32[3,8,128]{2,1,0:T(8,128)S(1)} collective-permute-done((f32[3,8,128]{2,1,0:T(8,128)S(1)}, f32[3,8,128]{2,1,0:T(8,128)S(1)}, u32[]{:S(2)}, u32[]{:S(2)}) %collective-permute-start.1) | collective-permute-done | bytes 12320 | tf_op jit(solution)/shard_map/ppermute | solution.py:537
  15.3 1.1 %collective-permute-done.3.refs_1_ = f32[32,128]{1,0:T(8,128)S(1)} collective-permute-done((f32[32,128]{1,0:T(8,128)S(1)}, f32[32,128]{1,0:T(8,128)S(1)}, u32[]{:S(2)}, u32[]{:S(2)}) %collective-permute-start.3) | collective-permute-done | bytes 16416 | tf_op jit(solution)/shard_map/ppermute | solution.py:481
  16.4 0.0 collective-permute-done.2.odd_ref
  16.4 0.4 %first_image.1 = (f32[64,8,128]{2,1,0:T(8,128)S(1)}, f32[64,8,128]{2,1,0:T(8,128)S(1)}, f32[2,8,128]{2,1,0:T(8,128)S(1)}) custom-call(f32[64,8,128]{2,1,0:T(8,128)S(1)} %get-tuple-element.27.field_ref.start_ref, f32[64,8,128]{2,1,0:T(8,128)S(1)} %get-tuple-element.25.shifted_ref, f32[3,8,128]{2,1,0:T(8,128)S(1)} %collective-permute-done.1.even_ref.rim_ref, ...), custom_call_target="tpu_custom_call" | custom-call | tf_op jit(solution)/shard_map/first_image/pallas_call | solution.py:538
  16.8 0.1 collective-permute-start.4
  16.9 0.7 %inner_image.1 = (f32[64,8,128]{2,1,0:T(8,128)S(1)}, f32[2,8,128]{2,1,0:T(8,128)S(1)}, f32[4,8,128]{2,1,0:T(8,128)S(1)}, f32[32,128]{1,0:T(8,128)S(1)}) custom-call(f32[64,8,128]{2,1,0:T(8,128)S(1)} %get-tuple-element.36.field_ref.next_ref, f32[64,8,128]{2,1,0:T(8,128)S(1)} %get-tuple-element.25.shifted_ref, ...), custom_call_target="tpu_custom_call" | custom-call | flops 4294967296 | tf_op jit(solution)/shard_map/inner_image/pallas_call | solution.py:547
  17.5 0.5 %collective-permute-done.4.even_ref = f32[2,8,128]{2,1,0:T(8,128)S(1)} collective-permute-done((f32[2,8,128]{2,1,0:T(8,128)S(1)}, f32[2,8,128]{2,1,0:T(8,128)S(1)}, u32[]{:S(2)}, u32[]{:S(2)}) %collective-permute-start.4) | collective-permute-done | bytes 8224 | tf_op jit(solution)/shard_map/ppermute | solution.py:546
  18.0 0.8 %edge_sums.1 = f32[288,128]{1,0:T(8,128)} custom-call(f32[64,8,128]{2,1,0:T(8,128)S(1)} %get-tuple-element.36.field_ref.next_ref, f32[2,8,128]{2,1,0:T(8,128)S(1)} %collective-permute-done.4.even_ref, f32[2,8,128]{2,1,0:T(8,128)S(1)} %get-tuple-element.40.ends_ref, f32[4,8,128]{2,1,0:T(8,128)S(1)} %get-tuple-element.41.parts_ref), custom_call_target="tpu_custom_call" | custom-call | tf_op jit(solution)/shard_map/edge_sums/pallas_call | solution.py:557
  18.8 2.9 %all-to-all-start = ((f32[288,1,128]{2,1,0:T(1,128)}), f32[288,1,128]{2,1,0:T(1,128)S(1)}, u32[]{:S(2)}, u32[]{:S(2)}) async-start(f32[288,1,128]{2,1,0:T(1,128)} %bitcast.3), calls=%async_computation | async-start | bytes 294912 | tf_op jit(solution)/shard_map/all_to_all | solution.py:560
  21.7 1.8 %collective-permute-start.5 = (f32[32,128]{1,0:T(8,128)S(1)}, f32[32,128]{1,0:T(8,128)S(1)}, u32[]{:S(2)}, u32[]{:S(2)}) collective-permute-start(f32[32,128]{1,0:T(8,128)S(1)} %get-tuple-element.43.refs_0_), channel_id=1, source_target_pairs={{16,0},{0,16},{17,1},{1,17},{18,2},{2,18},{19,3},{3,19},{20,4},{4,... | collective-permute-start | bytes 49160 | tf_op jit(solution)/shard_map/ppermute | solution.py:481
  23.6 2.0 %collective-permute-done.5.refs_1_ = f32[32,128]{1,0:T(8,128)S(1)} collective-permute-done((f32[32,128]{1,0:T(8,128)S(1)}, f32[32,128]{1,0:T(8,128)S(1)}, u32[]{:S(2)}, u32[]{:S(2)}) %collective-permute-start.5) | collective-permute-done | bytes 16416 | tf_op jit(solution)/shard_map/ppermute | solution.py:481
  25.5 4.6 %all-to-all-done = f32[288,1,128]{2,1,0:T(1,128)S(1)} async-done(((f32[288,1,128]{2,1,0:T(1,128)}), f32[288,1,128]{2,1,0:T(1,128)S(1)}, u32[]{:S(2)}, u32[]{:S(2)}) %all-to-all-start) | async-done | bytes 147488 | tf_op jit(solution)/shard_map/all_to_all | solution.py:560
  30.1 1.0 %combine.1 = (f32[64,1024]{1,0:T(8,128)}, f32[64,1024]{1,0:T(8,128)}) custom-call(f32[288,128]{1,0:T(8,128)S(1)} %bitcast.6, f32[64,8,128]{2,1,0:T(8,128)S(1)} %get-tuple-element.27.field_ref.start_ref, f32[64,8,128]{2,1,0:T(8,128)S(1)} %get-tuple-element.36.field_ref.next_ref, f32[64,8,128]{2,1,0:T(8,128)S(1)} %get-tuple-element.38.right_ref, ...), custom_call_target="tpu_custom_call" | custom-call | tf_op jit(solution)/shard_map/combine/pallas_call | solution.py:561
Async XLA Ops:
  0.6 5.5 %copy-start = (f32[64,1024]{1,0:T(8,128)S(1)}, f32[64,1024]{1,0:T(8,128)}, u32[]{:S(2)}) copy-start(f32[64,1024]{1,0:T(8,128)} %kappa_ref.1) | copy-start | bytes 786436
  3.1 4.9 %collective-permute-start = (f32[72,128]{1,0:T(8,128)S(1)}, f32[72,128]{1,0:T(8,128)S(1)}, u32[]{:S(2)}, u32[]{:S(2)}) collective-permute-start(f32[72,128]{1,0:T(8,128)S(1)} %get-tuple-element.26.refs_0_), channel_id=1, source_target_pairs={{16,0},{0,16},{17,1},{1,17},{18,2},{2,18},{19,3},{3,19},{20,4},{4,... | collective-permute-start | bytes 110600 | tf_op jit(solution)/shard_map/ppermute | solution.py:481
  8.3 8.1 %collective-permute-start.2 = (f32[5,8,128]{2,1,0:T(8,128)S(1)}, f32[5,8,128]{2,1,0:T(8,128)S(1)}, u32[]{:S(2)}, u32[]{:S(2)}) collective-permute-start(f32[5,8,128]{2,1,0:T(8,128)S(1)} %get-tuple-element.32), channel_id=1, source_target_pairs={{0,15},{1,2},{2,1},{3,4},{4,3},{5,6},{6,5},{7,8},{8,7},{9,10},{10,... | collective-permute-start | bytes 61448 | tf_op jit(solution)/shard_map/ppermute | solution.py:532
  12.6 3.8 %collective-permute-start.3 = (f32[32,128]{1,0:T(8,128)S(1)}, f32[32,128]{1,0:T(8,128)S(1)}, u32[]{:S(2)}, u32[]{:S(2)}) collective-permute-start(f32[32,128]{1,0:T(8,128)S(1)} %get-tuple-element.35.refs_0_), channel_id=1, source_target_pairs={{16,0},{0,16},{17,1},{1,17},{18,2},{2,18},{19,3},{3,19},{20,4},{4,... | collective-permute-start | bytes 49160 | tf_op jit(solution)/shard_map/ppermute | solution.py:481
  14.2 1.2 %collective-permute-start.1 = (f32[3,8,128]{2,1,0:T(8,128)S(1)}, f32[3,8,128]{2,1,0:T(8,128)S(1)}, u32[]{:S(2)}, u32[]{:S(2)}) collective-permute-start(f32[3,8,128]{2,1,0:T(8,128)S(1)} %get-tuple-element.31), channel_id=1, source_target_pairs={{0,1},{1,0},{2,3},{3,2},{4,5},{5,4},{6,7},{7,6},{8,9},{9,8},{10,11... | collective-permute-start | bytes 36872 | tf_op jit(solution)/shard_map/ppermute | solution.py:537
  16.8 1.2 %collective-permute-start.4 = (f32[2,8,128]{2,1,0:T(8,128)S(1)}, f32[2,8,128]{2,1,0:T(8,128)S(1)}, u32[]{:S(2)}, u32[]{:S(2)}) collective-permute-start(f32[2,8,128]{2,1,0:T(8,128)S(1)} %get-tuple-element.37), channel_id=1, source_target_pairs={{0,1},{1,0},{2,3},{3,2},{4,5},{5,4},{6,7},{7,6},{8,9},{9,8},{10,11... | collective-permute-start | bytes 24584 | tf_op jit(solution)/shard_map/ppermute | solution.py:546
  18.8 11.3 %all-to-all-start = ((f32[288,1,128]{2,1,0:T(1,128)}), f32[288,1,128]{2,1,0:T(1,128)S(1)}, u32[]{:S(2)}, u32[]{:S(2)}) async-start(f32[288,1,128]{2,1,0:T(1,128)} %bitcast.3), calls=%async_computation | async-start | bytes 294912 | tf_op jit(solution)/shard_map/all_to_all | solution.py:560
  21.7 3.8 %collective-permute-start.5 = (f32[32,128]{1,0:T(8,128)S(1)}, f32[32,128]{1,0:T(8,128)S(1)}, u32[]{:S(2)}, u32[]{:S(2)}) collective-permute-start(f32[32,128]{1,0:T(8,128)S(1)} %get-tuple-element.43.refs_0_), channel_id=1, source_target_pairs={{16,0},{0,16},{17,1},{1,17},{18,2},{2,18},{19,3},{3,19},{20,4},{4,... | collective-permute-start | bytes 49160 | tf_op jit(solution)/shard_map/ppermute | solution.py:481

commit v4 on v3

--- a/solution.py
+++ b/solution.py
@@ -216,9 +216,21 @@
     store_edges(parity, top, bottom, even_ref, odd_ref)
 
 
-def normal_kernel(pick_ref, field_ref, blocks_ref, even_ref, out_ref, even_out_ref):
-    normal_slots(pick_ref, field_ref[...], blocks_ref, out_ref)
+def normal_kernel(
+    count_ref, pick_ref, field_ref, blocks_ref, even_ref, out_ref, even_out_ref
+):
     even_out_ref[...] = even_ref[...]
+    slots = pick_ref.shape[0]
+    half = max(slots // (2 * GROUP), 1) * GROUP
+    few = count_ref[0, 0] <= half
+
+    @pl.when(few)
+    def _():
+        normal_slots(pick_ref, field_ref[...], blocks_ref, out_ref, half)
+
+    @pl.when(jnp.logical_not(few))
+    def _():
+        normal_slots(pick_ref, field_ref[...], blocks_ref, out_ref)
 
 
 def scattered(one_hot, slots):
@@ -245,13 +257,17 @@
     return jnp.where(flip, even, odd), jnp.where(flip, odd, even)
 
 
-def normal_slots(pick_ref, field, blocks_ref, out_ref):
+def normal_slots(pick_ref, field, blocks_ref, out_ref, used=None):
     width = field.shape[-1]
     field = field.reshape(pick_ref.shape[1], width)
-    picked = dot(pick_ref[...], jnp.concatenate(two_terms(field), axis=1))
+    used = used or pick_ref.shape[0]
+    picked = dot(pick_ref[pl.ds(0, used), :], jnp.concatenate(two_terms(field), axis=1))
     picked = picked[:, :width] + picked[:, width:]
     energy = jnp.zeros((GROUP, width), F32)
-    for group in range(picked.shape[0] // GROUP):
+    spare = pick_ref.shape[0] - used
+    if spare:
+        out_ref[pl.ds(used, spare), :] = jnp.zeros((spare, width), F32)
+    for group in range(used // GROUP):
         cells = picked[group * GROUP : (group + 1) * GROUP]
         rows = stacked_terms(cells)
         rows = jnp.concatenate([rows, rows], axis=1)
@@ -282,7 +298,7 @@
     return scattered(scatter_ref[...], order_ref[...])
 
 
-def first_kernel(
+def pair_edge_kernel(
     parity,
     orbits,
     field_ref,
@@ -294,17 +310,28 @@
     *refs,
 ):
     slot_refs = refs[:orbits]
-    image_ref, next_ref, edge_ref, order_ref = refs[orbits:]
-    normal = scattered_slots(orbits, scatter_ref, slot_refs, order_ref)
+    edge_ref, order_ref = refs[orbits:]
+    slots = slot_refs[0].shape[0]
+    gather_messages(orbits, slots, [ref[...] for ref in slot_refs], order_ref)
+    columns, pieces, width = field_ref.shape
+    flip = parity()
     top, bottom = load_edges(parity, even_ref, odd_ref)
-    prior = prior_parts(
-        field_ref[...], shifted_ref[...], top[:2], bottom[:2], top[2:], bottom[2:]
-    )
-    image = prior + normal.reshape(field_ref.shape)
-    following = image / precond_ref[...]
-    image_ref[...] = image
-    next_ref[...] = following
-    edge_ref[...] = jnp.where(parity(), following[:2], following[following.shape[0] - 2 :])
+    field = jnp.where(
+        flip,
+        extended(field_ref[pl.ds(0, 2)], top[:2], field_ref[pl.ds(2, 2)]),
+        extended(field_ref[pl.ds(columns - 2, 2)], field_ref[pl.ds(columns - 4, 2)], bottom[:2]),
+    )
+    shifted = jnp.where(
+        flip,
+        jnp.concatenate([top[2:], shifted_ref[pl.ds(0, 3)]], axis=0),
+        jnp.concatenate([shifted_ref[pl.ds(columns - 3, 3)], bottom[2:]], axis=0),
+    )
+    once = stencil(field, shifted)
+    twice = stencil(once, shifted[1:-1])
+    start = jnp.where(flip, 0, columns - 2)
+    rows = pl.ds(pl.multiple_of(start * pieces, 2 * pieces), 2 * pieces)
+    normal = scattered(scatter_ref[rows, :], order_ref[...]).reshape(twice.shape)
+    edge_ref[...] = (PRIOR_WEIGHT * twice + normal) / precond_ref[pl.ds(start, 2)]
 
 
 def alone(field, shifted):
@@ -312,33 +339,6 @@
     return stencil(extended(field, zero, zero), shifted)
 
 
-def inner_kernel(
-    field_ref,
-    shifted_ref,
-    start_ref,
-    right_ref,
-    first_ref,
-    pick_ref,
-    blocks_ref,
-    base_ref,
-    ends_ref,
-    parts_ref,
-    out_ref,
-):
-    field, shifted = field_ref[...], shifted_ref[...]
-    energy = normal_slots(pick_ref, field, blocks_ref, out_ref)
-    start, first = start_ref[...], first_ref[...]
-    once = alone(field, shifted)
-    base_ref[...] = PRIOR_WEIGHT * alone(once, shifted)
-    ends_ref[0] = once[0]
-    ends_ref[1] = once[once.shape[0] - 1]
-    own = jnp.where(lax.axis_index("orbit") == 0, 1.0, 0.0)
-    parts_ref[0] = own * jnp.sum(right_ref[...] * start, axis=0)
-    parts_ref[1] = own * jnp.sum(start * first, axis=0)
-    parts_ref[2] = own * jnp.sum(first * field, axis=0)
-    parts_ref[3] = own * PRIOR_WEIGHT * jnp.sum(once * once, axis=0) + energy
-
-
 def sides(parity, top, bottom):
     flip = parity()
     return jnp.where(flip, top, bottom), jnp.where(flip, bottom, top)
@@ -349,24 +349,70 @@
     return jnp.where(flip, even_ref[1], even_ref[0]), jnp.where(flip, even_ref[0], even_ref[1])
 
 
-def edge_kernel(parity, field_ref, even_ref, ends_ref, parts_ref, message_ref):
-    columns = field_ref.shape[0]
+def chunks_of(rows):
+    return jnp.concatenate([rows] * GROUP, axis=0)
+
+
+def images_kernel(
+    parity,
+    orbits,
+    field_ref,
+    shifted_ref,
+    even_ref,
+    odd_ref,
+    scatter_ref,
+    precond_ref,
+    right_ref,
+    pick_ref,
+    blocks_ref,
+    *refs,
+):
+    slot_refs = refs[:orbits]
+    image_ref, next_ref, base_ref, end_ref, parts_ref, chunks_ref, out_ref, order_ref = refs[orbits:]
+    normal = scattered_slots(orbits, scatter_ref, slot_refs, order_ref)
+    top, bottom = load_edges(parity, even_ref, odd_ref)
+    start, shifted = field_ref[...], shifted_ref[...]
+    prior = prior_parts(start, shifted, top[:2], bottom[:2], top[2:], bottom[2:])
+    image = prior + normal.reshape(start.shape)
+    field = image / precond_ref[...]
+    image_ref[...] = image
+    next_ref[...] = field
+    energy = normal_slots(pick_ref, field, blocks_ref, out_ref)
+    once = alone(field, shifted)
+    base_ref[...] = PRIOR_WEIGHT * alone(once, shifted)
+    last = once.shape[0] - 1
+    even_end, odd_end = sides(parity, once[0], once[last])
+    _, odd_field = sides(parity, field[0], field[last])
+    end_ref[...] = even_end
+    orbit = lax.axis_index("orbit")
+    own = jnp.where(orbit == 0, 1.0, 0.0)
+    squares = jnp.sum(once * once, axis=0) + odd_field * odd_field
+    parts = (
+        own * jnp.sum(right_ref[...] * start, axis=0),
+        own * jnp.sum(start * image, axis=0),
+        own * jnp.sum(image * field, axis=0),
+        own * PRIOR_WEIGHT * squares + energy,
+    )
+    for index, part in enumerate(parts):
+        parts_ref[pl.ds(index, 1), :] = jnp.sum(part, axis=0, keepdims=True)
+    edge = jnp.where(orbit == 0, odd_end, odd_field)
+    chunks_ref[...] = chunks_of(jnp.concatenate([edge, jnp.zeros((1, LANES), F32)], axis=0))
+
+
+def edge_kernel(parity, even_ref, end_ref, parts_ref, chunks_ref, message_ref):
     near, _ = near_far(parity, even_ref)
-    even_end, odd_end = sides(parity, ends_ref[0], ends_ref[1])
-    _, odd_field = sides(parity, field_ref[0], field_ref[columns - 1])
-    orbit = lax.axis_index("orbit")
-    own = jnp.where(orbit == 0, PRIOR_WEIGHT, 0.0)
-    more = own * (near * (near - 2.0 * even_end) + odd_field * odd_field)
-    sums = [jnp.sum(parts_ref[index], axis=0, keepdims=True) for index in range(3)]
-    sums.append(jnp.sum(parts_ref[3] + more, axis=0, keepdims=True))
-    sums = jnp.sum(jnp.concatenate(sums, axis=0), axis=1, keepdims=True)
+    own = jnp.where(lax.axis_index("orbit") == 0, PRIOR_WEIGHT, 0.0)
+    more = own * jnp.sum(near * (near - 2.0 * end_ref[...]), axis=0, keepdims=True)
+    index = lax.broadcasted_iota(jnp.int32, (4, LANES), 0)
     lane = lax.broadcasted_iota(jnp.int32, (4, LANES), 1)
-    index = lax.broadcasted_iota(jnp.int32, (4, LANES), 0)
+    sums = jnp.sum(parts_ref[...] + jnp.where(index == 3, more, 0.0), axis=1, keepdims=True)
     line = jnp.sum(jnp.where(lane == index, sums, 0.0), axis=0, keepdims=True)
-    row = jnp.concatenate([jnp.where(orbit == 0, odd_end, odd_field), line], axis=0)
-    several = jnp.concatenate([row] * GROUP, axis=0)
-    for index in range(message_ref.shape[0] // several.shape[0]):
-        message_ref[pl.ds(index * several.shape[0], several.shape[0]), :] = several
+    rows = chunks_ref.shape[0]
+    period = rows // GROUP
+    row = lax.broadcasted_iota(jnp.int32, (rows, LANES), 0)
+    chunks = jnp.where(lax.rem(row, period) == period - 1, line, chunks_ref[...])
+    for index in range(message_ref.shape[0] // rows):
+        message_ref[pl.ds(index * rows, rows), :] = chunks
 
 
 def last_kernel(
@@ -530,33 +576,47 @@
         "start",
     )(shifted, *messages)
     rim_odd = lax.ppermute(odd, "lon", odd_pairs)
-    terms, even = call(normal_kernel, (slot_terms, rim), [vmem] * 4, (), "normal_start", work=WORK)(
-        pick, start, blocks, even
-    )
+    terms, even = call(
+        normal_kernel,
+        (slot_terms, rim),
+        [smem] + [vmem] * 4,
+        (),
+        "normal_start",
+        work=WORK,
+    )(live_count, pick, start, blocks, even)
     terms = from_others(terms)
     rim_even = lax.ppermute(even, "lon", even_pairs)
-    first, following, even = call(
-        functools.partial(first_kernel, parity, orbits),
-        (field, field, edge),
+    image_inputs = (start, shifted, rim_even, rim_odd, scatter, precond, *terms)
+    (even,) = call(
+        functools.partial(pair_edge_kernel, parity, orbits),
+        (edge,),
         [vmem] * (6 + orbits),
         [order],
-        "first_image",
-    )(start, shifted, rim_even, rim_odd, scatter, precond, *terms)
-
+        "pair_edge",
+    )(*image_inputs)
     even = lax.ppermute(even, "lon", even_pairs)
-    base, ends, parts, terms = call(
-        inner_kernel,
-        (field, edge, ((4, pieces, width), F32), slot_terms),
-        [vmem] * 7,
-        (),
-        "inner_image",
+    chunk = pieces + 1
+    first, following, base, end, parts, chunks, terms = call(
+        functools.partial(images_kernel, parity, orbits),
+        (
+            field,
+            field,
+            field,
+            ((pieces, width), F32),
+            ((4, width), F32),
+            ((GROUP * chunk, width), F32),
+            slot_terms,
+        ),
+        [vmem] * (9 + orbits),
+        [order],
+        "images",
         work=WORK,
-    )(following, shifted, start, right_side, first, pick, blocks)
+    )(*image_inputs[:6], right_side, pick, blocks, *terms)
     terms = from_others(terms)
-    message = ((orbits * bands * (pieces + 1), width), F32)
+    message = ((orbits * bands * chunk, width), F32)
     (sums,) = call(
         functools.partial(edge_kernel, parity), (message,), [vmem] * 4, (), "edge_sums"
-    )(following, even, ends, parts)
+    )(even, end, parts, chunks)
     sums = lax.all_to_all(sums[:, None], ("orbit", "lon"), 0, 0, tiled=True)[:, 0]
     return call(
         functools.partial(last_kernel, parity, orbits, bands),

time: 31.3 us -> 30.9 us (0.987)
  Pallas kernels: 6.96 us -> 6.56 us
    ppermute x3, waiting for transfers between devices: 3.46 us -> 3.93 us  [from_others(): lax.ppermute(value, 'orbit', [((i + step) % orbits, i) for i in range(orb...]
where the time goes in v4:
time: 30.9 us; the launch traced here: 30.6 us
  starting transfers between devices  12.8 us (41%)
  waiting for transfers between devices  9.95 us (32%)
  Pallas kernels  6.56 us (21%)
  between operations  1.39 us (4%)
    ppermute x3, starting transfers between devices, from_others(): lax.ppermute(value, 'orbit', [((i + step) % orbits, i) for i in range(orb...  6.06 us
    all_to_all x1, waiting for transfers between devices, per_device(): lax.all_to_all(sums[:, None], ('orbit', 'lon'), 0, 0, tiled=True)[:, 0]  4.62 us
    ppermute x3, waiting for transfers between devices, from_others(): lax.ppermute(value, 'orbit', [((i + step) % orbits, i) for i in range(orb...  3.93 us
    ppermute x1, starting transfers between devices, per_device(): rim_odd = lax.ppermute(odd, 'lon', odd_pairs)  3.59 us
    all_to_all x1, starting transfers between devices, per_device(): lax.all_to_all(sums[:, None], ('orbit', 'lon'), 0, 0, tiled=True)[:, 0]  3.02 us
    pallas_call x1, Pallas kernels, per_device(): call(block_kernel, ((field_shape, F32), ((slots // 2, 2 * width, 2 * widt...  1.51 us
    pallas_call x1, Pallas kernels, per_device(): call(functools.partial(data_kernel, orbits), (((2 * slots + GROUP, width)...  1.45 us
    ppermute x1, waiting for transfers between devices, per_device(): rim_even = lax.ppermute(even, 'lon', even_pairs)  1.18 us
  transfers between devices with their start and end apart: 7, of which 6 were waited for; matrix products, arithmetic and copies ran while one was open for 0% of the time, Pallas kernels for 9%

profile of v4, /device:TPU:0, one launch (start us, length us, event | category | flops | bytes accessed | tf_op | source)
XLA Modules:
  0.0 30.6 jit_solution(13099246380702327190)
XLA Ops:
  0.6 0.0 copy-start
  1.3 1.5 %data_terms.1 = (f32[72,128]{1,0:T(8,128)S(1)}, bf16[32,256,128]{2,1,0:T(8,128)(2,1)S(1)}, f32[32,256]{1,0:T(8,128)S(1)}, bf16[32,512]{1,0:T(8,128)(2,1)S(1)}) custom-call(s32[1,1]{1,0:T(1,128)S(6)} %copy.9.count_ref, s32[32]{0:T(128)} %bitcast.8, bf16[32,256,128]{2,1,0:T(8,128)(2,1)} %bitcast.7, f32[32,1,256]{2,1,0:T(1,128)} %value_in.1, ...), custom_call_target="tpu_custom_call" | custom-call | tf_op jit(solution)/shard_map/data_terms/pallas_call | solution.py:536
  2.8 3.0 %collective-permute-start = (f32[72,128]{1,0:T(8,128)S(1)}, f32[72,128]{1,0:T(8,128)S(1)}, u32[]{:S(2)}, u32[]{:S(2)}) collective-permute-start(f32[72,128]{1,0:T(8,128)S(1)} %get-tuple-element.26.refs_0_), channel_id=1, source_target_pairs={{16,0},{0,16},{17,1},{1,17},{18,2},{2,18},{19,3},{3,19},{20,4},{4,... | collective-permute-start | bytes 110600 | tf_op jit(solution)/shard_map/ppermute | solution.py:527
  5.8 0.0 copy-done
  5.8 1.5 %blocks.1 = (f32[64,8,128]{2,1,0:T(8,128)S(1)}, bf16[16,256,256]{2,1,0:T(8,128)(2,1)S(1)}) custom-call(f32[64,1024]{1,0:T(8,128)S(1)} %copy-done, bf16[32,256,128]{2,1,0:T(8,128)(2,1)S(1)} %get-tuple-element.23.matrices_ref, f32[32,256]{1,0:T(8,128)S(1)} %get-tuple-element.24.weight_ref), custom_call_target="tpu_custom_call" | custom-call | flops 4294967296 | tf_op jit(solution)/shard_map/blocks/pallas_call | solution.py:555
  7.3 0.6 %collective-permute-done.refs_1_ = f32[72,128]{1,0:T(8,128)S(1)} collective-permute-done((f32[72,128]{1,0:T(8,128)S(1)}, f32[72,128]{1,0:T(8,128)S(1)}, u32[]{:S(2)}, u32[]{:S(2)}) %collective-permute-start) | collective-permute-done | bytes 36896 | tf_op jit(solution)/shard_map/ppermute | solution.py:527
  7.9 0.3 start.1
  8.2 3.6 %collective-permute-start.2 = (f32[5,8,128]{2,1,0:T(8,128)S(1)}, f32[5,8,128]{2,1,0:T(8,128)S(1)}, u32[]{:S(2)}, u32[]{:S(2)}) collective-permute-start(f32[5,8,128]{2,1,0:T(8,128)S(1)} %get-tuple-element.32), channel_id=1, source_target_pairs={{0,15},{1,2},{2,1},{3,4},{4,3},{5,6},{6,5},{7,8},{8,7},{9,10},{10,... | collective-permute-start | bytes 61448 | tf_op jit(solution)/shard_map/ppermute | solution.py:578
  11.8 0.4 %normal_start.1 = (f32[32,128]{1,0:T(8,128)S(1)}, f32[3,8,128]{2,1,0:T(8,128)S(1)}) custom-call(s32[1,1]{1,0:T(1,128)S(6)} %copy.9.count_ref, bf16[32,512]{1,0:T(8,128)(2,1)S(1)} %get-tuple-element.28.pick_ref, f32[64,8,128]{2,1,0:T(8,128)S(1)} %get-tuple-element.27.field_ref.start_ref, bf16[16,256,256]{2,1,0:T(8,128)(2,1)S(1)} %get-tuple-element.29.blocks_ref, ...), custom_call_target="tpu_custom_call" | custom-call | flops 4294967296 | tf_op jit(solution)/shard_map/normal_start/pallas_call | solution.py:579
  12.2 1.2 %collective-permute-start.3 = (f32[32,128]{1,0:T(8,128)S(1)}, f32[32,128]{1,0:T(8,128)S(1)}, u32[]{:S(2)}, u32[]{:S(2)}) collective-permute-start(f32[32,128]{1,0:T(8,128)S(1)} %get-tuple-element.35.refs_0_), channel_id=1, source_target_pairs={{16,0},{0,16},{17,1},{1,17},{18,2},{2,18},{19,3},{3,19},{20,4},{4,... | collective-permute-start | bytes 49160 | tf_op jit(solution)/shard_map/ppermute | solution.py:527
  13.4 0.0 collective-permute-start.1
  13.4 1.2 %collective-permute-done.1.even_ref.rim_ref = f32[3,8,128]{2,1,0:T(8,128)S(1)} collective-permute-done((f32[3,8,128]{2,1,0:T(8,128)S(1)}, f32[3,8,128]{2,1,0:T(8,128)S(1)}, u32[]{:S(2)}, u32[]{:S(2)}) %collective-permute-start.1) | collective-permute-done | bytes 12320 | tf_op jit(solution)/shard_map/ppermute | solution.py:588
  14.6 1.4 %collective-permute-done.3.refs_1_ = f32[32,128]{1,0:T(8,128)S(1)} collective-permute-done((f32[32,128]{1,0:T(8,128)S(1)}, f32[32,128]{1,0:T(8,128)S(1)}, u32[]{:S(2)}, u32[]{:S(2)}) %collective-permute-start.3) | collective-permute-done | bytes 16416 | tf_op jit(solution)/shard_map/ppermute | solution.py:527
  16.0 0.0 collective-permute-done.2.odd_ref
  16.0 0.2 pair_edge.1
  16.1 0.1 collective-permute-start.4
  16.2 0.9 %images.1 = (f32[64,8,128]{2,1,0:T(8,128)S(1)}, f32[64,8,128]{2,1,0:T(8,128)S(1)}, f32[64,8,128]{2,1,0:T(8,128)S(1)}, f32[8,128]{1,0:T(8,128)S(1)}, f32[4,128]{1...) custom-call(f32[64,8,128]{2,1,0:T(8,128)S(1)} %get-tuple-element.27.field_ref.start_ref, ...), custom_call_target="tpu_custom_call" | custom-call | flops 4294967296 | tf_op jit(solution)/shard_map/images/pallas_call | solution.py:599
  17.1 0.2 collective-permute-done.4.even_ref
  17.4 0.8 %edge_sums.1 = f32[288,128]{1,0:T(8,128)} custom-call(f32[2,8,128]{2,1,0:T(8,128)S(1)} %collective-permute-done.4.even_ref, f32[8,128]{1,0:T(8,128)S(1)} %get-tuple-element.37.end_ref, f32[4,128]{1,0:T(4,128)S(1)} %get-tuple-element.38.parts_ref, f32[72,128]{1,0:T(8,128)S(1)} %get-tuple-element.39.chunks_ref), custom_call_target="tpu_custom_call" | custom-call | tf_op jit(solution)/shard_map/edge_sums/pallas_call | solution.py:617
  18.1 3.0 %all-to-all-start = ((f32[288,1,128]{2,1,0:T(1,128)}), f32[288,1,128]{2,1,0:T(1,128)S(1)}, u32[]{:S(2)}, u32[]{:S(2)}) async-start(f32[288,1,128]{2,1,0:T(1,128)} %bitcast.3), calls=%async_computation | async-start | bytes 294912 | tf_op jit(solution)/shard_map/all_to_all | solution.py:620
  21.2 1.8 %collective-permute-start.5 = (f32[32,128]{1,0:T(8,128)S(1)}, f32[32,128]{1,0:T(8,128)S(1)}, u32[]{:S(2)}, u32[]{:S(2)}) collective-permute-start(f32[32,128]{1,0:T(8,128)S(1)} %get-tuple-element.43.refs_0_), channel_id=1, source_target_pairs={{16,0},{0,16},{17,1},{1,17},{18,2},{2,18},{19,3},{3,19},{20,4},{4,... | collective-permute-start | bytes 49160 | tf_op jit(solution)/shard_map/ppermute | solution.py:527
  23.0 2.0 %collective-permute-done.5.refs_1_ = f32[32,128]{1,0:T(8,128)S(1)} collective-permute-done((f32[32,128]{1,0:T(8,128)S(1)}, f32[32,128]{1,0:T(8,128)S(1)}, u32[]{:S(2)}, u32[]{:S(2)}) %collective-permute-start.5) | collective-permute-done | bytes 16416 | tf_op jit(solution)/shard_map/ppermute | solution.py:527
  25.0 4.6 %all-to-all-done = f32[288,1,128]{2,1,0:T(1,128)S(1)} async-done(((f32[288,1,128]{2,1,0:T(1,128)}), f32[288,1,128]{2,1,0:T(1,128)S(1)}, u32[]{:S(2)}, u32[]{:S(2)}) %all-to-all-start) | async-done | bytes 147488 | tf_op jit(solution)/shard_map/all_to_all | solution.py:620
  29.6 1.0 %combine.1 = (f32[64,1024]{1,0:T(8,128)}, f32[64,1024]{1,0:T(8,128)}) custom-call(f32[288,128]{1,0:T(8,128)S(1)} %bitcast.6, f32[64,8,128]{2,1,0:T(8,128)S(1)} %get-tuple-element.27.field_ref.start_ref, f32[64,8,128]{2,1,0:T(8,128)S(1)} %get-tuple-element.40.next_ref, f32[64,8,128]{2,1,0:T(8,128)S(1)} %get-tuple-element.36.right_ref, ...), custom_call_target="tpu_custom_call" | custom-call | tf_op jit(solution)/shard_map/combine/pallas_call | solution.py:621
Async XLA Ops:
  0.6 5.2 %copy-start = (f32[64,1024]{1,0:T(8,128)S(1)}, f32[64,1024]{1,0:T(8,128)}, u32[]{:S(2)}) copy-start(f32[64,1024]{1,0:T(8,128)} %kappa_ref.1) | copy-start | bytes 786436
  2.8 5.1 %collective-permute-start = (f32[72,128]{1,0:T(8,128)S(1)}, f32[72,128]{1,0:T(8,128)S(1)}, u32[]{:S(2)}, u32[]{:S(2)}) collective-permute-start(f32[72,128]{1,0:T(8,128)S(1)} %get-tuple-element.26.refs_0_), channel_id=1, source_target_pairs={{16,0},{0,16},{17,1},{1,17},{18,2},{2,18},{19,3},{3,19},{20,4},{4,... | collective-permute-start | bytes 110600 | tf_op jit(solution)/shard_map/ppermute | solution.py:527
  8.2 7.8 %collective-permute-start.2 = (f32[5,8,128]{2,1,0:T(8,128)S(1)}, f32[5,8,128]{2,1,0:T(8,128)S(1)}, u32[]{:S(2)}, u32[]{:S(2)}) collective-permute-start(f32[5,8,128]{2,1,0:T(8,128)S(1)} %get-tuple-element.32), channel_id=1, source_target_pairs={{0,15},{1,2},{2,1},{3,4},{4,3},{5,6},{6,5},{7,8},{8,7},{9,10},{10,... | collective-permute-start | bytes 61448 | tf_op jit(solution)/shard_map/ppermute | solution.py:578
  12.2 3.8 %collective-permute-start.3 = (f32[32,128]{1,0:T(8,128)S(1)}, f32[32,128]{1,0:T(8,128)S(1)}, u32[]{:S(2)}, u32[]{:S(2)}) collective-permute-start(f32[32,128]{1,0:T(8,128)S(1)} %get-tuple-element.35.refs_0_), channel_id=1, source_target_pairs={{16,0},{0,16},{17,1},{1,17},{18,2},{2,18},{19,3},{3,19},{20,4},{4,... | collective-permute-start | bytes 49160 | tf_op jit(solution)/shard_map/ppermute | solution.py:527
  13.4 1.2 %collective-permute-start.1 = (f32[3,8,128]{2,1,0:T(8,128)S(1)}, f32[3,8,128]{2,1,0:T(8,128)S(1)}, u32[]{:S(2)}, u32[]{:S(2)}) collective-permute-start(f32[3,8,128]{2,1,0:T(8,128)S(1)} %get-tuple-element.31), channel_id=1, source_target_pairs={{0,1},{1,0},{2,3},{3,2},{4,5},{5,4},{6,7},{7,6},{8,9},{9,8},{10,11... | collective-permute-start | bytes 36872 | tf_op jit(solution)/shard_map/ppermute | solution.py:588
  16.1 1.2 %collective-permute-start.4 = (f32[2,8,128]{2,1,0:T(8,128)S(1)}, f32[2,8,128]{2,1,0:T(8,128)S(1)}, u32[]{:S(2)}, u32[]{:S(2)}) collective-permute-start(f32[2,8,128]{2,1,0:T(8,128)S(1)} %pair_edge.1), channel_id=1, source_target_pairs={{0,1},{1,0},{2,3},{3,2},{4,5},{5,4},{6,7},{7,6},{8,9},{9,8},{10,11... | collective-permute-start | bytes 24584 | tf_op jit(solution)/shard_map/ppermute | solution.py:597
  18.1 11.5 %all-to-all-start = ((f32[288,1,128]{2,1,0:T(1,128)}), f32[288,1,128]{2,1,0:T(1,128)S(1)}, u32[]{:S(2)}, u32[]{:S(2)}) async-start(f32[288,1,128]{2,1,0:T(1,128)} %bitcast.3), calls=%async_computation | async-start | bytes 294912 | tf_op jit(solution)/shard_map/all_to_all | solution.py:620
  21.2 3.8 %collective-permute-start.5 = (f32[32,128]{1,0:T(8,128)S(1)}, f32[32,128]{1,0:T(8,128)S(1)}, u32[]{:S(2)}, u32[]{:S(2)}) collective-permute-start(f32[32,128]{1,0:T(8,128)S(1)} %get-tuple-element.43.refs_0_), channel_id=1, source_target_pairs={{16,0},{0,16},{17,1},{1,17},{18,2},{2,18},{19,3},{3,19},{20,4},{4,... | collective-permute-start | bytes 49160 | tf_op jit(solution)/shard_map/ppermute | solution.py:527

commit v5 on v4

--- a/solution.py
+++ b/solution.py
@@ -35,10 +35,6 @@
 
 def dot(left, right):
     return lax.dot_general(left, right, (((1,), (0,)), ((), ())), preferred_element_type=F32)
-
-
-def dot_transposed(left, right):
-    return lax.dot_general(left, right, (((1,), (1,)), ((), ())), preferred_element_type=F32)
 
 
 def pick_row(total, product, slot):
@@ -455,11 +451,9 @@
     )
     following = following - (2.0 * PRIOR_WEIGHT) * open_sides
     alpha = product / energy
-    later = product - 2.0 * alpha * energy + alpha * alpha * cross
+    later = alpha * alpha * cross - product
     grown = 1.0 + later / product
-    later_energy = (
-        grown * grown * energy - 2.0 * alpha * grown * cross + alpha * alpha * following
-    )
+    later_energy = alpha * alpha * following - grown * grown * energy
     later_alpha = later / later_energy
     on_start = alpha + later_alpha * grown
     on_next = -alpha * later_alpha

time: 30.9 us -> 31.1 us (level)
  starting transfers between devices: 12.8 us -> 13.5 us
  waiting for transfers between devices: 9.95 us -> 9.28 us
    ppermute x3, starting transfers between devices: 6.06 us -> 7.19 us  [from_others(): lax.ppermute(value, 'orbit', [((i + step) % orbits, i) for i in range(orb...]
    ppermute x3, waiting for transfers between devices: 3.93 us -> 3.26 us  [from_others(): lax.ppermute(value, 'orbit', [((i + step) % orbits, i) for i in range(orb...]
    ppermute x1, starting transfers between devices: 3.59 us -> 3.08 us  [per_device(): rim_odd = lax.ppermute(odd, 'lon', odd_pairs)]
where the time goes in v5:
time: 31.1 us; the launch traced here: 30.8 us
  starting transfers between devices  13.5 us (43%)
  waiting for transfers between devices  9.28 us (30%)
  Pallas kernels  6.55 us (21%)
  between operations  1.39 us (4%)
    ppermute x3, starting transfers between devices, from_others(): lax.ppermute(value, 'orbit', [((i + step) % orbits, i) for i in range(orb...  7.19 us
    all_to_all x1, waiting for transfers between devices, per_device(): lax.all_to_all(sums[:, None], ('orbit', 'lon'), 0, 0, tiled=True)[:, 0]  4.62 us
    ppermute x3, waiting for transfers between devices, from_others(): lax.ppermute(value, 'orbit', [((i + step) % orbits, i) for i in range(orb...  3.26 us
    all_to_all x1, starting transfers between devices, per_device(): lax.all_to_all(sums[:, None], ('orbit', 'lon'), 0, 0, tiled=True)[:, 0]  3.2 us
    ppermute x1, starting transfers between devices, per_device(): rim_odd = lax.ppermute(odd, 'lon', odd_pairs)  3.08 us
    pallas_call x1, Pallas kernels, per_device(): call(block_kernel, ((field_shape, F32), ((slots // 2, 2 * width, 2 * widt...  1.51 us
    pallas_call x1, Pallas kernels, per_device(): call(functools.partial(data_kernel, orbits), (((2 * slots + GROUP, width)...  1.45 us
    ppermute x1, waiting for transfers between devices, per_device(): rim_even = lax.ppermute(even, 'lon', even_pairs)  1.18 us
  transfers between devices with their start and end apart: 7, of which 6 were waited for; matrix products, arithmetic and copies ran while one was open for 0% of the time, Pallas kernels for 9%

profile of v5, /device:TPU:0, one launch (start us, length us, event | category | flops | bytes accessed | tf_op | source)
XLA Modules:
  0.0 30.8 jit_solution(3890428552288357925)
XLA Ops:
  0.6 0.0 copy-start
  1.3 1.5 %data_terms.1 = (f32[72,128]{1,0:T(8,128)S(1)}, bf16[32,256,128]{2,1,0:T(8,128)(2,1)S(1)}, f32[32,256]{1,0:T(8,128)S(1)}, bf16[32,512]{1,0:T(8,128)(2,1)S(1)}) custom-call(s32[1,1]{1,0:T(1,128)S(6)} %copy.9.count_ref, s32[32]{0:T(128)} %bitcast.8, bf16[32,256,128]{2,1,0:T(8,128)(2,1)} %bitcast.7, f32[32,1,256]{2,1,0:T(1,128)} %value_in.1, ...), custom_call_target="tpu_custom_call" | custom-call | tf_op jit(solution)/shard_map/data_terms/pallas_call | solution.py:530
  2.8 3.6 %collective-permute-start = (f32[72,128]{1,0:T(8,128)S(1)}, f32[72,128]{1,0:T(8,128)S(1)}, u32[]{:S(2)}, u32[]{:S(2)}) collective-permute-start(f32[72,128]{1,0:T(8,128)S(1)} %get-tuple-element.26.refs_0_), channel_id=1, source_target_pairs={{16,0},{0,16},{17,1},{1,17},{18,2},{2,18},{19,3},{3,19},{20,4},{4,... | collective-permute-start | bytes 110600 | tf_op jit(solution)/shard_map/ppermute | solution.py:521
  6.4 0.0 copy-done
  6.4 1.5 %blocks.1 = (f32[64,8,128]{2,1,0:T(8,128)S(1)}, bf16[16,256,256]{2,1,0:T(8,128)(2,1)S(1)}) custom-call(f32[64,1024]{1,0:T(8,128)S(1)} %copy-done, bf16[32,256,128]{2,1,0:T(8,128)(2,1)S(1)} %get-tuple-element.23.matrices_ref, f32[32,256]{1,0:T(8,128)S(1)} %get-tuple-element.24.weight_ref), custom_call_target="tpu_custom_call" | custom-call | flops 4294967296 | tf_op jit(solution)/shard_map/blocks/pallas_call | solution.py:549
  7.9 0.4 %collective-permute-done.refs_1_ = f32[72,128]{1,0:T(8,128)S(1)} collective-permute-done((f32[72,128]{1,0:T(8,128)S(1)}, f32[72,128]{1,0:T(8,128)S(1)}, u32[]{:S(2)}, u32[]{:S(2)}) %collective-permute-start) | collective-permute-done | bytes 36896 | tf_op jit(solution)/shard_map/ppermute | solution.py:521
  8.4 0.3 start.1
  8.6 3.1 %collective-permute-start.2 = (f32[5,8,128]{2,1,0:T(8,128)S(1)}, f32[5,8,128]{2,1,0:T(8,128)S(1)}, u32[]{:S(2)}, u32[]{:S(2)}) collective-permute-start(f32[5,8,128]{2,1,0:T(8,128)S(1)} %get-tuple-element.32), channel_id=1, source_target_pairs={{0,15},{1,2},{2,1},{3,4},{4,3},{5,6},{6,5},{7,8},{8,7},{9,10},{10,... | collective-permute-start | bytes 61448 | tf_op jit(solution)/shard_map/ppermute | solution.py:572
  11.7 0.4 %normal_start.1 = (f32[32,128]{1,0:T(8,128)S(1)}, f32[3,8,128]{2,1,0:T(8,128)S(1)}) custom-call(s32[1,1]{1,0:T(1,128)S(6)} %copy.9.count_ref, bf16[32,512]{1,0:T(8,128)(2,1)S(1)} %get-tuple-element.28.pick_ref, f32[64,8,128]{2,1,0:T(8,128)S(1)} %get-tuple-element.27.field_ref.start_ref, bf16[16,256,256]{2,1,0:T(8,128)(2,1)S(1)} %get-tuple-element.29.blocks_ref, ...), custom_call_target="tpu_custom_call" | custom-call | flops 4294967296 | tf_op jit(solution)/shard_map/normal_start/pallas_call | solution.py:573
  12.1 1.7 %collective-permute-start.3 = (f32[32,128]{1,0:T(8,128)S(1)}, f32[32,128]{1,0:T(8,128)S(1)}, u32[]{:S(2)}, u32[]{:S(2)}) collective-permute-start(f32[32,128]{1,0:T(8,128)S(1)} %get-tuple-element.35.refs_0_), channel_id=1, source_target_pairs={{16,0},{0,16},{17,1},{1,17},{18,2},{2,18},{19,3},{3,19},{20,4},{4,... | collective-permute-start | bytes 49160 | tf_op jit(solution)/shard_map/ppermute | solution.py:521
  13.9 0.0 collective-permute-start.1
  13.9 1.2 %collective-permute-done.1.even_ref.rim_ref = f32[3,8,128]{2,1,0:T(8,128)S(1)} collective-permute-done((f32[3,8,128]{2,1,0:T(8,128)S(1)}, f32[3,8,128]{2,1,0:T(8,128)S(1)}, u32[]{:S(2)}, u32[]{:S(2)}) %collective-permute-start.1) | collective-permute-done | bytes 12320 | tf_op jit(solution)/shard_map/ppermute | solution.py:582
  15.0 0.9 %collective-permute-done.3.refs_1_ = f32[32,128]{1,0:T(8,128)S(1)} collective-permute-done((f32[32,128]{1,0:T(8,128)S(1)}, f32[32,128]{1,0:T(8,128)S(1)}, u32[]{:S(2)}, u32[]{:S(2)}) %collective-permute-start.3) | collective-permute-done | bytes 16416 | tf_op jit(solution)/shard_map/ppermute | solution.py:521
  15.9 0.0 collective-permute-done.2.odd_ref
  15.9 0.2 pair_edge.1
  16.1 0.1 collective-permute-start.4
  16.2 0.9 %images.1 = (f32[64,8,128]{2,1,0:T(8,128)S(1)}, f32[64,8,128]{2,1,0:T(8,128)S(1)}, f32[64,8,128]{2,1,0:T(8,128)S(1)}, f32[8,128]{1,0:T(8,128)S(1)}, f32[4,128]{1...) custom-call(f32[64,8,128]{2,1,0:T(8,128)S(1)} %get-tuple-element.27.field_ref.start_ref, ...), custom_call_target="tpu_custom_call" | custom-call | flops 4294967296 | tf_op jit(solution)/shard_map/images/pallas_call | solution.py:593
  17.1 0.2 collective-permute-done.4.even_ref
  17.3 0.8 %edge_sums.1 = f32[288,128]{1,0:T(8,128)} custom-call(f32[2,8,128]{2,1,0:T(8,128)S(1)} %collective-permute-done.4.even_ref, f32[8,128]{1,0:T(8,128)S(1)} %get-tuple-element.37.end_ref, f32[4,128]{1,0:T(4,128)S(1)} %get-tuple-element.38.parts_ref, f32[72,128]{1,0:T(8,128)S(1)} %get-tuple-element.39.chunks_ref), custom_call_target="tpu_custom_call" | custom-call | tf_op jit(solution)/shard_map/edge_sums/pallas_call | solution.py:611
  18.1 3.2 %all-to-all-start = ((f32[288,1,128]{2,1,0:T(1,128)}), f32[288,1,128]{2,1,0:T(1,128)S(1)}, u32[]{:S(2)}, u32[]{:S(2)}) async-start(f32[288,1,128]{2,1,0:T(1,128)} %bitcast.3), calls=%async_computation | async-start | bytes 294912 | tf_op jit(solution)/shard_map/all_to_all | solution.py:614
  21.3 1.8 %collective-permute-start.5 = (f32[32,128]{1,0:T(8,128)S(1)}, f32[32,128]{1,0:T(8,128)S(1)}, u32[]{:S(2)}, u32[]{:S(2)}) collective-permute-start(f32[32,128]{1,0:T(8,128)S(1)} %get-tuple-element.43.refs_0_), channel_id=1, source_target_pairs={{16,0},{0,16},{17,1},{1,17},{18,2},{2,18},{19,3},{3,19},{20,4},{4,... | collective-permute-start | bytes 49160 | tf_op jit(solution)/shard_map/ppermute | solution.py:521
  23.1 2.0 %collective-permute-done.5.refs_1_ = f32[32,128]{1,0:T(8,128)S(1)} collective-permute-done((f32[32,128]{1,0:T(8,128)S(1)}, f32[32,128]{1,0:T(8,128)S(1)}, u32[]{:S(2)}, u32[]{:S(2)}) %collective-permute-start.5) | collective-permute-done | bytes 16416 | tf_op jit(solution)/shard_map/ppermute | solution.py:521
  25.1 4.6 %all-to-all-done = f32[288,1,128]{2,1,0:T(1,128)S(1)} async-done(((f32[288,1,128]{2,1,0:T(1,128)}), f32[288,1,128]{2,1,0:T(1,128)S(1)}, u32[]{:S(2)}, u32[]{:S(2)}) %all-to-all-start) | async-done | bytes 147488 | tf_op jit(solution)/shard_map/all_to_all | solution.py:614
  29.7 1.0 %combine.1 = (f32[64,1024]{1,0:T(8,128)}, f32[64,1024]{1,0:T(8,128)}) custom-call(f32[288,128]{1,0:T(8,128)S(1)} %bitcast.6, f32[64,8,128]{2,1,0:T(8,128)S(1)} %get-tuple-element.27.field_ref.start_ref, f32[64,8,128]{2,1,0:T(8,128)S(1)} %get-tuple-element.40.next_ref, f32[64,8,128]{2,1,0:T(8,128)S(1)} %get-tuple-element.36.right_ref, ...), custom_call_target="tpu_custom_call" | custom-call | tf_op jit(solution)/shard_map/combine/pallas_call | solution.py:615
Async XLA Ops:
  0.6 5.8 %copy-start = (f32[64,1024]{1,0:T(8,128)S(1)}, f32[64,1024]{1,0:T(8,128)}, u32[]{:S(2)}) copy-start(f32[64,1024]{1,0:T(8,128)} %kappa_ref.1) | copy-start | bytes 786436
  2.8 5.6 %collective-permute-start = (f32[72,128]{1,0:T(8,128)S(1)}, f32[72,128]{1,0:T(8,128)S(1)}, u32[]{:S(2)}, u32[]{:S(2)}) collective-permute-start(f32[72,128]{1,0:T(8,128)S(1)} %get-tuple-element.26.refs_0_), channel_id=1, source_target_pairs={{16,0},{0,16},{17,1},{1,17},{18,2},{2,18},{19,3},{3,19},{20,4},{4,... | collective-permute-start | bytes 110600 | tf_op jit(solution)/shard_map/ppermute | solution.py:521
  8.6 7.3 %collective-permute-start.2 = (f32[5,8,128]{2,1,0:T(8,128)S(1)}, f32[5,8,128]{2,1,0:T(8,128)S(1)}, u32[]{:S(2)}, u32[]{:S(2)}) collective-permute-start(f32[5,8,128]{2,1,0:T(8,128)S(1)} %get-tuple-element.32), channel_id=1, source_target_pairs={{0,15},{1,2},{2,1},{3,4},{4,3},{5,6},{6,5},{7,8},{8,7},{9,10},{10,... | collective-permute-start | bytes 61448 | tf_op jit(solution)/shard_map/ppermute | solution.py:572
  12.1 3.8 %collective-permute-start.3 = (f32[32,128]{1,0:T(8,128)S(1)}, f32[32,128]{1,0:T(8,128)S(1)}, u32[]{:S(2)}, u32[]{:S(2)}) collective-permute-start(f32[32,128]{1,0:T(8,128)S(1)} %get-tuple-element.35.refs_0_), channel_id=1, source_target_pairs={{16,0},{0,16},{17,1},{1,17},{18,2},{2,18},{19,3},{3,19},{20,4},{4,... | collective-permute-start | bytes 49160 | tf_op jit(solution)/shard_map/ppermute | solution.py:521
  13.9 1.2 %collective-permute-start.1 = (f32[3,8,128]{2,1,0:T(8,128)S(1)}, f32[3,8,128]{2,1,0:T(8,128)S(1)}, u32[]{:S(2)}, u32[]{:S(2)}) collective-permute-start(f32[3,8,128]{2,1,0:T(8,128)S(1)} %get-tuple-element.31), channel_id=1, source_target_pairs={{0,1},{1,0},{2,3},{3,2},{4,5},{5,4},{6,7},{7,6},{8,9},{9,8},{10,11... | collective-permute-start | bytes 36872 | tf_op jit(solution)/shard_map/ppermute | solution.py:582
  16.1 1.2 %collective-permute-start.4 = (f32[2,8,128]{2,1,0:T(8,128)S(1)}, f32[2,8,128]{2,1,0:T(8,128)S(1)}, u32[]{:S(2)}, u32[]{:S(2)}) collective-permute-start(f32[2,8,128]{2,1,0:T(8,128)S(1)} %pair_edge.1), channel_id=1, source_target_pairs={{0,1},{1,0},{2,3},{3,2},{4,5},{5,4},{6,7},{7,6},{8,9},{9,8},{10,11... | collective-permute-start | bytes 24584 | tf_op jit(solution)/shard_map/ppermute | solution.py:591
  18.1 11.6 %all-to-all-start = ((f32[288,1,128]{2,1,0:T(1,128)}), f32[288,1,128]{2,1,0:T(1,128)S(1)}, u32[]{:S(2)}, u32[]{:S(2)}) async-start(f32[288,1,128]{2,1,0:T(1,128)} %bitcast.3), calls=%async_computation | async-start | bytes 294912 | tf_op jit(solution)/shard_map/all_to_all | solution.py:614
  21.3 3.8 %collective-permute-start.5 = (f32[32,128]{1,0:T(8,128)S(1)}, f32[32,128]{1,0:T(8,128)S(1)}, u32[]{:S(2)}, u32[]{:S(2)}) collective-permute-start(f32[32,128]{1,0:T(8,128)S(1)} %get-tuple-element.43.refs_0_), channel_id=1, source_target_pairs={{16,0},{0,16},{17,1},{1,17},{18,2},{2,18},{19,3},{3,19},{20,4},{4,... | collective-permute-start | bytes 49160 | tf_op jit(solution)/shard_map/ppermute | solution.py:521

commit v6 on v5

--- a/solution.py
+++ b/solution.py
@@ -151,16 +151,26 @@
         pl.when(index * CHUNK < count)(functools.partial(work, index))
 
 
-def block_kernel(kappa_ref, matrices_ref, weight_ref, shifted_ref, blocks_ref):
+def block_kernel(count_ref, kappa_ref, matrices_ref, weight_ref, shifted_ref, blocks_ref):
     shifted_ref[...] = kappa_ref[...].reshape(shifted_ref.shape) + 4.0
-    width = matrices_ref.shape[2]
-    for slot in range(matrices_ref.shape[0]):
-        matrix = matrices_ref[slot]
-        weighted = matrix.T.astype(F32) * weight_ref[pl.ds(slot, 1), :]
-        high, low = two_terms(fold_terms(dot(stacked_terms(weighted), matrix)))
-        columns = pl.ds(slot % 2 * width, width)
-        blocks_ref[slot // 2, pl.ds(0, width), columns] = high
-        blocks_ref[slot // 2, pl.ds(width, width), columns] = low
+    slots, _, width = matrices_ref.shape
+    half = max(slots // (2 * GROUP), 1) * GROUP
+
+    def work(used):
+        for slot in range(used):
+            matrix = matrices_ref[slot]
+            weighted = matrix.T.astype(F32) * weight_ref[pl.ds(slot, 1), :]
+            high, low = two_terms(fold_terms(dot(stacked_terms(weighted), matrix)))
+            columns = pl.ds(slot % 2 * width, width)
+            blocks_ref[slot // 2, pl.ds(0, width), columns] = high
+            blocks_ref[slot // 2, pl.ds(width, width), columns] = low
+        if used < slots:
+            rest = (slots - used) // 2
+            blocks_ref[pl.ds(used // 2, rest)] = jnp.zeros((rest,) + blocks_ref.shape[1:], BF16)
+
+    few = count_ref[0, 0] <= half
+    pl.when(few)(functools.partial(work, half))
+    pl.when(jnp.logical_not(few))(functools.partial(work, slots))
 
 
 def gather_messages(orbits, slots, message_refs, order_ref):
@@ -549,11 +559,11 @@
     shifted, blocks = call(
         block_kernel,
         ((field_shape, F32), ((slots // 2, 2 * width, 2 * width), BF16)),
-        [vmem] * 3,
+        [smem] + [vmem] * 3,
         (),
         "blocks",
         work=WORK,
-    )(kappa2, matrices, weights)
+    )(live_count, kappa2, matrices, weights)
 
     order = pltpu.VMEM((orbits * slots, width), F32)
     edge_width = -(-2 * orbits * slots // LANES) * LANES

time: 31.1 us -> 31 us (level)
  waiting for transfers between devices: 9.28 us -> 10.1 us
  Pallas kernels: 6.55 us -> 5.96 us
  starting transfers between devices: 13.5 us -> 13 us
    ppermute x3, waiting for transfers between devices: 3.26 us -> 4.06 us  [from_others(): lax.ppermute(value, 'orbit', [((i + step) % orbits, i) for i in range(orb...]
    pallas_call x1, Pallas kernels: 1.51 us -> 0.91 us  [per_device(): call(block_kernel, ((field_shape, F32), ((slots // 2, 2 * width, 2 * widt...]
    ppermute x3, starting transfers between devices: 7.19 us -> 6.69 us  [from_others(): lax.ppermute(value, 'orbit', [((i + step) % orbits, i) for i in range(orb...]
  transfers between devices with their start and end apart: 7 -> 7, of which waited for: 6 -> 6; matrix products, arithmetic and copies ran while one was open for 0% -> 0% of each run, Pallas kernels for 9% -> 7%
where the time goes in v6:
time: 31 us; the launch traced here: 30.5 us
  starting transfers between devices  13 us (42%)
  waiting for transfers between devices  10.1 us (33%)
  Pallas kernels  5.96 us (19%)
  between operations  1.39 us (4%)
    ppermute x3, starting transfers between devices, from_others(): lax.ppermute(value, 'orbit', [((i + step) % orbits, i) for i in range(orb...  6.69 us
    all_to_all x1, waiting for transfers between devices, per_device(): lax.all_to_all(sums[:, None], ('orbit', 'lon'), 0, 0, tiled=True)[:, 0]  4.62 us
    ppermute x3, waiting for transfers between devices, from_others(): lax.ppermute(value, 'orbit', [((i + step) % orbits, i) for i in range(orb...  4.06 us
    all_to_all x1, starting transfers between devices, per_device(): lax.all_to_all(sums[:, None], ('orbit', 'lon'), 0, 0, tiled=True)[:, 0]  3.15 us
    ppermute x1, starting transfers between devices, per_device(): rim_odd = lax.ppermute(odd, 'lon', odd_pairs)  3.13 us
    pallas_call x1, Pallas kernels, per_device(): call(functools.partial(data_kernel, orbits), (((2 * slots + GROUP, width)...  1.45 us
    ppermute x1, waiting for transfers between devices, per_device(): rim_even = lax.ppermute(even, 'lon', even_pairs)  1.18 us
    pallas_call x1, Pallas kernels, per_device(): call(functools.partial(last_kernel, parity, orbits, bands), ((kappa2.shap...  1.05 us
  transfers between devices with their start and end apart: 7, of which 6 were waited for; matrix products, arithmetic and copies ran while one was open for 0% of the time, Pallas kernels for 7%

profile of v6, /device:TPU:0, one launch (start us, length us, event | category | flops | bytes accessed | tf_op | source)
XLA Modules:
  0.0 30.5 jit_solution(5775743462113266915)
XLA Ops:
  0.6 0.0 copy-start
  1.3 1.5 %data_terms.1 = (f32[72,128]{1,0:T(8,128)S(1)}, bf16[32,256,128]{2,1,0:T(8,128)(2,1)S(1)}, f32[32,256]{1,0:T(8,128)S(1)}, bf16[32,512]{1,0:T(8,128)(2,1)S(1)}) custom-call(s32[1,1]{1,0:T(1,128)S(6)} %copy.9.count_ref, s32[32]{0:T(128)} %bitcast.8, bf16[32,256,128]{2,1,0:T(8,128)(2,1)} %bitcast.7, f32[32,1,256]{2,1,0:T(1,128)} %value_in.1, ...), custom_call_target="tpu_custom_call" | custom-call | tf_op jit(solution)/shard_map/data_terms/pallas_call | solution.py:540
  2.8 3.3 %collective-permute-start = (f32[72,128]{1,0:T(8,128)S(1)}, f32[72,128]{1,0:T(8,128)S(1)}, u32[]{:S(2)}, u32[]{:S(2)}) collective-permute-start(f32[72,128]{1,0:T(8,128)S(1)} %get-tuple-element.26.refs_0_), channel_id=1, source_target_pairs={{16,0},{0,16},{17,1},{1,17},{18,2},{2,18},{19,3},{3,19},{20,4},{4,... | collective-permute-start | bytes 110600 | tf_op jit(solution)/shard_map/ppermute | solution.py:531
  6.1 0.0 copy-done
  6.1 0.9 %blocks.1 = (f32[64,8,128]{2,1,0:T(8,128)S(1)}, bf16[16,256,256]{2,1,0:T(8,128)(2,1)S(1)}) custom-call(s32[1,1]{1,0:T(1,128)S(6)} %copy.9.count_ref, f32[64,1024]{1,0:T(8,128)S(1)} %copy-done, bf16[32,256,128]{2,1,0:T(8,128)(2,1)S(1)} %get-tuple-element.23.matrices_ref, f32[32,256]{1,0:T(8,128)S(1)} %get-tuple-element.24.weight_ref), custom_call_target="tpu_custom_call" | custom-call | flops 4294967296 | tf_op jit(solution)/shard_map/blocks/pallas_call | solution.py:559
  7.0 1.0 %collective-permute-done.refs_1_ = f32[72,128]{1,0:T(8,128)S(1)} collective-permute-done((f32[72,128]{1,0:T(8,128)S(1)}, f32[72,128]{1,0:T(8,128)S(1)}, u32[]{:S(2)}, u32[]{:S(2)}) %collective-permute-start) | collective-permute-done | bytes 36896 | tf_op jit(solution)/shard_map/ppermute | solution.py:531
  8.0 0.3 start.1
  8.3 3.1 %collective-permute-start.2 = (f32[5,8,128]{2,1,0:T(8,128)S(1)}, f32[5,8,128]{2,1,0:T(8,128)S(1)}, u32[]{:S(2)}, u32[]{:S(2)}) collective-permute-start(f32[5,8,128]{2,1,0:T(8,128)S(1)} %get-tuple-element.32), channel_id=1, source_target_pairs={{0,15},{1,2},{2,1},{3,4},{4,3},{5,6},{6,5},{7,8},{8,7},{9,10},{10,... | collective-permute-start | bytes 61448 | tf_op jit(solution)/shard_map/ppermute | solution.py:582
  11.4 0.4 %normal_start.1 = (f32[32,128]{1,0:T(8,128)S(1)}, f32[3,8,128]{2,1,0:T(8,128)S(1)}) custom-call(s32[1,1]{1,0:T(1,128)S(6)} %copy.9.count_ref, bf16[32,512]{1,0:T(8,128)(2,1)S(1)} %get-tuple-element.28.pick_ref, f32[64,8,128]{2,1,0:T(8,128)S(1)} %get-tuple-element.27.field_ref.start_ref, bf16[16,256,256]{2,1,0:T(8,128)(2,1)S(1)} %get-tuple-element.29.blocks_ref, ...), custom_call_target="tpu_custom_call" | custom-call | flops 4294967296 | tf_op jit(solution)/shard_map/normal_start/pallas_call | solution.py:583
  11.9 1.5 %collective-permute-start.3 = (f32[32,128]{1,0:T(8,128)S(1)}, f32[32,128]{1,0:T(8,128)S(1)}, u32[]{:S(2)}, u32[]{:S(2)}) collective-permute-start(f32[32,128]{1,0:T(8,128)S(1)} %get-tuple-element.35.refs_0_), channel_id=1, source_target_pairs={{16,0},{0,16},{17,1},{1,17},{18,2},{2,18},{19,3},{3,19},{20,4},{4,... | collective-permute-start | bytes 49160 | tf_op jit(solution)/shard_map/ppermute | solution.py:531
  13.4 0.0 collective-permute-start.1
  13.4 1.2 %collective-permute-done.1.even_ref.rim_ref = f32[3,8,128]{2,1,0:T(8,128)S(1)} collective-permute-done((f32[3,8,128]{2,1,0:T(8,128)S(1)}, f32[3,8,128]{2,1,0:T(8,128)S(1)}, u32[]{:S(2)}, u32[]{:S(2)}) %collective-permute-start.1) | collective-permute-done | bytes 12320 | tf_op jit(solution)/shard_map/ppermute | solution.py:592
  14.6 1.1 %collective-permute-done.3.refs_1_ = f32[32,128]{1,0:T(8,128)S(1)} collective-permute-done((f32[32,128]{1,0:T(8,128)S(1)}, f32[32,128]{1,0:T(8,128)S(1)}, u32[]{:S(2)}, u32[]{:S(2)}) %collective-permute-start.3) | collective-permute-done | bytes 16416 | tf_op jit(solution)/shard_map/ppermute | solution.py:531
  15.7 0.0 collective-permute-done.2.odd_ref
  15.7 0.2 pair_edge.1
  15.8 0.1 collective-permute-start.4
  15.9 0.9 %images.1 = (f32[64,8,128]{2,1,0:T(8,128)S(1)}, f32[64,8,128]{2,1,0:T(8,128)S(1)}, f32[64,8,128]{2,1,0:T(8,128)S(1)}, f32[8,128]{1,0:T(8,128)S(1)}, f32[4,128]{1...) custom-call(f32[64,8,128]{2,1,0:T(8,128)S(1)} %get-tuple-element.27.field_ref.start_ref, ...), custom_call_target="tpu_custom_call" | custom-call | flops 4294967296 | tf_op jit(solution)/shard_map/images/pallas_call | solution.py:603
  16.8 0.2 collective-permute-done.4.even_ref
  17.1 0.8 %edge_sums.1 = f32[288,128]{1,0:T(8,128)} custom-call(f32[2,8,128]{2,1,0:T(8,128)S(1)} %collective-permute-done.4.even_ref, f32[8,128]{1,0:T(8,128)S(1)} %get-tuple-element.37.end_ref, f32[4,128]{1,0:T(4,128)S(1)} %get-tuple-element.38.parts_ref, f32[72,128]{1,0:T(8,128)S(1)} %get-tuple-element.39.chunks_ref), custom_call_target="tpu_custom_call" | custom-call | tf_op jit(solution)/shard_map/edge_sums/pallas_call | solution.py:621
  17.8 3.1 %all-to-all-start = ((f32[288,1,128]{2,1,0:T(1,128)}), f32[288,1,128]{2,1,0:T(1,128)S(1)}, u32[]{:S(2)}, u32[]{:S(2)}) async-start(f32[288,1,128]{2,1,0:T(1,128)} %bitcast.3), calls=%async_computation | async-start | bytes 294912 | tf_op jit(solution)/shard_map/all_to_all | solution.py:624
  21.0 1.8 %collective-permute-start.5 = (f32[32,128]{1,0:T(8,128)S(1)}, f32[32,128]{1,0:T(8,128)S(1)}, u32[]{:S(2)}, u32[]{:S(2)}) collective-permute-start(f32[32,128]{1,0:T(8,128)S(1)} %get-tuple-element.43.refs_0_), channel_id=1, source_target_pairs={{16,0},{0,16},{17,1},{1,17},{18,2},{2,18},{19,3},{3,19},{20,4},{4,... | collective-permute-start | bytes 49160 | tf_op jit(solution)/shard_map/ppermute | solution.py:531
  22.8 2.0 %collective-permute-done.5.refs_1_ = f32[32,128]{1,0:T(8,128)S(1)} collective-permute-done((f32[32,128]{1,0:T(8,128)S(1)}, f32[32,128]{1,0:T(8,128)S(1)}, u32[]{:S(2)}, u32[]{:S(2)}) %collective-permute-start.5) | collective-permute-done | bytes 16416 | tf_op jit(solution)/shard_map/ppermute | solution.py:531
  24.8 4.6 %all-to-all-done = f32[288,1,128]{2,1,0:T(1,128)S(1)} async-done(((f32[288,1,128]{2,1,0:T(1,128)}), f32[288,1,128]{2,1,0:T(1,128)S(1)}, u32[]{:S(2)}, u32[]{:S(2)}) %all-to-all-start) | async-done | bytes 147488 | tf_op jit(solution)/shard_map/all_to_all | solution.py:624
  29.4 1.0 %combine.1 = (f32[64,1024]{1,0:T(8,128)}, f32[64,1024]{1,0:T(8,128)}) custom-call(f32[288,128]{1,0:T(8,128)S(1)} %bitcast.6, f32[64,8,128]{2,1,0:T(8,128)S(1)} %get-tuple-element.27.field_ref.start_ref, f32[64,8,128]{2,1,0:T(8,128)S(1)} %get-tuple-element.40.next_ref, f32[64,8,128]{2,1,0:T(8,128)S(1)} %get-tuple-element.36.right_ref, ...), custom_call_target="tpu_custom_call" | custom-call | tf_op jit(solution)/shard_map/combine/pallas_call | solution.py:625
Async XLA Ops:
  0.6 5.5 %copy-start = (f32[64,1024]{1,0:T(8,128)S(1)}, f32[64,1024]{1,0:T(8,128)}, u32[]{:S(2)}) copy-start(f32[64,1024]{1,0:T(8,128)} %kappa_ref.1) | copy-start | bytes 786436
  2.8 5.3 %collective-permute-start = (f32[72,128]{1,0:T(8,128)S(1)}, f32[72,128]{1,0:T(8,128)S(1)}, u32[]{:S(2)}, u32[]{:S(2)}) collective-permute-start(f32[72,128]{1,0:T(8,128)S(1)} %get-tuple-element.26.refs_0_), channel_id=1, source_target_pairs={{16,0},{0,16},{17,1},{1,17},{18,2},{2,18},{19,3},{3,19},{20,4},{4,... | collective-permute-start | bytes 110600 | tf_op jit(solution)/shard_map/ppermute | solution.py:531
  8.3 7.3 %collective-permute-start.2 = (f32[5,8,128]{2,1,0:T(8,128)S(1)}, f32[5,8,128]{2,1,0:T(8,128)S(1)}, u32[]{:S(2)}, u32[]{:S(2)}) collective-permute-start(f32[5,8,128]{2,1,0:T(8,128)S(1)} %get-tuple-element.32), channel_id=1, source_target_pairs={{0,15},{1,2},{2,1},{3,4},{4,3},{5,6},{6,5},{7,8},{8,7},{9,10},{10,... | collective-permute-start | bytes 61448 | tf_op jit(solution)/shard_map/ppermute | solution.py:582
  11.9 3.8 %collective-permute-start.3 = (f32[32,128]{1,0:T(8,128)S(1)}, f32[32,128]{1,0:T(8,128)S(1)}, u32[]{:S(2)}, u32[]{:S(2)}) collective-permute-start(f32[32,128]{1,0:T(8,128)S(1)} %get-tuple-element.35.refs_0_), channel_id=1, source_target_pairs={{16,0},{0,16},{17,1},{1,17},{18,2},{2,18},{19,3},{3,19},{20,4},{4,... | collective-permute-start | bytes 49160 | tf_op jit(solution)/shard_map/ppermute | solution.py:531
  13.4 1.2 %collective-permute-start.1 = (f32[3,8,128]{2,1,0:T(8,128)S(1)}, f32[3,8,128]{2,1,0:T(8,128)S(1)}, u32[]{:S(2)}, u32[]{:S(2)}) collective-permute-start(f32[3,8,128]{2,1,0:T(8,128)S(1)} %get-tuple-element.31), channel_id=1, source_target_pairs={{0,1},{1,0},{2,3},{3,2},{4,5},{5,4},{6,7},{7,6},{8,9},{9,8},{10,11... | collective-permute-start | bytes 36872 | tf_op jit(solution)/shard_map/ppermute | solution.py:592
  15.8 1.2 %collective-permute-start.4 = (f32[2,8,128]{2,1,0:T(8,128)S(1)}, f32[2,8,128]{2,1,0:T(8,128)S(1)}, u32[]{:S(2)}, u32[]{:S(2)}) collective-permute-start(f32[2,8,128]{2,1,0:T(8,128)S(1)} %pair_edge.1), channel_id=1, source_target_pairs={{0,1},{1,0},{2,3},{3,2},{4,5},{5,4},{6,7},{7,6},{8,9},{9,8},{10,11... | collective-permute-start | bytes 24584 | tf_op jit(solution)/shard_map/ppermute | solution.py:601
  17.8 11.6 %all-to-all-start = ((f32[288,1,128]{2,1,0:T(1,128)}), f32[288,1,128]{2,1,0:T(1,128)S(1)}, u32[]{:S(2)}, u32[]{:S(2)}) async-start(f32[288,1,128]{2,1,0:T(1,128)} %bitcast.3), calls=%async_computation | async-start | bytes 294912 | tf_op jit(solution)/shard_map/all_to_all | solution.py:624
  21.0 3.8 %collective-permute-start.5 = (f32[32,128]{1,0:T(8,128)S(1)}, f32[32,128]{1,0:T(8,128)S(1)}, u32[]{:S(2)}, u32[]{:S(2)}) collective-permute-start(f32[32,128]{1,0:T(8,128)S(1)} %get-tuple-element.43.refs_0_), channel_id=1, source_target_pairs={{16,0},{0,16},{17,1},{1,17},{18,2},{2,18},{19,3},{3,19},{20,4},{4,... | collective-permute-start | bytes 49160 | tf_op jit(solution)/shard_map/ppermute | solution.py:531

commit v7 on v5

--- a/solution.py
+++ b/solution.py
@@ -172,7 +172,7 @@
 
 
 def start_kernel(
-    orbits, parity, shifted_ref, *refs
+    orbits, parity, ahead, shifted_ref, pick_ref, blocks_ref, *refs
 ):
     message_refs = refs[:orbits]
     (
@@ -182,6 +182,7 @@
         scatter_ref,
         even_ref,
         odd_ref,
+        out_ref,
         order_ref,
     ) = refs[orbits:]
     slots = (message_refs[0].shape[0] - GROUP) // 2
@@ -211,20 +212,29 @@
     bottom = jnp.concatenate([field[columns - 2 :], shifted[columns - 1 :]], axis=0)
     store_edges(parity, top, bottom, even_ref, odd_ref)
 
+    @pl.when(ahead())
+    def _():
+        normal_slots(pick_ref, field_ref[...], blocks_ref, out_ref)
+
 
 def normal_kernel(
-    count_ref, pick_ref, field_ref, blocks_ref, even_ref, out_ref, even_out_ref
+    ahead, count_ref, pick_ref, field_ref, blocks_ref, even_ref, done_ref, out_ref, even_out_ref
 ):
     even_out_ref[...] = even_ref[...]
+    first = ahead()
     slots = pick_ref.shape[0]
     half = max(slots // (2 * GROUP), 1) * GROUP
     few = count_ref[0, 0] <= half
 
-    @pl.when(few)
+    @pl.when(first)
+    def _():
+        out_ref[...] = done_ref[...]
+
+    @pl.when(jnp.logical_and(jnp.logical_not(first), few))
     def _():
         normal_slots(pick_ref, field_ref[...], blocks_ref, out_ref, half)
 
-    @pl.when(jnp.logical_not(few))
+    @pl.when(jnp.logical_not(jnp.logical_or(first, few)))
     def _():
         normal_slots(pick_ref, field_ref[...], blocks_ref, out_ref)
 
@@ -498,6 +508,9 @@
     def parity():
         return lax.rem(lax.axis_index("lon"), 2) == 1
 
+    def ahead():
+        return lax.axis_index("lon") == 0
+
     vmem = pl.BlockSpec(memory_space=pltpu.VMEM)
     smem = pl.BlockSpec(memory_space=pltpu.SMEM)
     anywhere = pl.BlockSpec(memory_space=pl.ANY)
@@ -562,22 +575,22 @@
     wide_edge = ((max(slots // pieces + 1, rim[0][0]), pieces, width), F32)
     field = (field_shape, F32)
     slot_terms = ((slots, width), F32)
-    start, right_side, precond, scatter, even, odd = call(
-        functools.partial(start_kernel, orbits, parity),
-        (field, field, field, ((cells, edge_width), BF16), rim, wide_edge),
-        [vmem] * (1 + orbits),
+    start, right_side, precond, scatter, even, odd, terms = call(
+        functools.partial(start_kernel, orbits, parity, ahead),
+        (field, field, field, ((cells, edge_width), BF16), rim, wide_edge, slot_terms),
+        [vmem] * (3 + orbits),
         [order],
         "start",
-    )(shifted, *messages)
+    )(shifted, pick, blocks, *messages)
     rim_odd = lax.ppermute(odd, "lon", odd_pairs)
     terms, even = call(
-        normal_kernel,
+        functools.partial(normal_kernel, ahead),
         (slot_terms, rim),
-        [smem] + [vmem] * 4,
+        [smem] + [vmem] * 5,
         (),
         "normal_start",
         work=WORK,
-    )(live_count, pick, start, blocks, even)
+    )(live_count, pick, start, blocks, even, terms)
     terms = from_others(terms)
     rim_even = lax.ppermute(even, "lon", even_pairs)
     image_inputs = (start, shifted, rim_even, rim_odd, scatter, precond, *terms)

time: 31.1 us -> 31.7 us (1.019); the launches traced: 30.8 us -> 31.9 us
  Pallas kernels: 6.55 us -> 7.32 us
  starting transfers between devices: 13.5 us -> 14.2 us
    all_to_all x1, starting transfers between devices: 3.2 us -> 4.1 us  [per_device(): lax.all_to_all(sums[:, None], ('orbit', 'lon'), 0, 0, tiled=True)[:, 0]]
    ppermute x3, starting transfers between devices: 7.19 us -> 6.5 us  [from_others(): lax.ppermute(value, 'orbit', [((i + step) % orbits, i) for i in range(orb...]
    pallas_call x1, Pallas kernels: 1.45 us -> 2.08 us  [per_device(): call(functools.partial(data_kernel, orbits), (((2 * slots + GROUP, width)...]
    ppermute x1, starting transfers between devices: 3.08 us -> 3.51 us  [per_device(): rim_odd = lax.ppermute(odd, 'lon', odd_pairs)]
  transfers between devices with their start and end apart: 7 -> 7, of which waited for: 6 -> 6; matrix products, arithmetic and copies ran while one was open for 0% -> 0% of each run, Pallas kernels for 9% -> 8%
where the time goes in v7:
time: 31.7 us; the launch traced here: 31.9 us
  starting transfers between devices  14.2 us (45%)
  waiting for transfers between devices  8.99 us (28%)
  Pallas kernels  7.32 us (23%)
  between operations  1.38 us (4%)
    ppermute x3, starting transfers between devices, from_others(): lax.ppermute(value, 'orbit', [((i + step) % orbits, i) for i in range(orb...  6.5 us
    all_to_all x1, waiting for transfers between devices, per_device(): lax.all_to_all(sums[:, None], ('orbit', 'lon'), 0, 0, tiled=True)[:, 0]  4.62 us
    all_to_all x1, starting transfers between devices, per_device(): lax.all_to_all(sums[:, None], ('orbit', 'lon'), 0, 0, tiled=True)[:, 0]  4.1 us
    ppermute x1, starting transfers between devices, per_device(): rim_odd = lax.ppermute(odd, 'lon', odd_pairs)  3.51 us
    ppermute x3, waiting for transfers between devices, from_others(): lax.ppermute(value, 'orbit', [((i + step) % orbits, i) for i in range(orb...  2.97 us
    pallas_call x1, Pallas kernels, per_device(): call(functools.partial(data_kernel, orbits), (((2 * slots + GROUP, width)...  2.08 us
    pallas_call x1, Pallas kernels, per_device(): call(block_kernel, ((field_shape, F32), ((slots // 2, 2 * width, 2 * widt...  1.51 us
    ppermute x1, waiting for transfers between devices, per_device(): rim_even = lax.ppermute(even, 'lon', even_pairs)  1.18 us
  transfers between devices with their start and end apart: 7, of which 6 were waited for; matrix products, arithmetic and copies ran while one was open for 0% of the time, Pallas kernels for 8%

profile of v7, /device:TPU:0, one launch (start us, length us, event | category | flops | bytes accessed | tf_op | source)
XLA Modules:
  0.0 31.9 jit_solution(13275535471838549586)
XLA Ops:
  0.6 0.0 copy-start
  1.3 2.1 %data_terms.1 = (f32[72,128]{1,0:T(8,128)S(1)}, bf16[32,256,128]{2,1,0:T(8,128)(2,1)S(1)}, f32[32,256]{1,0:T(8,128)S(1)}, bf16[32,512]{1,0:T(8,128)(2,1)S(1)}) custom-call(s32[1,1]{1,0:T(1,128)S(6)} %copy.9.count_ref, s32[32]{0:T(128)} %bitcast.8, bf16[32,256,128]{2,1,0:T(8,128)(2,1)} %bitcast.7, f32[32,1,256]{2,1,0:T(1,128)} %value_in.1, ...), custom_call_target="tpu_custom_call" | custom-call | tf_op jit(solution)/shard_map/data_terms/pallas_call | solution.py:543
  3.4 2.7 %collective-permute-start = (f32[72,128]{1,0:T(8,128)S(1)}, f32[72,128]{1,0:T(8,128)S(1)}, u32[]{:S(2)}, u32[]{:S(2)}) collective-permute-start(f32[72,128]{1,0:T(8,128)S(1)} %get-tuple-element.29.refs_0_), channel_id=1, source_target_pairs={{16,0},{0,16},{17,1},{1,17},{18,2},{2,18},{19,3},{3,19},{20,4},{4,... | collective-permute-start | bytes 110600 | tf_op jit(solution)/shard_map/ppermute | solution.py:534
  6.1 0.0 copy-done
  6.1 1.5 %blocks.1 = (f32[64,8,128]{2,1,0:T(8,128)S(1)}, bf16[16,256,256]{2,1,0:T(8,128)(2,1)S(1)}) custom-call(f32[64,1024]{1,0:T(8,128)S(1)} %copy-done, bf16[32,256,128]{2,1,0:T(8,128)(2,1)S(1)} %get-tuple-element.24.matrices_ref, f32[32,256]{1,0:T(8,128)S(1)} %get-tuple-element.25.weight_ref), custom_call_target="tpu_custom_call" | custom-call | flops 4294967296 | tf_op jit(solution)/shard_map/blocks/pallas_call | solution.py:562
  7.6 0.4 %collective-permute-done.refs_1_ = f32[72,128]{1,0:T(8,128)S(1)} collective-permute-done((f32[72,128]{1,0:T(8,128)S(1)}, f32[72,128]{1,0:T(8,128)S(1)}, u32[]{:S(2)}, u32[]{:S(2)}) %collective-permute-start) | collective-permute-done | bytes 36896 | tf_op jit(solution)/shard_map/ppermute | solution.py:534
  8.0 0.8 %start.1 = (f32[64,8,128]{2,1,0:T(8,128)S(1)}, f32[64,8,128]{2,1,0:T(8,128)S(1)}, f32[64,8,128]{2,1,0:T(8,128)S(1)}, bf16[512,128]{1,0:T(8,128)(2,1)S(1)}, f32[3...) custom-call(f32[64,8,128]{2,1,0:T(8,128)S(1)} %get-tuple-element.26.shifted_ref, ...), custom_call_target="tpu_custom_call" | custom-call | tf_op jit(solution)/shard_map/start/pallas_call | solution.py:578
  8.9 3.5 %collective-permute-start.2 = (f32[5,8,128]{2,1,0:T(8,128)S(1)}, f32[5,8,128]{2,1,0:T(8,128)S(1)}, u32[]{:S(2)}, u32[]{:S(2)}) collective-permute-start(f32[5,8,128]{2,1,0:T(8,128)S(1)} %get-tuple-element.34), channel_id=1, source_target_pairs={{0,15},{1,2},{2,1},{3,4},{4,3},{5,6},{6,5},{7,8},{8,7},{9,10},{10,... | collective-permute-start | bytes 61448 | tf_op jit(solution)/shard_map/ppermute | solution.py:585
  12.4 2.0 %collective-permute-start.3 = (f32[32,128]{1,0:T(8,128)S(1)}, f32[32,128]{1,0:T(8,128)S(1)}, u32[]{:S(2)}, u32[]{:S(2)}) collective-permute-start(f32[32,128]{1,0:T(8,128)S(1)} %get-tuple-element.37.refs_0_), channel_id=1, source_target_pairs={{16,0},{0,16},{17,1},{1,17},{18,2},{2,18},{19,3},{3,19},{20,4},{4,... | collective-permute-start | bytes 49160 | tf_op jit(solution)/shard_map/ppermute | solution.py:534
  14.4 0.0 collective-permute-start.1
  14.4 1.2 %collective-permute-done.1.even_ref.rim_ref = f32[3,8,128]{2,1,0:T(8,128)S(1)} collective-permute-done((f32[3,8,128]{2,1,0:T(8,128)S(1)}, f32[3,8,128]{2,1,0:T(8,128)S(1)}, u32[]{:S(2)}, u32[]{:S(2)}) %collective-permute-start.1) | collective-permute-done | bytes 12320 | tf_op jit(solution)/shard_map/ppermute | solution.py:595
  15.5 0.6 %collective-permute-done.3.refs_1_ = f32[32,128]{1,0:T(8,128)S(1)} collective-permute-done((f32[32,128]{1,0:T(8,128)S(1)}, f32[32,128]{1,0:T(8,128)S(1)}, u32[]{:S(2)}, u32[]{:S(2)}) %collective-permute-start.3) | collective-permute-done | bytes 16416 | tf_op jit(solution)/shard_map/ppermute | solution.py:534
  16.1 0.0 collective-permute-done.2.odd_ref
  16.1 0.2 pair_edge.1
  16.3 0.1 collective-permute-start.4
  16.4 0.9 %images.1 = (f32[64,8,128]{2,1,0:T(8,128)S(1)}, f32[64,8,128]{2,1,0:T(8,128)S(1)}, f32[64,8,128]{2,1,0:T(8,128)S(1)}, f32[8,128]{1,0:T(8,128)S(1)}, f32[4,128]{1...) custom-call(f32[64,8,128]{2,1,0:T(8,128)S(1)} %get-tuple-element.30.field_ref.start_ref, ...), custom_call_target="tpu_custom_call" | custom-call | flops 4294967296 | tf_op jit(solution)/shard_map/images/pallas_call | solution.py:606
  17.3 0.2 collective-permute-done.4.even_ref
  17.5 0.8 %edge_sums.1 = f32[288,128]{1,0:T(8,128)} custom-call(f32[2,8,128]{2,1,0:T(8,128)S(1)} %collective-permute-done.4.even_ref, f32[8,128]{1,0:T(8,128)S(1)} %get-tuple-element.39.end_ref, f32[4,128]{1,0:T(4,128)S(1)} %get-tuple-element.40.parts_ref, f32[72,128]{1,0:T(8,128)S(1)} %get-tuple-element.41.chunks_ref), custom_call_target="tpu_custom_call" | custom-call | tf_op jit(solution)/shard_map/edge_sums/pallas_call | solution.py:624
  18.3 4.1 %all-to-all-start = ((f32[288,1,128]{2,1,0:T(1,128)}), f32[288,1,128]{2,1,0:T(1,128)S(1)}, u32[]{:S(2)}, u32[]{:S(2)}) async-start(f32[288,1,128]{2,1,0:T(1,128)} %bitcast.3), calls=%async_computation | async-start | bytes 294912 | tf_op jit(solution)/shard_map/all_to_all | solution.py:627
  22.4 1.8 %collective-permute-start.5 = (f32[32,128]{1,0:T(8,128)S(1)}, f32[32,128]{1,0:T(8,128)S(1)}, u32[]{:S(2)}, u32[]{:S(2)}) collective-permute-start(f32[32,128]{1,0:T(8,128)S(1)} %get-tuple-element.45.refs_0_), channel_id=1, source_target_pairs={{16,0},{0,16},{17,1},{1,17},{18,2},{2,18},{19,3},{3,19},{20,4},{4,... | collective-permute-start | bytes 49160 | tf_op jit(solution)/shard_map/ppermute | solution.py:534
  24.2 2.0 %collective-permute-done.5.refs_1_ = f32[32,128]{1,0:T(8,128)S(1)} collective-permute-done((f32[32,128]{1,0:T(8,128)S(1)}, f32[32,128]{1,0:T(8,128)S(1)}, u32[]{:S(2)}, u32[]{:S(2)}) %collective-permute-start.5) | collective-permute-done | bytes 16416 | tf_op jit(solution)/shard_map/ppermute | solution.py:534
  26.2 4.6 %all-to-all-done = f32[288,1,128]{2,1,0:T(1,128)S(1)} async-done(((f32[288,1,128]{2,1,0:T(1,128)}), f32[288,1,128]{2,1,0:T(1,128)S(1)}, u32[]{:S(2)}, u32[]{:S(2)}) %all-to-all-start) | async-done | bytes 147488 | tf_op jit(solution)/shard_map/all_to_all | solution.py:627
  30.8 1.0 %combine.1 = (f32[64,1024]{1,0:T(8,128)}, f32[64,1024]{1,0:T(8,128)}) custom-call(f32[288,128]{1,0:T(8,128)S(1)} %bitcast.6, f32[64,8,128]{2,1,0:T(8,128)S(1)} %get-tuple-element.30.field_ref.start_ref, f32[64,8,128]{2,1,0:T(8,128)S(1)} %get-tuple-element.42.next_ref, f32[64,8,128]{2,1,0:T(8,128)S(1)} %get-tuple-element.38.right_ref, ...), custom_call_target="tpu_custom_call" | custom-call | tf_op jit(solution)/shard_map/combine/pallas_call | solution.py:628
  (1 shorter events, 0.0 us)
Async XLA Ops:
  0.6 5.5 %copy-start = (f32[64,1024]{1,0:T(8,128)S(1)}, f32[64,1024]{1,0:T(8,128)}, u32[]{:S(2)}) copy-start(f32[64,1024]{1,0:T(8,128)} %kappa_ref.1) | copy-start | bytes 786436
  3.4 4.6 %collective-permute-start = (f32[72,128]{1,0:T(8,128)S(1)}, f32[72,128]{1,0:T(8,128)S(1)}, u32[]{:S(2)}, u32[]{:S(2)}) collective-permute-start(f32[72,128]{1,0:T(8,128)S(1)} %get-tuple-element.29.refs_0_), channel_id=1, source_target_pairs={{16,0},{0,16},{17,1},{1,17},{18,2},{2,18},{19,3},{3,19},{20,4},{4,... | collective-permute-start | bytes 110600 | tf_op jit(solution)/shard_map/ppermute | solution.py:534
  8.9 7.3 %collective-permute-start.2 = (f32[5,8,128]{2,1,0:T(8,128)S(1)}, f32[5,8,128]{2,1,0:T(8,128)S(1)}, u32[]{:S(2)}, u32[]{:S(2)}) collective-permute-start(f32[5,8,128]{2,1,0:T(8,128)S(1)} %get-tuple-element.34), channel_id=1, source_target_pairs={{0,15},{1,2},{2,1},{3,4},{4,3},{5,6},{6,5},{7,8},{8,7},{9,10},{10,... | collective-permute-start | bytes 61448 | tf_op jit(solution)/shard_map/ppermute | solution.py:585
  12.4 3.7 %collective-permute-start.3 = (f32[32,128]{1,0:T(8,128)S(1)}, f32[32,128]{1,0:T(8,128)S(1)}, u32[]{:S(2)}, u32[]{:S(2)}) collective-permute-start(f32[32,128]{1,0:T(8,128)S(1)} %get-tuple-element.37.refs_0_), channel_id=1, source_target_pairs={{16,0},{0,16},{17,1},{1,17},{18,2},{2,18},{19,3},{3,19},{20,4},{4,... | collective-permute-start | bytes 49160 | tf_op jit(solution)/shard_map/ppermute | solution.py:534
  14.4 1.2 %collective-permute-start.1 = (f32[3,8,128]{2,1,0:T(8,128)S(1)}, f32[3,8,128]{2,1,0:T(8,128)S(1)}, u32[]{:S(2)}, u32[]{:S(2)}) collective-permute-start(f32[3,8,128]{2,1,0:T(8,128)S(1)} %get-tuple-element.33), channel_id=1, source_target_pairs={{0,1},{1,0},{2,3},{3,2},{4,5},{5,4},{6,7},{7,6},{8,9},{9,8},{10,11... | collective-permute-start | bytes 36872 | tf_op jit(solution)/shard_map/ppermute | solution.py:595
  16.3 1.2 %collective-permute-start.4 = (f32[2,8,128]{2,1,0:T(8,128)S(1)}, f32[2,8,128]{2,1,0:T(8,128)S(1)}, u32[]{:S(2)}, u32[]{:S(2)}) collective-permute-start(f32[2,8,128]{2,1,0:T(8,128)S(1)} %pair_edge.1), channel_id=1, source_target_pairs={{0,1},{1,0},{2,3},{3,2},{4,5},{5,4},{6,7},{7,6},{8,9},{9,8},{10,11... | collective-permute-start | bytes 24584 | tf_op jit(solution)/shard_map/ppermute | solution.py:604
  18.3 12.5 %all-to-all-start = ((f32[288,1,128]{2,1,0:T(1,128)}), f32[288,1,128]{2,1,0:T(1,128)S(1)}, u32[]{:S(2)}, u32[]{:S(2)}) async-start(f32[288,1,128]{2,1,0:T(1,128)} %bitcast.3), calls=%async_computation | async-start | bytes 294912 | tf_op jit(solution)/shard_map/all_to_all | solution.py:627
  22.4 3.8 %collective-permute-start.5 = (f32[32,128]{1,0:T(8,128)S(1)}, f32[32,128]{1,0:T(8,128)S(1)}, u32[]{:S(2)}, u32[]{:S(2)}) collective-permute-start(f32[32,128]{1,0:T(8,128)S(1)} %get-tuple-element.45.refs_0_), channel_id=1, source_target_pairs={{16,0},{0,16},{17,1},{1,17},{18,2},{2,18},{19,3},{3,19},{20,4},{4,... | collective-permute-start | bytes 49160 | tf_op jit(solution)/shard_map/ppermute | solution.py:534

commit v8 on v5

--- a/solution.py
+++ b/solution.py
@@ -395,7 +395,9 @@
     chunks_ref[...] = chunks_of(jnp.concatenate([edge, jnp.zeros((1, LANES), F32)], axis=0))
 
 
-def edge_kernel(parity, even_ref, end_ref, parts_ref, chunks_ref, message_ref):
+def edge_kernel(
+    parity, even_ref, end_ref, parts_ref, chunks_ref, message_ref, filled_ref, sems
+):
     near, _ = near_far(parity, even_ref)
     own = jnp.where(lax.axis_index("orbit") == 0, PRIOR_WEIGHT, 0.0)
     more = own * jnp.sum(near * (near - 2.0 * end_ref[...]), axis=0, keepdims=True)
@@ -406,9 +408,17 @@
     rows = chunks_ref.shape[0]
     period = rows // GROUP
     row = lax.broadcasted_iota(jnp.int32, (rows, LANES), 0)
-    chunks = jnp.where(lax.rem(row, period) == period - 1, line, chunks_ref[...])
-    for index in range(message_ref.shape[0] // rows):
-        message_ref[pl.ds(index * rows, rows), :] = chunks
+    filled_ref[...] = jnp.where(lax.rem(row, period) == period - 1, line, chunks_ref[...])
+    copies = [
+        pltpu.make_async_copy(
+            filled_ref, message_ref.at[pl.ds(index * rows, rows)], sems.at[index]
+        )
+        for index in range(message_ref.shape[0] // rows)
+    ]
+    for copy in copies:
+        copy.start()
+    for copy in copies:
+        copy.wait()
 
 
 def last_kernel(
@@ -509,7 +519,7 @@
             kernel,
             out_shape=tuple(held(shape, dtype) for shape, dtype in outs),
             in_specs=in_specs,
-            out_specs=tuple(vmem for _ in outs),
+            out_specs=tuple(anywhere if name == "edge_sums" else vmem for _ in outs),
             scratch_shapes=list(scratch),
             compiler_params=pltpu.CompilerParams(vmem_limit_bytes=limit),
             cost_estimate=cost,
@@ -609,7 +619,14 @@
     terms = from_others(terms)
     message = ((orbits * bands * chunk, width), F32)
     (sums,) = call(
-        functools.partial(edge_kernel, parity), (message,), [vmem] * 4, (), "edge_sums"
+        functools.partial(edge_kernel, parity),
+        (message,),
+        [vmem] * 4,
+        [
+            pltpu.VMEM((GROUP * chunk, width), F32),
+            pltpu.SemaphoreType.DMA((orbits * bands // GROUP,)),
+        ],
+        "edge_sums",
     )(even, end, parts, chunks)
     sums = lax.all_to_all(sums[:, None], ("orbit", "lon"), 0, 0, tiled=True)[:, 0]
     return call(

time: 31.1 us -> 31 us (level)
  starting transfers between devices: 13.5 us -> 12.4 us
  Pallas kernels: 6.55 us -> 7.33 us
  waiting for transfers between devices: 9.28 us -> 9.71 us
    ppermute x3, starting transfers between devices: 7.19 us -> 5.98 us  [from_others(): lax.ppermute(value, 'orbit', [((i + step) % orbits, i) for i in range(orb...]
    pallas_call x1, Pallas kernels: 1.45 us -> 2.08 us  [per_device(): call(functools.partial(data_kernel, orbits), (((2 * slots + GROUP, width)...]
    ppermute x3, waiting for transfers between devices: 3.26 us -> 3.69 us  [from_others(): lax.ppermute(value, 'orbit', [((i + step) % orbits, i) for i in range(orb...]
  transfers between devices with their start and end apart: 7 -> 7, of which waited for: 6 -> 6; matrix products, arithmetic and copies ran while one was open for 0% -> 0% of each run, Pallas kernels for 9% -> 10%
where the time goes in v8:
time: 31 us; the launch traced here: 30.8 us
  starting transfers between devices  12.4 us (40%)
  waiting for transfers between devices  9.71 us (31%)
  Pallas kernels  7.33 us (24%)
  between operations  1.4 us (5%)
    ppermute x3, starting transfers between devices, from_others(): lax.ppermute(value, 'orbit', [((i + step) % orbits, i) for i in range(orb...  5.98 us
    all_to_all x1, waiting for transfers between devices, per_device(): lax.all_to_all(sums[:, None], ('orbit', 'lon'), 0, 0, tiled=True)[:, 0]  4.62 us
    ppermute x3, waiting for transfers between devices, from_others(): lax.ppermute(value, 'orbit', [((i + step) % orbits, i) for i in range(orb...  3.69 us
    ppermute x1, starting transfers between devices, per_device(): rim_odd = lax.ppermute(odd, 'lon', odd_pairs)  3.22 us
    all_to_all x1, starting transfers between devices, per_device(): lax.all_to_all(sums[:, None], ('orbit', 'lon'), 0, 0, tiled=True)[:, 0]  3.08 us
    pallas_call x1, Pallas kernels, per_device(): call(functools.partial(data_kernel, orbits), (((2 * slots + GROUP, width)...  2.08 us
    pallas_call x1, Pallas kernels, per_device(): call(block_kernel, ((field_shape, F32), ((slots // 2, 2 * width, 2 * widt...  1.51 us
    ppermute x1, waiting for transfers between devices, per_device(): rim_even = lax.ppermute(even, 'lon', even_pairs)  1.18 us
  transfers between devices with their start and end apart: 7, of which 6 were waited for; matrix products, arithmetic and copies ran while one was open for 0% of the time, Pallas kernels for 10%

profile of v8, /device:TPU:0, one launch (start us, length us, event | category | flops | bytes accessed | tf_op | source)
XLA Modules:
  0.0 30.8 jit_solution(11909166765741759882)
XLA Ops:
  0.6 0.0 copy-start
  1.3 2.1 %data_terms.1 = (f32[72,128]{1,0:T(8,128)S(1)}, bf16[32,256,128]{2,1,0:T(8,128)(2,1)S(1)}, f32[32,256]{1,0:T(8,128)S(1)}, bf16[32,512]{1,0:T(8,128)(2,1)S(1)}) custom-call(s32[1,1]{1,0:T(1,128)S(6)} %copy.9.count_ref, s32[32]{0:T(128)} %bitcast.8, bf16[32,256,128]{2,1,0:T(8,128)(2,1)} %bitcast.7, f32[32,1,256]{2,1,0:T(1,128)} %value_in.1, ...), custom_call_target="tpu_custom_call" | custom-call | tf_op jit(solution)/shard_map/data_terms/pallas_call | solution.py:540
  3.4 2.7 %collective-permute-start = (f32[72,128]{1,0:T(8,128)S(1)}, f32[72,128]{1,0:T(8,128)S(1)}, u32[]{:S(2)}, u32[]{:S(2)}) collective-permute-start(f32[72,128]{1,0:T(8,128)S(1)} %get-tuple-element.26.refs_0_), channel_id=1, source_target_pairs={{16,0},{0,16},{17,1},{1,17},{18,2},{2,18},{19,3},{3,19},{20,4},{4,... | collective-permute-start | bytes 110600 | tf_op jit(solution)/shard_map/ppermute | solution.py:531
  6.1 0.0 copy-done
  6.1 1.5 %blocks.1 = (f32[64,8,128]{2,1,0:T(8,128)S(1)}, bf16[16,256,256]{2,1,0:T(8,128)(2,1)S(1)}) custom-call(f32[64,1024]{1,0:T(8,128)S(1)} %copy-done, bf16[32,256,128]{2,1,0:T(8,128)(2,1)S(1)} %get-tuple-element.23.matrices_ref, f32[32,256]{1,0:T(8,128)S(1)} %get-tuple-element.24.weight_ref), custom_call_target="tpu_custom_call" | custom-call | flops 4294967296 | tf_op jit(solution)/shard_map/blocks/pallas_call | solution.py:559
  7.6 0.6 %collective-permute-done.refs_1_ = f32[72,128]{1,0:T(8,128)S(1)} collective-permute-done((f32[72,128]{1,0:T(8,128)S(1)}, f32[72,128]{1,0:T(8,128)S(1)}, u32[]{:S(2)}, u32[]{:S(2)}) %collective-permute-start) | collective-permute-done | bytes 36896 | tf_op jit(solution)/shard_map/ppermute | solution.py:531
  8.2 0.3 start.1
  8.5 3.2 %collective-permute-start.2 = (f32[5,8,128]{2,1,0:T(8,128)S(1)}, f32[5,8,128]{2,1,0:T(8,128)S(1)}, u32[]{:S(2)}, u32[]{:S(2)}) collective-permute-start(f32[5,8,128]{2,1,0:T(8,128)S(1)} %get-tuple-element.32), channel_id=1, source_target_pairs={{0,15},{1,2},{2,1},{3,4},{4,3},{5,6},{6,5},{7,8},{8,7},{9,10},{10,... | collective-permute-start | bytes 61448 | tf_op jit(solution)/shard_map/ppermute | solution.py:582
  11.7 0.6 %normal_start.1 = (f32[32,128]{1,0:T(8,128)S(1)}, f32[3,8,128]{2,1,0:T(8,128)S(1)}) custom-call(s32[1,1]{1,0:T(1,128)S(6)} %copy.9.count_ref, bf16[32,512]{1,0:T(8,128)(2,1)S(1)} %get-tuple-element.28.pick_ref, f32[64,8,128]{2,1,0:T(8,128)S(1)} %get-tuple-element.27.field_ref.start_ref, bf16[16,256,256]{2,1,0:T(8,128)(2,1)S(1)} %get-tuple-element.29.blocks_ref, ...), custom_call_target="tpu_custom_call" | custom-call | flops 4294967296 | tf_op jit(solution)/shard_map/normal_start/pallas_call | solution.py:583
  12.3 1.5 %collective-permute-start.3 = (f32[32,128]{1,0:T(8,128)S(1)}, f32[32,128]{1,0:T(8,128)S(1)}, u32[]{:S(2)}, u32[]{:S(2)}) collective-permute-start(f32[32,128]{1,0:T(8,128)S(1)} %get-tuple-element.35.refs_0_), channel_id=1, source_target_pairs={{16,0},{0,16},{17,1},{1,17},{18,2},{2,18},{19,3},{3,19},{20,4},{4,... | collective-permute-start | bytes 49160 | tf_op jit(solution)/shard_map/ppermute | solution.py:531
  13.7 0.0 collective-permute-start.1
  13.7 1.2 %collective-permute-done.1.even_ref.rim_ref = f32[3,8,128]{2,1,0:T(8,128)S(1)} collective-permute-done((f32[3,8,128]{2,1,0:T(8,128)S(1)}, f32[3,8,128]{2,1,0:T(8,128)S(1)}, u32[]{:S(2)}, u32[]{:S(2)}) %collective-permute-start.1) | collective-permute-done | bytes 12320 | tf_op jit(solution)/shard_map/ppermute | solution.py:592
  14.9 1.1 %collective-permute-done.3.refs_1_ = f32[32,128]{1,0:T(8,128)S(1)} collective-permute-done((f32[32,128]{1,0:T(8,128)S(1)}, f32[32,128]{1,0:T(8,128)S(1)}, u32[]{:S(2)}, u32[]{:S(2)}) %collective-permute-start.3) | collective-permute-done | bytes 16416 | tf_op jit(solution)/shard_map/ppermute | solution.py:531
  16.0 0.0 collective-permute-done.2.odd_ref
  16.1 0.2 pair_edge.1
  16.2 0.1 collective-permute-start.4
  16.3 0.9 %images.1 = (f32[64,8,128]{2,1,0:T(8,128)S(1)}, f32[64,8,128]{2,1,0:T(8,128)S(1)}, f32[64,8,128]{2,1,0:T(8,128)S(1)}, f32[8,128]{1,0:T(8,128)S(1)}, f32[4,128]{1...) custom-call(f32[64,8,128]{2,1,0:T(8,128)S(1)} %get-tuple-element.27.field_ref.start_ref, ...), custom_call_target="tpu_custom_call" | custom-call | flops 4294967296 | tf_op jit(solution)/shard_map/images/pallas_call | solution.py:603
  17.2 0.2 collective-permute-done.4.even_ref
  17.4 0.8 %edge_sums.1 = f32[288,128]{1,0:T(8,128)} custom-call(f32[2,8,128]{2,1,0:T(8,128)S(1)} %collective-permute-done.4.even_ref, f32[8,128]{1,0:T(8,128)S(1)} %get-tuple-element.37.end_ref, f32[4,128]{1,0:T(4,128)S(1)} %get-tuple-element.38.parts_ref, f32[72,128]{1,0:T(8,128)S(1)} %get-tuple-element.39.chunks_ref), custom_call_target="tpu_custom_call" | custom-call | tf_op jit(solution)/shard_map/edge_sums/pallas_call | solution.py:621
  18.3 3.1 %all-to-all-start = ((f32[288,1,128]{2,1,0:T(1,128)}), f32[288,1,128]{2,1,0:T(1,128)S(1)}, u32[]{:S(2)}, u32[]{:S(2)}) async-start(f32[288,1,128]{2,1,0:T(1,128)} %bitcast.3), calls=%async_computation | async-start | bytes 294912 | tf_op jit(solution)/shard_map/all_to_all | solution.py:631
  21.3 1.8 %collective-permute-start.5 = (f32[32,128]{1,0:T(8,128)S(1)}, f32[32,128]{1,0:T(8,128)S(1)}, u32[]{:S(2)}, u32[]{:S(2)}) collective-permute-start(f32[32,128]{1,0:T(8,128)S(1)} %get-tuple-element.43.refs_0_), channel_id=1, source_target_pairs={{16,0},{0,16},{17,1},{1,17},{18,2},{2,18},{19,3},{3,19},{20,4},{4,... | collective-permute-start | bytes 49160 | tf_op jit(solution)/shard_map/ppermute | solution.py:531
  23.2 2.0 %collective-permute-done.5.refs_1_ = f32[32,128]{1,0:T(8,128)S(1)} collective-permute-done((f32[32,128]{1,0:T(8,128)S(1)}, f32[32,128]{1,0:T(8,128)S(1)}, u32[]{:S(2)}, u32[]{:S(2)}) %collective-permute-start.5) | collective-permute-done | bytes 16416 | tf_op jit(solution)/shard_map/ppermute | solution.py:531
  25.1 4.6 %all-to-all-done = f32[288,1,128]{2,1,0:T(1,128)S(1)} async-done(((f32[288,1,128]{2,1,0:T(1,128)}), f32[288,1,128]{2,1,0:T(1,128)S(1)}, u32[]{:S(2)}, u32[]{:S(2)}) %all-to-all-start) | async-done | bytes 147488 | tf_op jit(solution)/shard_map/all_to_all | solution.py:631
  29.8 1.0 %combine.1 = (f32[64,1024]{1,0:T(8,128)}, f32[64,1024]{1,0:T(8,128)}) custom-call(f32[288,128]{1,0:T(8,128)S(1)} %bitcast.6, f32[64,8,128]{2,1,0:T(8,128)S(1)} %get-tuple-element.27.field_ref.start_ref, f32[64,8,128]{2,1,0:T(8,128)S(1)} %get-tuple-element.40.next_ref, f32[64,8,128]{2,1,0:T(8,128)S(1)} %get-tuple-element.36.right_ref, ...), custom_call_target="tpu_custom_call" | custom-call | tf_op jit(solution)/shard_map/combine/pallas_call | solution.py:632
Async XLA Ops:
  0.6 5.5 %copy-start = (f32[64,1024]{1,0:T(8,128)S(1)}, f32[64,1024]{1,0:T(8,128)}, u32[]{:S(2)}) copy-start(f32[64,1024]{1,0:T(8,128)} %kappa_ref.1) | copy-start | bytes 786436
  3.4 4.8 %collective-permute-start = (f32[72,128]{1,0:T(8,128)S(1)}, f32[72,128]{1,0:T(8,128)S(1)}, u32[]{:S(2)}, u32[]{:S(2)}) collective-permute-start(f32[72,128]{1,0:T(8,128)S(1)} %get-tuple-element.26.refs_0_), channel_id=1, source_target_pairs={{16,0},{0,16},{17,1},{1,17},{18,2},{2,18},{19,3},{3,19},{20,4},{4,... | collective-permute-start | bytes 110600 | tf_op jit(solution)/shard_map/ppermute | solution.py:531
  8.5 7.6 %collective-permute-start.2 = (f32[5,8,128]{2,1,0:T(8,128)S(1)}, f32[5,8,128]{2,1,0:T(8,128)S(1)}, u32[]{:S(2)}, u32[]{:S(2)}) collective-permute-start(f32[5,8,128]{2,1,0:T(8,128)S(1)} %get-tuple-element.32), channel_id=1, source_target_pairs={{0,15},{1,2},{2,1},{3,4},{4,3},{5,6},{6,5},{7,8},{8,7},{9,10},{10,... | collective-permute-start | bytes 61448 | tf_op jit(solution)/shard_map/ppermute | solution.py:582
  12.3 3.8 %collective-permute-start.3 = (f32[32,128]{1,0:T(8,128)S(1)}, f32[32,128]{1,0:T(8,128)S(1)}, u32[]{:S(2)}, u32[]{:S(2)}) collective-permute-start(f32[32,128]{1,0:T(8,128)S(1)} %get-tuple-element.35.refs_0_), channel_id=1, source_target_pairs={{16,0},{0,16},{17,1},{1,17},{18,2},{2,18},{19,3},{3,19},{20,4},{4,... | collective-permute-start | bytes 49160 | tf_op jit(solution)/shard_map/ppermute | solution.py:531
  13.7 1.2 %collective-permute-start.1 = (f32[3,8,128]{2,1,0:T(8,128)S(1)}, f32[3,8,128]{2,1,0:T(8,128)S(1)}, u32[]{:S(2)}, u32[]{:S(2)}) collective-permute-start(f32[3,8,128]{2,1,0:T(8,128)S(1)} %get-tuple-element.31), channel_id=1, source_target_pairs={{0,1},{1,0},{2,3},{3,2},{4,5},{5,4},{6,7},{7,6},{8,9},{9,8},{10,11... | collective-permute-start | bytes 36872 | tf_op jit(solution)/shard_map/ppermute | solution.py:592
  16.2 1.2 %collective-permute-start.4 = (f32[2,8,128]{2,1,0:T(8,128)S(1)}, f32[2,8,128]{2,1,0:T(8,128)S(1)}, u32[]{:S(2)}, u32[]{:S(2)}) collective-permute-start(f32[2,8,128]{2,1,0:T(8,128)S(1)} %pair_edge.1), channel_id=1, source_target_pairs={{0,1},{1,0},{2,3},{3,2},{4,5},{5,4},{6,7},{7,6},{8,9},{9,8},{10,11... | collective-permute-start | bytes 24584 | tf_op jit(solution)/shard_map/ppermute | solution.py:601
  18.3 11.5 %all-to-all-start = ((f32[288,1,128]{2,1,0:T(1,128)}), f32[288,1,128]{2,1,0:T(1,128)S(1)}, u32[]{:S(2)}, u32[]{:S(2)}) async-start(f32[288,1,128]{2,1,0:T(1,128)} %bitcast.3), calls=%async_computation | async-start | bytes 294912 | tf_op jit(solution)/shard_map/all_to_all | solution.py:631
  21.3 3.8 %collective-permute-start.5 = (f32[32,128]{1,0:T(8,128)S(1)}, f32[32,128]{1,0:T(8,128)S(1)}, u32[]{:S(2)}, u32[]{:S(2)}) collective-permute-start(f32[32,128]{1,0:T(8,128)S(1)} %get-tuple-element.43.refs_0_), channel_id=1, source_target_pairs={{16,0},{0,16},{17,1},{1,17},{18,2},{2,18},{19,3},{3,19},{20,4},{4,... | collective-permute-start | bytes 49160 | tf_op jit(solution)/shard_map/ppermute | solution.py:531
